TPU v7x, 128 devices: a whole 4x4x4 slice. The times are simulated.
128 devices in a mesh: wide: 16 (over x, z_lo, core), narrow: 8 (over y, z_hi).
Axes of the slice: x: 4, y: 4, z: 4 (z_hi: 2, z_lo: 2; z = z_hi * 2 + z_lo), core: 2. Of those that a mesh axis runs over, the one named last changes fastest.
Arguments:
- pair_rep: bfloat16 [256, 256, 128], P('wide', 'narrow'), may hold values from -6 to 6
- cotangent: bfloat16 [256, 256, 128], P('wide', 'narrow'), may hold values from -6 to 6
- norm_gain: float32 [128], replicated, may hold values from 0.1 to 1.9
- proj_weight: bfloat16 [128, 512], replicated, may hold values from -0.5 to 0.5
- bias_weight: bfloat16 [128, 4], replicated, may hold values from -0.5 to 0.5
- out_weight: bfloat16 [128, 128], replicated, may hold values from -0.5 to 0.5
- residue_mask: int32 [256], replicated, may hold values 0 or 1
Outputs:
- d_pair: bfloat16 [256, 256, 128], P('wide', 'narrow')
- grad_proj: float32 [128, 512], replicated
- grad_bias: float32 [128, 4], replicated
- grad_out: float32 [128, 128], replicated
- grad_gain: float32 [128], replicated
All inputs are finite; a program needn't handle non-finite values.
Results may differ from a plain program's by a relative error of at most 0.019.
Values may be sent and summed in bfloat16 or wider, within the bound.
No kernel may reach another device: no remote copies, remote signals or barrier semaphores. Data moves between devices by JAX's collectives and lax.ppermute only.
A program may use at most 128 MiB of HBM per device.

v0:
```python
import math

import jax
import jax.numpy as jnp
from jax import lax
from jax.sharding import PartitionSpec as P

NORM_EPSILON = 1e-05
MASK_FILL = 1000000000.0


def normalize(pair_rep, norm_gain):
    widened = pair_rep.astype(jnp.float32)
    centre = jnp.mean(widened, axis=-1, keepdims=True)
    centered = widened - centre
    inverse = lax.rsqrt(jnp.mean(centered * centered, axis=-1, keepdims=True) + NORM_EPSILON)
    normal_hat = centered * inverse
    normed = (normal_hat * norm_gain).astype(jnp.bfloat16)
    return (normed, normal_hat, inverse)


def local(pair_rep, cotangent, norm_gain, proj_weight, bias_weight, out_weight, residue_mask):
    row_count, col_count, chan_count = pair_rep.shape
    head_width = out_weight.shape[0]
    head_count = bias_weight.shape[1]
    head_size = head_width // head_count
    score_scale = head_size ** (-0.5)
    key_count = residue_mask.shape[0]
    wide_index = lax.axis_index("wide")
    zero_index = jnp.zeros((), jnp.int32)
    normed, normal_hat, inverse = normalize(pair_rep, norm_gain)
    flat_normed = normed.reshape(row_count * col_count, chan_count)
    queries = jnp.dot(flat_normed, proj_weight[:, :head_width], preferred_element_type=jnp.float32)
    queries = queries.astype(jnp.bfloat16).reshape(row_count, col_count, head_count, head_size)
    gating = jax.nn.sigmoid(
        jnp.dot(flat_normed, proj_weight[:, 3 * head_width :], preferred_element_type=jnp.float32)
    )
    gating = gating.reshape(row_count, col_count, head_width)
    bias_local = jnp.dot(flat_normed, bias_weight, preferred_element_type=jnp.float32).astype(
        jnp.bfloat16
    )
    bias_local = bias_local.reshape(row_count, col_count, head_count)
    kv_weight = proj_weight[:, head_width : 3 * head_width]
    kv_local = jnp.dot(flat_normed, kv_weight, preferred_element_type=jnp.float32)
    kv_local = kv_local.astype(jnp.bfloat16).reshape(row_count, col_count, 2 * head_width)
    kv_all = lax.all_gather(kv_local, "wide", axis=0, tiled=True)
    all_keys = kv_all[..., :head_width].reshape(key_count, col_count, head_count, head_size)
    values = kv_all[..., head_width:].reshape(key_count, col_count, head_count, head_size)
    bias_turned = jnp.transpose(bias_local, (1, 2, 0))
    bias_cols = lax.all_gather(bias_turned, "wide", axis=2, tiled=True)
    bias_all = lax.all_gather(bias_cols, "narrow", axis=0, tiled=True)
    bias_here = lax.dynamic_slice_in_dim(bias_all, wide_index * row_count, row_count, 0)
    masking = (residue_mask.astype(jnp.float32) - 1.0) * MASK_FILL
    block_size = math.gcd(key_count, 64)
    blocks = key_count // block_size

    def scores(key_start, size):
        key_block = lax.dynamic_slice_in_dim(all_keys, key_start, size, 0)
        logits = (
            jnp.einsum("ijhd,kjhd->ijhk", queries, key_block, preferred_element_type=jnp.float32)
            * score_scale
        )
        bias_block = lax.dynamic_slice_in_dim(bias_here, key_start, size, 2).astype(jnp.float32)
        logits = (
            logits + bias_block[:, None] + lax.dynamic_slice_in_dim(masking, key_start, size, 0)
        )
        return (logits, key_block)

    def running(block_index, carried):
        run_max, run_sum = carried
        logits, _ = scores(block_index * block_size, block_size)
        new_max = jnp.maximum(run_max, jnp.max(logits, axis=-1))
        run_sum = run_sum * jnp.exp(run_max - new_max) + jnp.sum(
            jnp.exp(logits - new_max[..., None]), axis=-1
        )
        return (new_max, run_sum)

    stat_shape = (row_count, col_count, head_count)
    run_max, run_sum = lax.fori_loop(
        0,
        blocks,
        running,
        (jnp.full(stat_shape, -jnp.inf, jnp.float32), jnp.zeros(stat_shape, jnp.float32)),
    )
    log_total = run_max + jnp.log(run_sum)

    def attend(block_index, carried):
        key_start = block_index * block_size
        logits, _ = scores(key_start, block_size)
        soft_bf = jnp.exp(logits - log_total[..., None]).astype(jnp.bfloat16)
        value_block = lax.dynamic_slice_in_dim(values, key_start, block_size, 0)
        return carried + jnp.einsum(
            "ijhk,kjhd->ijhd", soft_bf, value_block, preferred_element_type=jnp.float32
        )

    attended = lax.fori_loop(
        0, blocks, attend, jnp.zeros((row_count, col_count, head_count, head_size), jnp.float32)
    )
    attended = attended.reshape(row_count, col_count, head_width)
    gated = (gating * attended).astype(jnp.bfloat16)
    out_grad = jnp.dot(
        cotangent.reshape(-1, chan_count), out_weight.T, preferred_element_type=jnp.float32
    )
    out_grad = out_grad.reshape(row_count, col_count, head_width)
    d_att = (out_grad * gating).astype(jnp.bfloat16)
    d_gate = out_grad * attended * gating * (1.0 - gating)
    d_att4 = d_att.reshape(row_count, col_count, head_count, head_size)
    row_delta = jnp.sum(
        d_att4.astype(jnp.float32) * attended.reshape(row_count, col_count, head_count, head_size),
        axis=-1,
    )

    def block_grads(key_start, size):
        logits, key_block = scores(key_start, size)
        value_block = lax.dynamic_slice_in_dim(values, key_start, size, 0)
        soft = jnp.exp(logits - log_total[..., None])
        d_soft = jnp.einsum(
            "ijhd,kjhd->ijhk", d_att4, value_block, preferred_element_type=jnp.float32
        )
        d_logits = (soft * (d_soft - row_delta[..., None])).astype(jnp.bfloat16)
        return (soft.astype(jnp.bfloat16), d_logits, key_block)

    def query_pass(block_index, carried):
        d_query, bias_part = carried
        key_start = block_index * block_size
        _, d_logits, key_block = block_grads(key_start, block_size)
        d_query = (
            d_query
            + jnp.einsum("ijhk,kjhd->ijhd", d_logits, key_block, preferred_element_type=jnp.float32)
            * score_scale
        )
        bias_part = lax.dynamic_update_slice_in_dim(
            bias_part, jnp.sum(d_logits.astype(jnp.float32), axis=1), key_start, 2
        )
        return (d_query, bias_part)

    d_query, bias_part = lax.fori_loop(
        0,
        blocks,
        query_pass,
        (
            jnp.zeros((row_count, col_count, head_count, head_size), jnp.float32),
            jnp.zeros((row_count, head_count, key_count), jnp.float32),
        ),
    )
    piece_rows = row_count * lax.axis_size("wide")
    sub_size = math.gcd(piece_rows, block_size)

    def add_block(block_index, partial_value):
        offset = block_index * sub_size
        soft_bf, d_logits, _ = block_grads(offset, sub_size)
        d_key = (
            jnp.einsum("ijhk,ijhd->kjhd", d_logits, queries, preferred_element_type=jnp.float32)
            * score_scale
        )
        d_value = jnp.einsum("ijhk,ijhd->kjhd", soft_bf, d_att4, preferred_element_type=jnp.float32)
        stacked = jnp.concatenate(
            [
                d_key.reshape(sub_size, col_count, head_width),
                d_value.reshape(sub_size, col_count, head_width),
            ],
            axis=-1,
        )
        return lax.dynamic_update_slice_in_dim(partial_value, stacked, offset, 0)

    d_kv = lax.psum_scatter(
        lax.fori_loop(
            0,
            piece_rows // sub_size,
            add_block,
            jnp.zeros((piece_rows, col_count, 2 * head_width), jnp.float32),
        ).astype(jnp.bfloat16),
        "wide",
        scatter_dimension=0,
        tiled=True,
    )
    wide_size = lax.axis_size("wide")
    narrow_size = lax.axis_size("narrow")
    spread = bias_part.reshape(row_count, head_count, wide_size, row_count)
    spread = jnp.transpose(spread, (2, 3, 1, 0))
    padded_terms = jnp.zeros(
        (wide_size, narrow_size, row_count, head_count, col_count), jnp.float32
    )
    padded_terms = lax.dynamic_update_slice(
        padded_terms,
        spread[:, None],
        (zero_index, wide_index // 2, zero_index, zero_index, wide_index % 2 * row_count),
    )
    padded_terms = padded_terms.reshape(wide_size * narrow_size * row_count, head_count * col_count)
    bias_tile = lax.psum_scatter(padded_terms, ("wide", "narrow"), scatter_dimension=0, tiled=True)
    bias_tile = bias_tile.reshape(row_count, head_count, col_count)
    bias_grad = jnp.transpose(bias_tile, (0, 2, 1)).astype(jnp.bfloat16)
    grads = jnp.concatenate(
        [
            d_query.reshape(row_count, col_count, head_width).astype(jnp.bfloat16),
            d_kv,
            d_gate.astype(jnp.bfloat16),
        ],
        axis=-1,
    )
    flat_grads = grads.reshape(-1, 4 * head_width)
    flat_bias = bias_grad.reshape(-1, head_count)
    d_normed = jnp.dot(flat_grads, proj_weight.T, preferred_element_type=jnp.float32)
    d_normed = d_normed + jnp.dot(flat_bias, bias_weight.T, preferred_element_type=jnp.float32)
    contract = (((0,), (0,)), ((), ()))
    proj_part = lax.dot_general(
        flat_normed, flat_grads, contract, preferred_element_type=jnp.float32
    )
    bias_w_part = lax.dot_general(
        flat_normed, flat_bias, contract, preferred_element_type=jnp.float32
    )
    out_part = lax.dot_general(
        gated.reshape(-1, head_width),
        cotangent.reshape(-1, chan_count),
        contract,
        preferred_element_type=jnp.float32,
    )
    flat_hat = normal_hat.reshape(-1, chan_count)
    gain_part = jnp.sum(d_normed * flat_hat, axis=0)
    grad_proj, grad_bias, grad_out, grad_gain = lax.psum(
        (proj_part, bias_w_part, out_part, gain_part), ("wide", "narrow")
    )
    d_hat = d_normed * norm_gain
    d_pair = inverse.reshape(-1, 1) * (
        d_hat
        - jnp.mean(d_hat, axis=-1, keepdims=True)
        - flat_hat * jnp.mean(d_hat * flat_hat, axis=-1, keepdims=True)
    )
    d_pair = d_pair.reshape(row_count, col_count, chan_count).astype(jnp.bfloat16)
    return (d_pair, grad_proj, grad_bias, grad_out, grad_gain)


def solution(mesh):
    in_specs = (P("wide", "narrow", None), P("wide", "narrow", None), P(), P(), P(), P(), P())
    out_specs = (P("wide", "narrow", None), P(), P(), P(), P())
    return jax.shard_map(local, mesh=mesh, in_specs=in_specs, out_specs=out_specs, check_vma=False)
```

profile of v0, /device:TPU:1, one launch (start us, length us, event | category | flops | bytes accessed | tf_op | source)
XLA Modules:
  0.0 1052.6 jit_solution(16865890909880874251)
XLA Ops:
  14.3 22.2 %all_gather.10 = bf16[32,4,256]{0,1,2:T(4,128)(2,1)S(1)} all-gather(bf16[32,4,16]{0,1,2:T(4,128)(2,1)S(1)} %bitcast.195), channel_id=1, replica_groups=mesh['wide'=16,'narrow'=8] {'wide'}, dimensions={2}, use_global_device_ids=true | all-gather | bytes 69632 | tf_op jit(solution)/shard_map/all_gather | solution.py:50
  37.7 30.9 %all_gather.11 = bf16[256,4,256]{2,1,0:T(4,128)(2,1)S(1)} all-gather(bf16[32,4,256]{2,1,0:T(4,128)(2,1)S(1)} %copy.102), channel_id=1, replica_groups=mesh['wide'=16,'narrow'=8] {'narrow'}, dimensions={0}, use_global_device_ids=true | all-gather | bytes 589824 | tf_op jit(solution)/shard_map/all_gather | solution.py:51
  68.9 5.0 fusion.74
  76.9 6.9 while.60
  88.1 15.3 %while.61 = (s32[]{:T(128)}, f32[16,32,4,32]{3,0,2,1:T(8,128)}, bf16[256,32,4,32]{0,3,2,1:T(8,128)(2,1)S(1)}, bf16[256,32,4,32]{0,3,2,1:T(8,128)(2,1)}, bf16[16,...) while((s32[]{:T(128)}, f32[16,32,4,32]{3,0,2,1:T(8,128)}, ...), condition=%wide.region_7.0_spmd.clone, body=%wide.region_6.0_spmd.clone.sunk | while | flops 17567752 | bytes 4057788 | solution.py:96
  88.3 3.4 fusion.136
  91.9 3.8 fusion.136
  95.8 3.8 fusion.136
  99.7 3.8 fusion.136
  114.1 28.3 %while.62 = (s32[]{:T(128)}, f32[16,32,4,32]{3,0,2,1:T(8,128)}, f32[16,4,256]{2,0,1:T(8,128)S(1)}, bf16[256,32,4,32]{0,3,2,1:T(8,128)(2,1)}, bf16[16,32,4,32]{3,...) while((s32[]{:T(128)}, f32[16,32,4,32]{3,0,2,1:T(8,128)}, ...), condition=%wide.region_11.0_spmd.clone, body=%wide.region_9.0_spmd.clone.sunk | while | flops 26542084 | bytes 16491777 | solution.py:137
  124.6 3.5 fusion.143
  131.5 3.5 fusion.143
  138.9 3.5 fusion.143
  146.4 42.6 %dynamic_update_slice.17 = f32[16,8,16,4,32]{4,3,2,1,0:T(4,128)} dynamic-update-slice(f32[16,8,16,4,32]{4,3,2,1,0:T(4,128)} %broadcast_in_dim.70, f32[16,1,16,4,16]{4,3,2,1,0:T(4,128)} %bitcast.190, s32[]{:T(128)} %constant.207.clone.1, s32[]{:T(128)S(6)} %select_n.63, s32[]{:T(128)} %constant.207.clone.1, s32[]{:T(128)} %constant.207.clone.1, s32[]{:T(128)S(6)} %select_n.65) | dynamic-update-slice | bytes 131076 | tf_op jit(solution)/shard_map/dynamic_update_slice | solution.py:184
  189.0 4.5 reshape.138
  196.1 56.8 %while.59 = (s32[]{:T(128)}, bf16[256,32,256]{2,1,0:T(8,128)(2,1)}, bf16[256,32,4,32]{0,3,2,1:T(8,128)(2,1)}, bf16[16,32,4,32]{3,0,2,1:T(8,128)(2,1)S(1)}, bf16[...) while((s32[]{:T(128)}, bf16[256,32,256]{2,1,0:T(8,128)(2,1)}, ...), condition=%wide.region_13.0_spmd, body=%wide.region_12.0_spmd.sunk | while | flops 37228548 | bytes 31310876 | solution.py:167
  196.3 3.5 fusion.128
  210.5 3.5 fusion.128
  224.7 3.5 fusion.128
  238.9 3.5 fusion.128
  255.7 564.9 %reduce-scatter.5.cloned.1.call-done = f32[16,128]{1,0:T(8,128)} async-done(((f32[2048,128]{1,0:T(8,128)}), f32[16,128]{1,0:T(8,128)}) %reduce-scatter.5.cloned.1.call-update) | async-done | bytes 8208 | tf_op jit(solution)/shard_map/reduce_scatter | solution.py:190
  821.6 69.2 %reduce-scatter.3.cloned.1.call-done = bf16[16,32,256]{2,1,0:T(8,128)(2,1)} async-done(((bf16[256,32,256]{2,1,0:T(8,128)(2,1)}), bf16[16,32,256]{2,1,0:T(8,128)(2,1)}) %reduce-scatter.3.cloned.1.call-update) | async-done | bytes 262160 | tf_op jit(solution)/shard_map/reduce_scatter | solution.py:166
  894.5 68.1 %all-reduce = (f32[128,4]{0,1:T(4,128)}, f32[128]{0:T(128)}) all-reduce(f32[128,4]{0,1:T(4,128)S(1)} %convolution_bitcast_fusion.5, f32[128]{0:T(128)S(1)} %get-tuple-element.932), channel_id=1, replica_groups=mesh['wide'=16,'narrow'=8] {'wide','narrow'}, use_global_device_ids=true, to_apply=%region_19.20 | all-reduce | flops 640 | bytes 5120 | tf_op jit(solution)/shard_map/psum | solution.py:220
  963.6 79.3 %all-reduce.4.cloned.1.call-done = (f32[128,512]{1,0:T(8,128)}, f32[128,128]{1,0:T(8,128)}) async-done(((f32[128,512]{1,0:T(8,128)}, f32[128,128]{1,0:T(8,128)}), (f32[128,512]{1,0:T(8,128)}, f32[128,128]{1,0:T(8,128)})) %all-reduce.4.cloned.1.call-update) | async-done | bytes 327696 | tf_op jit(solution)/shard_map/psum | solution.py:220
  (214 shorter events, 112.0 us)
Async XLA Ops:
  7.2 100.7 %copy-start = (bf16[16,32,128]{2,1,0:T(8,128)(2,1)S(1)}, bf16[16,32,128]{2,1,0:T(8,128)(2,1)}, u32[]{:S(2)}) copy-start(bf16[16,32,128]{2,1,0:T(8,128)(2,1)} %param.16) | copy-start | bytes 393220
  7.2 29.4 %copy-start.16 = (bf16[128,512]{1,0:T(8,128)(2,1)S(1)}, bf16[128,512]{1,0:T(8,128)(2,1)}, u32[]{:S(2)}) copy-start(bf16[128,512]{1,0:T(8,128)(2,1)} %param.18) | copy-start | bytes 393220
  7.2 61.7 %all-gather.2.cloned.1.call-start = ((), (), s32[]{:S(2)}) async-start(), calls=%async_computation.2 | async-start | bytes 4456448 | tf_op jit(solution)/shard_map/all_gather | solution.py:46
  11.3 57.3 %copy-start.11 = (bf16[16,32,128]{2,1,0:T(8,128)(2,1)}, bf16[16,32,128]{2,1,0:T(8,128)(2,1)S(1)}, u32[]{:S(2)}) copy-start(bf16[16,32,128]{2,1,0:T(8,128)(2,1)S(1)} %get-tuple-element.1019) | copy-start | bytes 393220
  11.4 57.3 %copy-start.21 = (s32[256]{0:T(256)S(1)}, s32[256]{0:T(256)}, u32[]{:S(2)}) copy-start(s32[256]{0:T(256)} %param.21) | copy-start | bytes 3076
  13.2 807.4 %reduce-scatter.5.cloned.1.call-start = ((), (), s32[]{:S(2)}) async-start(), calls=%async_computation.4 | async-start | bytes 1056768 | tf_op jit(solution)/shard_map/reduce_scatter | solution.py:190
  68.9 38.9 %copy-start.13 = (f32[512,128]{1,0:T(8,128)}, f32[512,128]{1,0:T(8,128)S(1)}, u32[]{:S(2)}) copy-start(f32[512,128]{1,0:T(8,128)S(1)} %fusion.58) | copy-start | bytes 786436
  103.5 4.4 copy-start.18
  193.6 697.2 %reduce-scatter.3.cloned.1.call-start = ((), (), s32[]{:S(2)}) async-start(), calls=%async_computation.3 | async-start | bytes 4456448 | tf_op jit(solution)/shard_map/reduce_scatter | solution.py:166
  196.1 7.0 copy-start.1
  207.9 2.4 copy-start.2
  210.3 7.0 copy-start.1
  222.1 2.5 copy-start.2
  224.5 7.0 copy-start.1
  236.3 2.4 copy-start.2
  238.7 7.0 copy-start.1
  250.5 2.4 copy-start.2
  253.0 568.5 %copy-start.12 = (bf16[16,32,128]{2,1,0:T(8,128)(2,1)S(1)}, bf16[16,32,128]{2,1,0:T(8,128)(2,1)}, u32[]{:S(2)}) copy-start(bf16[16,32,128]{2,1,0:T(8,128)(2,1)} %copy-done.11) | copy-start | bytes 393220
  253.0 789.9 %all-reduce.4.cloned.1.call-start = ((), (), s32[]{:S(2)}) async-start(), calls=%async_computation.5 | async-start | bytes 655360 | tf_op jit(solution)/shard_map/psum | solution.py:220
  254.2 636.6 %copy-start.15 = (bf16[16,32,128]{2,1,0:T(8,128)(2,1)S(1)}, bf16[16,32,128]{2,1,0:T(8,128)(2,1)}, u32[]{:S(2)}) copy-start(bf16[16,32,128]{2,1,0:T(8,128)(2,1)} %get-tuple-element.1018) | copy-start | bytes 393220
  254.3 637.6 %copy-start.17 = (bf16[128,512]{1,0:T(8,128)(2,1)S(1)}, bf16[128,512]{1,0:T(8,128)(2,1)}, u32[]{:S(2)}) copy-start(bf16[128,512]{1,0:T(8,128)(2,1)} %param.18) | copy-start | bytes 393220
  255.7 638.4 %copy-start.8 = (f32[16,32,128]{2,1,0:T(8,128)S(1)}, f32[16,32,128]{2,1,0:T(8,128)}, u32[]{:S(2)}) copy-start(f32[16,32,128]{2,1,0:T(8,128)} %get-tuple-element.1020) | copy-start | bytes 786436
  255.7 638.4 %copy-start.19 = (f32[128]{0:T(128)S(1)}, f32[128]{0:T(128)}, u32[]{:S(2)}) copy-start(f32[128]{0:T(128)} %param.17) | copy-start | bytes 1540
  255.7 638.4 %copy-start.20 = (bf16[128,4]{0,1:T(4,128)(2,1)S(1)}, bf16[128,4]{0,1:T(4,128)(2,1)}, u32[]{:S(2)}) copy-start(bf16[128,4]{0,1:T(4,128)(2,1)} %param.19) | copy-start | bytes 3076
  (14 other events, 21.8 us)
Sparse Core Ops, SparseCore 0:
  13.3 44.0 all-gather.1
  193.7 626.7 reduce-scatter.4
  823.1 67.6 reduce-scatter.2
  896.9 145.9 all-reduce.3
where the time goes:
time: 1050 us
  waiting for transfers between devices  713 us (68%)
  blocking collectives  121 us (12%)
  local copies, waits for them, and re-layouts  106 us (10%)
  matrix products  82.5 us (8%)
  other arithmetic  15.1 us (1%)
  between operations  14.2 us (1%)
    reduce_scatter x1, waiting for transfers between devices, local(): lax.psum_scatter(padded_terms, ('wide', 'narrow'), scatter_dimension=0, t...  565 us
    psum x1, waiting for transfers between devices, local(): lax.psum((proj_part, bias_w_part, out_part, gain_part), ('wide', 'narrow'))  79.3 us
    reduce_scatter x1, waiting for transfers between devices, local(): lax.psum_scatter(lax.fori_loop(0, piece_rows // sub_size, add_block, jnp....  69.2 us
    psum x1, blocking collectives, local(): lax.psum((proj_part, bias_w_part, out_part, gain_part), ('wide', 'narrow'))  68.1 us
    dynamic_update_slice x1, local copies, waits for them, and re-layouts, local(): lax.dynamic_update_slice(padded_terms, spread[:, None], (zero_index, wide...  42.6 us
    all_gather x1, blocking collectives, local(): bias_all = lax.all_gather(bias_cols, 'narrow', axis=0, tiled=True)  30.9 us
    dot_general x12, matrix products, scores(): jnp.einsum('ijhd,kjhd->ijhk', queries, key_block, preferred_element_type=...  23.1 us
    all_gather x1, blocking collectives, local(): bias_cols = lax.all_gather(bias_turned, 'wide', axis=2, tiled=True)  22.2 us
  transfers between devices with their start and end apart: 4, of which 3 were waited for; matrix products, arithmetic and copies ran while one was open for 6% of the time, Pallas kernels for 0%

commit v1 on v0

v1 whole, which is shorter than its diff:
```python
import jax
import jax.numpy as jnp
from jax import lax
from jax.experimental import pallas as pl
from jax.experimental.pallas import tpu as pltpu
from jax.sharding import PartitionSpec as P

NORM_EPSILON = 1e-05
MASK_FILL = 1000000000.0
BF = jnp.bfloat16
F32 = jnp.float32
BOTH = ("wide", "narrow")

ROWS = 16
COLS = 32
TILE = ROWS * COLS
N_WIDE = 16
N_NARROW = 8
DEVICES = N_WIDE * N_NARROW
LENGTH = 256
CH = 128
HEADS = 4
DIM = 32
IN_ROWS = 40
MID_ROWS = 24
OUT_ROWS = 16

NT = (((1,), (1,)), ((), ()))
NN = (((1,), (0,)), ((), ()))
TN = (((0,), (0,)), ((), ()))


def mm(a, b, dims=NN):
    return lax.dot_general(a, b, dims, preferred_element_type=F32)


def normal(x):
    centered = x - jnp.mean(x, axis=-1, keepdims=True)
    inverse = lax.rsqrt(jnp.mean(centered * centered, axis=-1, keepdims=True) + NORM_EPSILON)
    return centered * inverse, inverse


def lane_group(shape):
    return lax.broadcasted_iota(jnp.int32, shape, 1) // COLS


def pre_kernel(pair_ref, cot_ref, gain_ref, wbt_ref, send_ref, normed_ref, xs, cs):
    hat, _ = normal(pair_ref[...].astype(F32).reshape(TILE, CH))
    normed = (hat * gain_ref[...]).astype(BF)
    normed_ref[...] = normed
    xs[...] = normed.astype(F32)
    cs[...] = cot_ref[...].astype(F32).reshape(TILE, CH)
    bias = mm(wbt_ref[...], normed, NT)
    turned = [pltpu.roll(bias[:, b * CH : (b + 1) * CH], 64, 1) for b in range(4)]
    for h in range(HEADS):
        rows = []
        for b in range(4):
            rows += [bias[h : h + 1, b * CH : (b + 1) * CH], turned[b][h : h + 1]]
        chunk = jnp.concatenate(rows, axis=0).astype(BF)
        for col in range(COLS):
            send_ref[h * COLS + col, 32:40, :] = chunk
    for col in range(COLS):
        x = xs[pl.ds(col, ROWS, stride=COLS), :].astype(BF)
        c = cs[pl.ds(col, ROWS, stride=COLS), :].astype(BF)
        for h in range(HEADS):
            send_ref[h * COLS + col, 0:16, :] = x
            send_ref[h * COLS + col, 16:32, :] = c


def attention_kernel(
    recv_ref, wall_ref, ow_ref, mask_ref, send_ref, bias_s, sum_s, tail_s, grad_s, gout_s
):
    me = lax.axis_index("wide") * N_NARROW + lax.axis_index("narrow")
    head = me // COLS
    scale = DIM**-0.5
    weight = wall_ref[head]
    out_w = ow_ref[pl.ds(pl.multiple_of(head * DIM, DIM), DIM), :]
    group = lane_group((CH, CH))
    for half in range(2):
        for kq in range(2):
            acc = jnp.zeros((CH, CH), F32)
            for q in range(4):
                got = recv_ref[:, half * 4 + q, 32:40, :].astype(F32).reshape(CH, CH)
                shift = (q - kq) * COLS % CH
                acc = jnp.where(group == q, pltpu.roll(got, shift, 1) if shift else got, acc)
            bias_s.at[half][pl.ds(kq, CH, stride=2), :] = acc
    mask = mask_ref[...]
    zero = jnp.zeros((DIM, CH), BF)
    eye = (
        lax.broadcasted_iota(jnp.int32, (LENGTH, LENGTH), 0)
        == lax.broadcasted_iota(jnp.int32, (LENGTH, LENGTH), 1)
    ).astype(BF)

    for n in range(N_NARROW):
        x = recv_ref[:, n, 0:16, :].reshape(LENGTH, CH)
        cot = recv_ref[:, n, 16:32, :].reshape(LENGTH, CH)
        proj_t = mm(weight, x, NT)
        kv = mm(x, weight[DIM : 3 * DIM], NT).astype(BF)
        k_t = proj_t[DIM : 2 * DIM].astype(BF)
        v_t = proj_t[2 * DIM : 3 * DIM].astype(BF)
        out_grad = mm(out_w, cot, NT)
        dq, dg, gated = [], [], []
        dk = dv = None
        for half in range(2):
            part = slice(half * CH, (half + 1) * CH)
            q_t = proj_t[0:DIM, part].astype(BF)
            gate = jax.nn.sigmoid(proj_t[3 * DIM :, part])
            og = out_grad[:, part]
            da_t = (og * gate).astype(BF)
            logits = mm(kv, jnp.concatenate([q_t, zero], axis=0)) * scale
            logits = logits + bias_s[half] + mask
            top = jnp.max(logits, axis=0, keepdims=True)
            e = jnp.exp(logits - top)
            soft = e * (1.0 / jnp.sum(e, axis=0, keepdims=True))
            soft_bf = soft.astype(BF)
            att = mm(v_t, soft_bf)
            delta = jnp.sum(da_t.astype(F32) * att, axis=0, keepdims=True)
            d_soft = mm(kv, jnp.concatenate([zero, da_t], axis=0))
            d_log = (soft * (d_soft - delta)).astype(BF)
            if n == 0:
                sum_s[half] = d_log.astype(F32)
            else:
                sum_s[half] += d_log.astype(F32)
            dq.append(mm(k_t, d_log) * scale)
            dk_half = mm(q_t, d_log, NT)
            dv_half = mm(da_t, soft_bf, NT)
            dk = dk_half if half == 0 else dk + dk_half
            dv = dv_half if half == 0 else dv + dv_half
            dg.append(og * att * gate * (1.0 - gate))
            gated.append((gate * att).astype(BF))
        dq = jnp.concatenate(dq, axis=1)
        dg = jnp.concatenate(dg, axis=1)
        gated = jnp.concatenate(gated, axis=1)
        grads_t = jnp.concatenate([dq, dk * scale, dv, dg], axis=0).astype(BF)
        part = mm(grads_t, x)
        out_part = mm(gated, cot)
        if n == 0:
            grad_s[...] = part
            gout_s[...] = out_part
        else:
            grad_s[...] += part
            gout_s[...] += out_part
        grads = mm(eye, grads_t, NT).astype(BF)
        send_ref[:, n, 0:16, :] = grads.reshape(N_WIDE, ROWS, CH)

    group = lane_group((64, CH))
    tail_s[...] = jnp.zeros_like(tail_s)
    for n in range(N_NARROW):
        half, q = n // 4, n % 4
        acc = jnp.zeros((64, CH), F32)
        for kq in range(4):
            got = sum_s.at[half][pl.ds(kq, 64, stride=4), :]
            shift = (kq - q) * COLS % CH
            acc = jnp.where(group == kq, pltpu.roll(got, shift, 1) if shift else got, acc)
        for w in range(N_WIDE):
            at = (w * N_NARROW + n) * 8
            tail_s[at : at + 4, :] = acc[w * 4 : (w + 1) * 4, :]
    tail_s[pl.ds(4, DEVICES, stride=8), :] = jnp.transpose(grad_s[...])
    out_part = gout_s[...]
    for r in range(4):
        tail_s[pl.ds(5 + 8 * r, DIM, stride=32), :] = out_part
    tail = tail_s[...].astype(BF).reshape(N_WIDE, N_NARROW, 8, CH)
    send_ref[:, :, 16:24, :] = tail


def reduce_kernel(recv_ref, normed_ref, send_ref, bias_ref):
    sums = [
        jnp.sum(recv_ref[h * COLS : (h + 1) * COLS, 16:24, :].astype(F32), axis=0)
        for h in range(HEADS)
    ]
    blocks = [
        jnp.concatenate([sums[h][b : b + 1] for h in range(HEADS)], axis=0) for b in range(4)
    ]
    bias = jnp.concatenate(blocks, axis=1).astype(BF)
    bias = jnp.concatenate([bias, jnp.zeros_like(bias)], axis=0)
    bias_ref[...] = bias
    grad_bias = mm(bias, normed_ref[...])
    own = jnp.concatenate([sums[h][4:5] for h in range(HEADS)], axis=0)
    group = lane_group((1, CH))
    rows = []
    for t in range(4):
        row = jnp.zeros((1, CH), F32)
        for h in range(HEADS):
            shift = (h - t) * COLS % CH
            got = own[h : h + 1]
            row = jnp.where(group == h, pltpu.roll(got, shift, 1) if shift else got, row)
        rows.append(row)
    rows += [sums[h][5:6] for h in range(HEADS)]
    rows.append(grad_bias)
    chunk = jnp.concatenate(rows, axis=0).astype(BF)
    send_ref[...] = jnp.broadcast_to(chunk[None], (DEVICES, OUT_ROWS, CH))


def pair_kernel(recv_ref, bias_ref, pair_ref, gain_ref, wall_ref, wbt_ref, out_ref, ds):
    total = jnp.zeros((TILE, CH), F32)
    for h in range(HEADS):
        g = recv_ref[h * COLS : (h + 1) * COLS, 0:16, :].reshape(TILE, CH)
        total = total + mm(g, wall_ref[h])
    ds[...] = total
    d_normed = jnp.concatenate([ds[pl.ds(r, COLS, stride=ROWS), :] for r in range(ROWS)], axis=0)
    d_normed = d_normed + mm(bias_ref[...], wbt_ref[...], TN)
    hat, inverse = normal(pair_ref[...].astype(F32).reshape(TILE, CH))
    d_hat = d_normed * gain_ref[...]
    d_pair = inverse * (
        d_hat
        - jnp.mean(d_hat, axis=-1, keepdims=True)
        - hat * jnp.mean(d_hat * hat, axis=-1, keepdims=True)
    )
    out_ref[...] = d_pair.astype(BF).reshape(ROWS, COLS, CH)


def final_kernel(
    recv_ref, pw_ref, wbt_ref, gain_ref, gp_ref, gb_ref, go_ref, gg_ref, vs
):
    vs[...] = recv_ref[...].astype(F32).reshape(DEVICES * OUT_ROWS, CH)
    dots = jnp.zeros((CH, CH), F32)
    for t in range(4):
        got = vs[pl.ds(t, CH, stride=OUT_ROWS), :]
        gp_ref[:, t * CH : (t + 1) * CH] = got
        dots = dots + got * pw_ref[:, t * CH : (t + 1) * CH].astype(F32)
    for h in range(HEADS):
        go_ref[h * DIM : (h + 1) * DIM, :] = vs[pl.ds(4 + h, DIM, stride=4 * OUT_ROWS), :]
    grad_bias = jnp.sum(recv_ref[:, 8:16, :].astype(F32), axis=0)
    gb_ref[...] = jnp.transpose(grad_bias)[:, :HEADS]
    dots_row = jnp.sum(jnp.transpose(dots), axis=0, keepdims=True)
    bias_row = jnp.sum(grad_bias * wbt_ref[...].astype(F32), axis=0, keepdims=True)
    gg_ref[...] = (dots_row + bias_row) / gain_ref[...]


def call(kernel, out_shape, scratch=(), cost=None):
    many = isinstance(out_shape, (list, tuple))
    spec = pl.BlockSpec(memory_space=pltpu.VMEM)
    return pl.pallas_call(
        kernel,
        out_shape=out_shape,
        out_specs=[spec] * len(out_shape) if many else spec,
        scratch_shapes=list(scratch),
        compiler_params=pltpu.CompilerParams(vmem_limit_bytes=32 * 1024 * 1024),
        cost_estimate=cost,
    )


def shape(*dims, dtype=BF):
    return jax.ShapeDtypeStruct(dims, dtype)


def exchange(x):
    return lax.all_to_all(x, BOTH, 0, 0, tiled=True)


def local(pair_rep, cotangent, norm_gain, proj_weight, bias_weight, out_weight, residue_mask):
    gain = norm_gain.reshape(1, CH)
    wbt = jnp.concatenate([bias_weight.T, jnp.zeros((HEADS, CH), BF)], axis=0)
    wall = proj_weight.reshape(CH, 4, HEADS, DIM).transpose(2, 1, 3, 0).reshape(HEADS, CH, CH)
    masking = (residue_mask.astype(F32) - 1.0) * MASK_FILL
    masking = jnp.broadcast_to(masking[:, None], (LENGTH, CH))
    tile_f32 = pltpu.VMEM((TILE, CH), F32)

    send, normed = call(
        pre_kernel, [shape(DEVICES, IN_ROWS, CH), shape(TILE, CH)], [tile_f32, tile_f32]
    )(pair_rep, cotangent, gain, wbt)
    recv = exchange(send)
    mid = call(
        attention_kernel,
        shape(N_WIDE, N_NARROW, MID_ROWS, CH),
        [
            pltpu.VMEM((2, LENGTH, CH), F32),
            pltpu.VMEM((2, LENGTH, CH), F32),
            pltpu.VMEM((DEVICES * 8, CH), F32),
            pltpu.VMEM((CH, CH), F32),
            pltpu.VMEM((DIM, CH), F32),
        ],
    )(recv.reshape(N_WIDE, N_NARROW, IN_ROWS, CH), wall, out_weight, masking)
    mid = exchange(mid.reshape(DEVICES, MID_ROWS, CH))
    send, bias = call(reduce_kernel, [shape(DEVICES, OUT_ROWS, CH), shape(8, TILE)])(mid, normed)
    last = exchange(send)
    d_pair = call(
        pair_kernel,
        shape(ROWS, COLS, CH),
        [tile_f32],
        pl.CostEstimate(flops=100_000_000, bytes_accessed=4_000_000, transcendentals=512),
    )(mid, bias, pair_rep, gain, wall, wbt)
    grad_proj, grad_bias, grad_out, grad_gain = call(
        final_kernel,
        [
            shape(CH, 4 * CH, dtype=F32),
            shape(CH, HEADS, dtype=F32),
            shape(CH, CH, dtype=F32),
            shape(1, CH, dtype=F32),
        ],
        [pltpu.VMEM((DEVICES * OUT_ROWS, CH), F32)],
    )(last, proj_weight, wbt, gain)
    return (d_pair, grad_proj, grad_bias, grad_out, grad_gain.reshape(CH))


def solution(mesh):
    in_specs = (P("wide", "narrow", None), P("wide", "narrow", None), P(), P(), P(), P(), P())
    out_specs = (P("wide", "narrow", None), P(), P(), P(), P())
    return jax.shard_map(local, mesh=mesh, in_specs=in_specs, out_specs=out_specs, check_vma=False)
```

time: 1050 us -> 89.9 us (0.09)
  waiting for transfers between devices: 713 us -> 34.9 us
  local copies, waits for them, and re-layouts: 106 us -> 4.04 us
  blocking collectives: 121 us -> 20.6 us
  matrix products: 82.5 us -> 0 us
  starting transfers between devices: 0.16 us -> 15.3 us
  other arithmetic: 15.1 us -> 0.01 us
  Pallas kernels: 0 us -> 13.9 us
  between operations: 14.2 us -> 0.73 us
    reduce_scatter x2 -> x0, waiting for transfers between devices: 634 us -> none  [the longest x1 565 us: local(): lax.psum_scatter(padded_terms, ('wide', 'narrow'), scatter_dimension=0, t...]
    dot_general x42 -> x0, matrix products: 82.5 us -> none  [the longest x12 23.1 us: scores(): jnp.einsum('ijhd,kjhd->ijhk', queries, key_block, preferred_element_type=...]
    psum x1 -> x0, waiting for transfers between devices: 79.3 us -> none  [local(): lax.psum((proj_part, bias_w_part, out_part, gain_part), ('wide', 'narrow'))]
    psum x1 -> x0, blocking collectives: 68.1 us -> none  [local(): lax.psum((proj_part, bias_w_part, out_part, gain_part), ('wide', 'narrow'))]
    dynamic_update_slice x13 -> x0, local copies, waits for them, and re-layouts: 63.8 us -> none  [the longest x1 42.6 us: local(): lax.dynamic_update_slice(padded_terms, spread[:, None], (zero_index, wide...]
    all_gather x2 -> x0, blocking collectives: 53.1 us -> none  [the longest x1 30.9 us: local(): bias_all = lax.all_gather(bias_cols, 'narrow', axis=0, tiled=True)]
    all_to_all x0 -> x2, waiting for transfers between devices: none -> 34.9 us  [exchange(): return lax.all_to_all(x, BOTH, 0, 0, tiled=True)]
    all_to_all x0 -> x1, blocking collectives: none -> 20.6 us  [exchange(): return lax.all_to_all(x, BOTH, 0, 0, tiled=True)]
  transfers between devices with their start and end apart: 4 -> 2, of which waited for: 3 -> 2; matrix products, arithmetic and copies ran while one was open for 6% -> 0% of each run, Pallas kernels for 0% -> 1%
where the time goes in v1:
time: 89.9 us; the launch traced here: 89.6 us
  waiting for transfers between devices  34.9 us (39%)
  blocking collectives  20.6 us (23%)
  starting transfers between devices  15.3 us (17%)
  Pallas kernels  13.9 us (15%)
  local copies, waits for them, and re-layouts  4.04 us (4%)
    all_to_all x2, waiting for transfers between devices, exchange(): return lax.all_to_all(x, BOTH, 0, 0, tiled=True)  34.9 us
    all_to_all x1, blocking collectives, exchange(): return lax.all_to_all(x, BOTH, 0, 0, tiled=True)  20.6 us
    all_to_all x2, starting transfers between devices, exchange(): return lax.all_to_all(x, BOTH, 0, 0, tiled=True)  15.3 us
    pallas_call x1, Pallas kernels, local(): call(attention_kernel, shape(N_WIDE, N_NARROW, MID_ROWS, CH), [pltpu.VMEM...  9.08 us
    unnamed x18, local copies, waits for them, and re-layouts  3.25 us
  transfers between devices with their start and end apart: 2, of which 2 were waited for; matrix products, arithmetic and copies ran while one was open for 0% of the time, Pallas kernels for 1%

profile of v1, /device:TPU:1, one launch (start us, length us, event | category | flops | bytes accessed | tf_op | source)
XLA Modules:
  0.0 89.6 jit_solution(15133264506468715385)
XLA Ops:
  0.6 0.7 concatenate.3.wbt_ref
  1.3 0.0 copy-start
  1.3 0.9 %copy-done = bf16[16,32,128]{2,1,0:T(8,128)(2,1)S(1)} copy-done((bf16[16,32,128]{2,1,0:T(8,128)(2,1)S(1)}, bf16[16,32,128]{2,1,0:T(8,128)(2,1)}, u32[]{:S(2)}) %copy-start) | copy-done | bytes 131096
  2.2 0.0 copy-start.3
  2.2 0.9 %copy-done.3 = bf16[16,32,128]{2,1,0:T(8,128)(2,1)S(1)} copy-done((bf16[16,32,128]{2,1,0:T(8,128)(2,1)S(1)}, bf16[16,32,128]{2,1,0:T(8,128)(2,1)}, u32[]{:S(2)}) %copy-start.3) | copy-done | bytes 131096
  3.1 0.7 copy-done.5
  3.8 1.7 %shard_map.110 = (bf16[128,40,128]{2,1,0:T(8,128)(2,1)}, bf16[512,128]{1,0:T(8,128)(2,1)S(1)}) custom-call(bf16[16,32,128]{2,1,0:T(8,128)(2,1)S(1)} %copy-done, bf16[16,32,128]{2,1,0:T(8,128)(2,1)S(1)} %copy-done.3, f32[1,128]{1,0:T(1,128)S(1)} %bitcast.13, bf16[8,128]{1,0:T(8,128)(2,1)S(1)} %concatenate.3.wbt_ref), custom_call_target="tpu_custom_call" | custom-call | tf_op jit(solution)/shard_map/pallas_call | solution.py:259
  5.5 11.5 %all-to-all-start = ((bf16[128,40,128]{2,1,0:T(8,128)(2,1)}), bf16[128,40,128]{2,1,0:T(8,128)(2,1)S(1)}, u32[]{:S(2)}, u32[]{:S(2)}) async-start(bf16[128,40,128]{2,1,0:T(8,128)(2,1)} %get-tuple-element.13), calls=%async_computation | async-start | bytes 2621440 | tf_op jit(solution)/shard_map/all_to_all | solution.py:248
  17.0 0.0 copy-done.2
  17.0 0.1 copy.14
  17.2 0.0 copy-done.7
  17.2 22.1 %all-to-all-done = bf16[128,40,128]{2,1,0:T(8,128)(2,1)S(1)} async-done(((bf16[128,40,128]{2,1,0:T(8,128)(2,1)}), bf16[128,40,128]{2,1,0:T(8,128)(2,1)S(1)}, u32[]{:S(2)}, u32[]{:S(2)}) %all-to-all-start) | async-done | bytes 1310752 | tf_op jit(solution)/shard_map/all_to_all | solution.py:248
  39.3 0.1 broadcast_in_dim.2.mask_ref
  39.4 0.0 copy-done.4
  39.4 9.1 %shard_map.111 = bf16[16,8,24,128]{3,2,1,0:T(8,128)(2,1)S(1)} custom-call(bf16[16,8,40,128]{3,2,1,0:T(8,128)(2,1)S(1)} %bitcast.9, bf16[4,128,128]{2,1,0:T(8,128)(2,1)S(1)} %bitcast.11, bf16[128,128]{1,0:T(8,128)(2,1)S(1)} %copy-done.4, f32[256,128]{1,0:T(8,128)S(1)} %broadcast_in_dim.2.mask_ref), custom_call_target="tpu_custom_call" | custom-call | tf_op jit(solution)/shard_map/pallas_call | solution.py:263
  48.5 20.6 %all_to_all.15.recv_ref = bf16[128,24,128]{2,1,0:T(8,128)(2,1)S(1)} all-to-all(bf16[128,24,128]{2,1,0:T(8,128)(2,1)S(1)} %bitcast.10), channel_id=1, replica_groups=mesh['wide'=16,'narrow'=8] {'wide','narrow'}, dimensions={0} | all-to-all | bytes 1572864 | tf_op jit(solution)/shard_map/all_to_all | solution.py:248
  69.1 1.0 %shard_map.112 = (bf16[128,16,128]{2,1,0:T(8,128)(2,1)}, bf16[8,512]{1,0:T(8,128)(2,1)S(1)}) custom-call(bf16[128,24,128]{2,1,0:T(8,128)(2,1)S(1)} %all_to_all.15.recv_ref, bf16[512,128]{1,0:T(8,128)(2,1)S(1)} %get-tuple-element.14.normed_ref), custom_call_target="tpu_custom_call" | custom-call | tf_op jit(solution)/shard_map/pallas_call | solution.py:275
  70.1 3.8 %all-to-all-start.2 = ((bf16[128,16,128]{2,1,0:T(8,128)(2,1)}), bf16[128,16,128]{2,1,0:T(8,128)(2,1)S(1)}, u32[]{:S(2)}, u32[]{:S(2)}) async-start(bf16[128,16,128]{2,1,0:T(8,128)(2,1)} %get-tuple-element.16), calls=%async_computation.2 | async-start | bytes 1048576 | tf_op jit(solution)/shard_map/all_to_all | solution.py:248
  73.9 0.0 copy-done.1
  73.9 0.0 copy-done.6
  73.9 1.2 %shard_map.113 = bf16[16,32,128]{2,1,0:T(8,128)(2,1)} custom-call(bf16[128,24,128]{2,1,0:T(8,128)(2,1)S(1)} %all_to_all.15.recv_ref, bf16[8,512]{1,0:T(8,128)(2,1)S(1)} %get-tuple-element.15.bias_ref, bf16[16,32,128]{2,1,0:T(8,128)(2,1)S(1)} %copy-done.1, f32[1,128]{1,0:T(1,128)S(1)} %bitcast.14, bf16[4,128,128]{2,1,0:T(8,128)(2,1)S(1)} %bitcast.12, ...), custom_call_target="tpu_custom_call" | custom-call | flops 100000000 | bytes 4000000 | tf_op jit(solution)/shard_map/pallas_call | solution.py:277
  75.1 12.8 %all-to-all-done.2.recv_ref = bf16[128,16,128]{2,1,0:T(8,128)(2,1)S(1)} async-done(((bf16[128,16,128]{2,1,0:T(8,128)(2,1)}), bf16[128,16,128]{2,1,0:T(8,128)(2,1)S(1)}, u32[]{:S(2)}, u32[]{:S(2)}) %all-to-all-start.2) | async-done | bytes 524320 | tf_op jit(solution)/shard_map/all_to_all | solution.py:248
  88.0 0.9 %shard_map.114 = (f32[128,512]{1,0:T(8,128)}, f32[128,4]{1,0:T(8,128)S(1)}, f32[128,128]{1,0:T(8,128)}, f32[1,128]{1,0:T(1,128)}) custom-call(bf16[128,16,128]{2,1,0:T(8,128)(2,1)S(1)} %all-to-all-done.2.recv_ref, bf16[128,512]{1,0:T(8,128)(2,1)S(1)} %copy-done.2, bf16[8,128]{1,0:T(8,128)(2,1)S(1)} %concatenate.3.wbt_ref, f32[1,128]{1,0:T(1,128)S(1)} %bitcast.15), custom_call_target="tpu_custom_call" | custom-call | tf_op jit(solution)/shard_map/pallas_call | solution.py:283
  88.9 0.7 copy.16
  (8 shorter events, 0.0 us)
Async XLA Ops:
  1.3 0.9 %copy-start = (bf16[16,32,128]{2,1,0:T(8,128)(2,1)S(1)}, bf16[16,32,128]{2,1,0:T(8,128)(2,1)}, u32[]{:S(2)}) copy-start(bf16[16,32,128]{2,1,0:T(8,128)(2,1)} %pair_ref.3) | copy-start | bytes 393220
  2.2 0.9 %copy-start.3 = (bf16[16,32,128]{2,1,0:T(8,128)(2,1)S(1)}, bf16[16,32,128]{2,1,0:T(8,128)(2,1)}, u32[]{:S(2)}) copy-start(bf16[16,32,128]{2,1,0:T(8,128)(2,1)} %cot_ref.1) | copy-start | bytes 393220
  3.1 0.7 copy-start.5
  5.5 11.5 %copy-start.2 = (bf16[128,512]{1,0:T(8,128)(2,1)S(1)}, bf16[128,512]{1,0:T(8,128)(2,1)}, u32[]{:S(2)}) copy-start(bf16[128,512]{1,0:T(8,128)(2,1)} %pw_ref.1) | copy-start | bytes 393220
  5.5 11.7 %copy-start.7 = (s32[256]{0:T(256)S(1)}, s32[256]{0:T(256)}, u32[]{:S(2)}) copy-start(s32[256]{0:T(256)} %param.13) | copy-start | bytes 3076
  5.5 33.9 %copy-start.4 = (bf16[128,128]{1,0:T(8,128)(2,1)S(1)}, bf16[128,128]{1,0:T(8,128)(2,1)}, u32[]{:S(2)}) copy-start(bf16[128,128]{1,0:T(8,128)(2,1)} %ow_ref.1) | copy-start | bytes 98308
  5.5 33.8 %all-to-all-start = ((bf16[128,40,128]{2,1,0:T(8,128)(2,1)}), bf16[128,40,128]{2,1,0:T(8,128)(2,1)S(1)}, u32[]{:S(2)}, u32[]{:S(2)}) async-start(bf16[128,40,128]{2,1,0:T(8,128)(2,1)} %get-tuple-element.13), calls=%async_computation | async-start | bytes 2621440 | tf_op jit(solution)/shard_map/all_to_all | solution.py:248
  69.1 4.8 %copy-start.1 = (bf16[16,32,128]{2,1,0:T(8,128)(2,1)S(1)}, bf16[16,32,128]{2,1,0:T(8,128)(2,1)}, u32[]{:S(2)}) copy-start(bf16[16,32,128]{2,1,0:T(8,128)(2,1)} %pair_ref.3) | copy-start | bytes 393220
  69.1 4.9 %copy-start.6 = (f32[128]{0:T(128)S(1)}, f32[128]{0:T(128)}, u32[]{:S(2)}) copy-start(f32[128]{0:T(128)} %param.9) | copy-start | bytes 1540
  70.1 17.9 %all-to-all-start.2 = ((bf16[128,16,128]{2,1,0:T(8,128)(2,1)}), bf16[128,16,128]{2,1,0:T(8,128)(2,1)S(1)}, u32[]{:S(2)}, u32[]{:S(2)}) async-start(bf16[128,16,128]{2,1,0:T(8,128)(2,1)} %get-tuple-element.16), calls=%async_computation.2 | async-start | bytes 1048576 | tf_op jit(solution)/shard_map/all_to_all | solution.py:248

commit v2 on v1

v2 whole, which is shorter than its diff:
```python
import jax
import jax.numpy as jnp
from jax import lax
from jax.experimental import pallas as pl
from jax.experimental.pallas import tpu as pltpu
from jax.sharding import Mesh, PartitionSpec as P

NORM_EPSILON = 1e-05
MASK_FILL = 1000000000.0
BF = jnp.bfloat16
F32 = jnp.float32
CHIPS = ("chip", "narrow")
BOTH = ("chip", "core", "narrow")

ROWS = 16
COLS = 32
TILE = ROWS * COLS
N_WIDE = 16
N_CHIP = 8
N_NARROW = 8
DEVICES = N_WIDE * N_NARROW
LENGTH = 256
CH = 128
HEADS = 4
DIM = 32
IN_ROWS = 40
TOGETHER = 4
MID_ROWS = 24
OUT_ROWS = 10

NT = (((1,), (1,)), ((), ()))
NN = (((1,), (0,)), ((), ()))
TN = (((0,), (0,)), ((), ()))


def mm(a, b, dims=NN):
    return lax.dot_general(a, b, dims, preferred_element_type=F32)


def normal(x):
    centered = x - jnp.mean(x, axis=-1, keepdims=True)
    inverse = lax.rsqrt(jnp.mean(centered * centered, axis=-1, keepdims=True) + NORM_EPSILON)
    return centered * inverse, inverse


def lane_group(shape):
    return lax.broadcasted_iota(jnp.int32, shape, 1) // COLS


def pre_kernel(
    pair_hbm, cot_hbm, gain_hbm, wbt_ref, send_ref, normed_ref, pair_v, cot_v, gain_v, xs, cs, sems
):
    copies = [
        pltpu.make_async_copy(src, dst, sems.at[i])
        for i, (src, dst) in enumerate(
            ((pair_hbm, pair_v), (gain_hbm, gain_v), (cot_hbm, cot_v))
        )
    ]
    for copy in copies:
        copy.start()
    copies[0].wait()
    hat, _ = normal(pair_v[...].astype(F32).reshape(TILE, CH))
    copies[1].wait()
    normed = (hat * gain_v[...]).astype(BF)
    normed_ref[...] = normed
    xs[...] = normed.astype(F32)
    bias = mm(wbt_ref[...], normed, NT)
    for pair in range(2):
        rows = [
            bias[h : h + 1, b * CH : (b + 1) * CH]
            for h in (2 * pair, 2 * pair + 1)
            for b in range(4)
        ]
        chunk = jnp.concatenate(rows, axis=0).astype(BF)
        for col in range(COLS):
            send_ref[pair * COLS + col, 32:40, :] = chunk
    copies[2].wait()
    cs[...] = cot_v[...].astype(F32).reshape(TILE, CH)
    for col in range(COLS):
        x = xs[pl.ds(col, ROWS, stride=COLS), :].astype(BF)
        c = cs[pl.ds(col, ROWS, stride=COLS), :].astype(BF)
        for pair in range(2):
            send_ref[pair * COLS + col, 0:16, :] = x
            send_ref[pair * COLS + col, 16:32, :] = c


def attention_kernel(
    own_ref, other_ref, wall_ref, ow_ref, mask_ref, send_ref, bias_s, sum_s, tail_s, grad_s, gout_s
):
    core = lax.axis_index("core")
    head = 2 * (lax.axis_index("chip") // 4) + core
    scale = DIM**-0.5
    weight = wall_ref[head]
    out_w = ow_ref[pl.ds(pl.multiple_of(head * DIM, DIM), DIM), :]
    zero = jnp.zeros((DIM, CH), BF)

    def rows(n, start, stop):
        own, other = own_ref[:, n, start:stop, :], other_ref[:, n, start:stop, :]
        low, high = jnp.where(core == 0, own, other), jnp.where(core == 0, other, own)
        return jnp.stack([low, high], axis=1)

    group = lane_group((64, CH))
    for half in range(2):
        got = []
        for q in range(4):
            both = rows(half * 4 + q, 32, 40).astype(F32).reshape(N_WIDE, 8, CH)
            got.append(jnp.where(core == 0, both[:, 0:4], both[:, 4:8]).reshape(64, CH))
        for kq in range(4):
            acc = jnp.zeros((64, CH), F32)
            for q in range(4):
                shift = (q - kq) * COLS % CH
                acc = jnp.where(group == q, pltpu.roll(got[q], shift, 1) if shift else got[q], acc)
            bias_s.at[half][pl.ds(kq, 64, stride=4), :] = acc

    class Unit:
        pass

    def project(n):
        u = Unit()
        u.n = n
        u.x = rows(n, 0, 16).reshape(LENGTH, CH)
        u.cot = rows(n, 16, 32).reshape(LENGTH, CH)
        projected = mm(weight, u.x, NT)
        u.kv = mm(u.x, weight[DIM : 3 * DIM], NT).astype(BF)
        u.q, u.k, u.v = [projected[DIM * t : DIM * (t + 1)].astype(BF) for t in range(3)]
        u.gate = jax.nn.sigmoid(projected[3 * DIM :])
        u.og = mm(out_w, u.cot, NT)
        u.da = (u.og * u.gate).astype(BF)
        return u

    def score(u, half):
        part = slice(half * CH, (half + 1) * CH)
        h = Unit()
        h.half, h.q, h.da, h.v, h.n = half, u.q[:, part], u.da[:, part], u.v, u.n
        right = jnp.concatenate(
            [
                jnp.concatenate([h.q, zero], axis=1),
                jnp.concatenate([zero, h.da], axis=1),
            ],
            axis=0,
        )
        both = mm(u.kv, right)
        h.logits, h.d_soft = both[:, :CH], both[:, CH:]
        return h

    def softmax(h):
        logits = h.logits * scale + bias_s[h.half] + mask_ref[...]
        top = jnp.max(logits, axis=0, keepdims=True)
        e = jnp.exp(logits - top)
        h.soft = e * (1.0 / jnp.sum(e, axis=0, keepdims=True))
        h.soft_bf = h.soft.astype(BF)

    def attend(h):
        h.att = mm(h.v, h.soft_bf)
        h.delta = jnp.sum(h.da.astype(F32) * h.att, axis=0, keepdims=True)

    def logit_grads(h):
        h.d_log = (h.soft * (h.d_soft - h.delta)).astype(BF)
        if h.n == 0:
            sum_s[h.half] = h.d_log.astype(F32)
        else:
            sum_s[h.half] += h.d_log.astype(F32)

    def gradients(u, halves):
        d_log = jnp.concatenate([h.d_log for h in halves], axis=1)
        soft_bf = jnp.concatenate([h.soft_bf for h in halves], axis=1)
        att = jnp.concatenate([h.att for h in halves], axis=1)
        dq = mm(u.k, d_log) * scale
        dk = mm(u.q, d_log, NT) * scale
        dv = mm(u.da, soft_bf, NT)
        dg = u.og * att * u.gate * (1.0 - u.gate)
        u.grads = jnp.concatenate([dq, dk, dv, dg], axis=0).astype(BF)
        u.gated = (u.gate * att).astype(BF)

    def emit(u):
        part = mm(u.grads, u.x)
        out_part = mm(u.gated, u.cot)
        if u.n == 0:
            grad_s[...] = part
            gout_s[...] = out_part
        else:
            grad_s[...] += part
            gout_s[...] += out_part
        turned = jnp.transpose(u.grads.astype(F32)).astype(BF)
        send_ref[:, u.n, 0:16, :] = turned.reshape(N_WIDE, ROWS, CH)

    for first in range(0, N_NARROW, TOGETHER):
        units = [project(n) for n in range(first, first + TOGETHER)]
        pieces = [[score(u, half) for half in range(2)] for u in units]
        flat = [h for halves in pieces for h in halves]
        for step in (softmax, attend, logit_grads):
            for h in flat:
                step(h)
        for u, halves in zip(units, pieces):
            gradients(u, halves)
        for u in units:
            emit(u)

    tail_s[...] = jnp.zeros_like(tail_s)
    for n in range(N_NARROW):
        half, q = n // 4, n % 4
        acc = jnp.zeros((64, CH), F32)
        for kq in range(4):
            got = sum_s.at[half][pl.ds(kq, 64, stride=4), :]
            shift = (kq - q) * COLS % CH
            acc = jnp.where(group == kq, pltpu.roll(got, shift, 1) if shift else got, acc)
        for w in range(N_WIDE):
            at = (w * N_NARROW + n) * 8
            tail_s[at : at + 4, :] = acc[w * 4 : (w + 1) * 4, :]
    tail_s[pl.ds(4, DEVICES, stride=8), :] = jnp.transpose(grad_s[...])
    out_part = gout_s[...]
    for r in range(4):
        tail_s[pl.ds(5 + 8 * r, DIM, stride=32), :] = out_part
    tail = tail_s[...].astype(BF).reshape(N_WIDE, N_NARROW, 8, CH)
    send_ref[:, :, 16:24, :] = tail


def of_head(recv_ref, h, start, stop):
    got = recv_ref[h // 2, :, h % 2, :, start:stop, :]
    return got.reshape(COLS, stop - start, CH)


def reduce_kernel(recv_ref, normed_ref, send_ref, bias_ref):
    sums = [jnp.sum(of_head(recv_ref, h, 16, 24).astype(F32), axis=0) for h in range(HEADS)]
    blocks = [
        jnp.concatenate([sums[h][b : b + 1] for h in range(HEADS)], axis=0) for b in range(4)
    ]
    bias = jnp.concatenate(blocks, axis=1)
    bias = jnp.concatenate([bias, jnp.zeros_like(bias)], axis=0).astype(BF)
    bias_ref[...] = bias
    grad_bias = mm(bias, normed_ref[...])[:HEADS]
    group = lane_group((1, CH))
    rows = []
    for t in range(4):
        row = jnp.zeros((1, CH), F32)
        for h in range(HEADS):
            shift = (h - t) * COLS % CH
            got = sums[h][4:5]
            row = jnp.where(group == h, pltpu.roll(got, shift, 1) if shift else got, row)
        rows.append(row)
    place = lax.rem(lax.axis_index("narrow"), 4)
    row = jnp.zeros((1, CH), F32)
    for h in range(HEADS):
        shift = lax.rem(h * COLS + CH - place * COLS, CH)
        row = jnp.where(group == h, pltpu.roll(sums[h][5:6], shift, 1), row)
    rows += [row, jnp.zeros((1, CH), F32), grad_bias]
    chunk = jnp.concatenate(rows, axis=0)
    block = jnp.concatenate([chunk] * 8, axis=0).astype(BF)
    for i in range(DEVICES // 8):
        send_ref[i * 80 : (i + 1) * 80, :] = block


def pair_kernel(recv_ref, bias_ref, pair_ref, gain_ref, wall_ref, wbt_ref, out_ref, ds):
    total = jnp.zeros((TILE, CH), F32)
    for h in range(HEADS):
        g = of_head(recv_ref, h, 0, 16).reshape(TILE, CH)
        total = total + mm(g, wall_ref[h])
    ds[...] = total
    d_normed = jnp.concatenate([ds[pl.ds(r, COLS, stride=ROWS), :] for r in range(ROWS)], axis=0)
    wbt = wbt_ref[...].astype(F32)
    wbt = jnp.concatenate([wbt, jnp.zeros_like(wbt)], axis=0).astype(BF)
    d_normed = d_normed + mm(bias_ref[...], wbt, TN)
    hat, inverse = normal(pair_ref[...].astype(F32).reshape(TILE, CH))
    d_hat = d_normed * gain_ref[...]
    d_pair = inverse * (
        d_hat
        - jnp.mean(d_hat, axis=-1, keepdims=True)
        - hat * jnp.mean(d_hat * hat, axis=-1, keepdims=True)
    )
    out_ref[...] = d_pair.astype(BF).reshape(ROWS, COLS, CH)


def final_kernel(recv_ref, pw_ref, wbt_ref, gain_ref, gp_ref, gb_ref, go_ref, gg_ref, vs):
    vs[...] = recv_ref[...].astype(F32)
    dots = jnp.zeros((CH, CH), F32)
    for t in range(4):
        got = vs[pl.ds(t, CH, stride=OUT_ROWS), :]
        gp_ref[:, t * CH : (t + 1) * CH] = got
        dots = dots + got * pw_ref[:, t * CH : (t + 1) * CH].astype(F32)
    group = lane_group((DIM, CH))
    quarters = [vs[pl.ds(OUT_ROWS * q + 4, DIM, stride=4 * OUT_ROWS), :] for q in range(4)]
    for h in range(HEADS):
        acc = jnp.zeros((DIM, CH), F32)
        for q in range(4):
            shift = (q - h) * COLS % CH
            got = pltpu.roll(quarters[q], shift, 1) if shift else quarters[q]
            acc = jnp.where(group == q, got, acc)
        go_ref[h * DIM : (h + 1) * DIM, :] = acc
    grad_bias = jnp.concatenate(
        [
            jnp.sum(vs[pl.ds(6 + h, DEVICES, stride=OUT_ROWS), :], axis=0, keepdims=True)
            for h in range(HEADS)
        ],
        axis=0,
    )
    gb_ref[...] = grad_bias
    dots_row = jnp.sum(jnp.transpose(dots), axis=0, keepdims=True)
    bias_row = jnp.sum(grad_bias * wbt_ref[...].astype(F32), axis=0, keepdims=True)
    gg_ref[...] = (dots_row + bias_row) / gain_ref[...]


def call(kernel, out_shape, scratch=(), cost=None, outside=0):
    many = isinstance(out_shape, (list, tuple))
    spec = pl.BlockSpec(memory_space=pltpu.VMEM)

    def run(*args):
        specs = [
            pl.BlockSpec(memory_space=pltpu.HBM) if i < outside else spec for i in range(len(args))
        ]
        return pl.pallas_call(
            kernel,
            out_shape=out_shape,
            in_specs=specs,
            out_specs=[spec] * len(out_shape) if many else spec,
            scratch_shapes=list(scratch),
            compiler_params=pltpu.CompilerParams(vmem_limit_bytes=32 * 1024 * 1024),
            cost_estimate=cost,
        )(*args)

    return run


def shape(*dims, dtype=BF):
    return jax.ShapeDtypeStruct(dims, dtype)


def local(pair_rep, cotangent, norm_gain, proj_weight, bias_weight, out_weight, residue_mask):
    gain = norm_gain.reshape(1, CH)
    wbt = bias_weight.T
    wall = proj_weight.reshape(CH, 4, HEADS, DIM).transpose(2, 1, 3, 0).reshape(HEADS, CH, CH)
    masking = (residue_mask.astype(F32) - 1.0) * MASK_FILL
    masking = jnp.broadcast_to(masking[:, None], (LENGTH, CH))
    tile_f32 = pltpu.VMEM((TILE, CH), F32)

    send, normed = call(
        pre_kernel,
        [shape(DEVICES // 2, IN_ROWS, CH), shape(TILE, CH)],
        [
            pltpu.VMEM((ROWS, COLS, CH), BF),
            pltpu.VMEM((ROWS, COLS, CH), BF),
            pltpu.VMEM((1, CH), F32),
            tile_f32,
            tile_f32,
            pltpu.SemaphoreType.DMA((3,)),
        ],
        outside=3,
    )(pair_rep, cotangent, gain, wbt)
    own = lax.all_to_all(send, CHIPS, 0, 0, tiled=True)
    other = lax.ppermute(own, "core", [(0, 1), (1, 0)])
    mid = call(
        attention_kernel,
        shape(N_WIDE, N_NARROW, MID_ROWS, CH),
        [
            pltpu.VMEM((2, LENGTH, CH), F32),
            pltpu.VMEM((2, LENGTH, CH), F32),
            pltpu.VMEM((DEVICES * 8, CH), F32),
            pltpu.VMEM((CH, CH), F32),
            pltpu.VMEM((DIM, CH), F32),
        ],
    )(
        own.reshape(N_CHIP, N_NARROW, IN_ROWS, CH),
        other.reshape(N_CHIP, N_NARROW, IN_ROWS, CH),
        wall,
        out_weight,
        masking,
    )
    mid = lax.all_to_all(mid.reshape(DEVICES, MID_ROWS, CH), BOTH, 0, 0, tiled=True)
    mid = mid.reshape(2, N_CHIP // 2, 2, N_NARROW, MID_ROWS, CH)
    send, bias = call(reduce_kernel, [shape(DEVICES * OUT_ROWS, CH), shape(8, TILE)])(mid, normed)
    last = lax.all_to_all(send.reshape(DEVICES, OUT_ROWS // 2, 2, CH), BOTH, 0, 0, tiled=True)
    d_pair = call(
        pair_kernel,
        shape(ROWS, COLS, CH),
        [tile_f32],
        pl.CostEstimate(flops=100_000_000, bytes_accessed=4_000_000, transcendentals=512),
    )(mid, bias, pair_rep, gain, wall, wbt)
    grad_proj, grad_bias, grad_out, grad_gain = call(
        final_kernel,
        [
            shape(CH, 4 * CH, dtype=F32),
            shape(HEADS, CH, dtype=F32),
            shape(CH, CH, dtype=F32),
            shape(1, CH, dtype=F32),
        ],
        [pltpu.VMEM((DEVICES * OUT_ROWS, CH), F32)],
    )(last.reshape(DEVICES * OUT_ROWS, CH), proj_weight, wbt, gain)
    return (d_pair, grad_proj, grad_bias.T, grad_out, grad_gain.reshape(CH))


def solution(mesh):
    cores = Mesh(mesh.devices.reshape(N_CHIP, 2, N_NARROW), BOTH)
    tile = P(("chip", "core"), "narrow", None)
    in_specs = (tile, tile, P(), P(), P(), P(), P())
    out_specs = (tile, P(), P(), P(), P())
    return jax.shard_map(local, mesh=cores, in_specs=in_specs, out_specs=out_specs, check_vma=False)
```

time: 89.9 us -> 75.1 us (0.84)
  blocking collectives: 20.6 us -> 45.9 us
  waiting for transfers between devices: 34.9 us -> 11.8 us
  starting transfers between devices: 15.3 us -> 6 us
  Pallas kernels: 13.9 us -> 7 us
    all_to_all x1 -> x2, blocking collectives: 20.6 us -> 45.9 us  [the longest x1 25.3 us: local(): own = lax.all_to_all(send, CHIPS, 0, 0, tiled=True)]
    all_to_all x2 -> x1, waiting for transfers between devices: 34.9 us -> 10.9 us  [local(): lax.all_to_all(send.reshape(DEVICES, OUT_ROWS // 2, 2, CH), BOTH, 0, 0, t...]
    all_to_all x2 -> x1, starting transfers between devices: 15.3 us -> 3.84 us  [local(): lax.all_to_all(send.reshape(DEVICES, OUT_ROWS // 2, 2, CH), BOTH, 0, 0, t...]
    pallas_call x5, Pallas kernels: 13.9 us -> 7 us  [run(): pl.pallas_call(kernel, out_shape=out_shape, in_specs=specs, out_specs=[sp...]
    ppermute x0 -> x1, starting transfers between devices: none -> 2.16 us  [local(): other = lax.ppermute(own, 'core', [(0, 1), (1, 0)])]
    ppermute x0 -> x1, waiting for transfers between devices: none -> 0.91 us  [local(): other = lax.ppermute(own, 'core', [(0, 1), (1, 0)])]
    unnamed x18 -> x17, local copies, waits for them, and re-layouts: 3.25 us -> 3.26 us
  transfers between devices with their start and end apart: 2 -> 2, of which waited for: 2 -> 2; matrix products, arithmetic and copies ran while one was open for 0% -> 0% of each run, Pallas kernels for 1% -> 2%
where the time goes in v2:
time: 75.1 us; the launch traced here: 74.8 us
  blocking collectives  45.9 us (61%)
  waiting for transfers between devices  11.8 us (16%)
  Pallas kernels  7 us (9%)
  starting transfers between devices  6 us (8%)
  local copies, waits for them, and re-layouts  3.36 us (4%)
    all_to_all x1, blocking collectives, local(): own = lax.all_to_all(send, CHIPS, 0, 0, tiled=True)  25.3 us
    all_to_all x1, blocking collectives, local(): lax.all_to_all(mid.reshape(DEVICES, MID_ROWS, CH), BOTH, 0, 0, tiled=True)  20.6 us
    all_to_all x1, waiting for transfers between devices, local(): lax.all_to_all(send.reshape(DEVICES, OUT_ROWS // 2, 2, CH), BOTH, 0, 0, t...  10.9 us
    pallas_call x5, Pallas kernels, run(): pl.pallas_call(kernel, out_shape=out_shape, in_specs=specs, out_specs=[sp...  7 us
    all_to_all x1, starting transfers between devices, local(): lax.all_to_all(send.reshape(DEVICES, OUT_ROWS // 2, 2, CH), BOTH, 0, 0, t...  3.84 us
    unnamed x17, local copies, waits for them, and re-layouts  3.26 us
    ppermute x1, starting transfers between devices, local(): other = lax.ppermute(own, 'core', [(0, 1), (1, 0)])  2.16 us
  transfers between devices with their start and end apart: 2, of which 2 were waited for; matrix products, arithmetic and copies ran while one was open for 0% of the time, Pallas kernels for 2%

profile of v2, /device:TPU:1, one launch (start us, length us, event | category | flops | bytes accessed | tf_op | source)
XLA Modules:
  0.0 74.8 jit_solution(704246153073945684)
XLA Ops:
  0.6 0.0 copy-start.5
  0.6 0.0 copy-start.6
  0.7 0.7 copy-done.5
  1.3 0.0 copy-done.6
  1.3 0.9 %copy-done = bf16[16,32,128]{2,1,0:T(8,128)(2,1)S(1)} copy-done((bf16[16,32,128]{2,1,0:T(8,128)(2,1)S(1)}, bf16[16,32,128]{2,1,0:T(8,128)(2,1)}, u32[]{:S(2)}) %copy-start) | copy-done | bytes 131096
  2.2 0.9 %copy-done.3 = bf16[16,32,128]{2,1,0:T(8,128)(2,1)S(1)} copy-done((bf16[16,32,128]{2,1,0:T(8,128)(2,1)S(1)}, bf16[16,32,128]{2,1,0:T(8,128)(2,1)}, u32[]{:S(2)}) %copy-start.3) | copy-done | bytes 131096
  3.1 1.1 %shard_map.110 = (bf16[64,40,128]{2,1,0:T(8,128)(2,1)S(1)}, bf16[512,128]{1,0:T(8,128)(2,1)S(1)}) custom-call(bf16[16,32,128]{2,1,0:T(8,128)(2,1)S(1)} %copy-done, bf16[16,32,128]{2,1,0:T(8,128)(2,1)S(1)} %copy-done.3, f32[1,128]{1,0:T(1,128)S(1)} %bitcast.25, bf16[4,128]{1,0:T(4,128)(2,1)S(1)} %bitcast.22), custom_call_target="tpu_custom_call" | custom-call | tf_op jit(solution)/shard_map/pallas_call | solution.py:310
  4.2 0.0 copy-start.2
  4.2 25.3 %all_to_all.15 = bf16[64,40,128]{2,1,0:T(8,128)(2,1)S(1)} all-to-all(bf16[64,40,128]{2,1,0:T(8,128)(2,1)S(1)} %get-tuple-element.13), channel_id=1, replica_groups=mesh['chip'=8,'core'=2,'narrow'=8] {'chip','narrow'}, dimensions={0} | all-to-all | bytes 1310720 | tf_op jit(solution)/shard_map/all_to_all | solution.py:348
  29.5 2.2 %collective-permute-start = (bf16[64,40,128]{2,1,0:T(8,128)(2,1)S(1)}, bf16[64,40,128]{2,1,0:T(8,128)(2,1)S(1)}, u32[]{:S(2)}, u32[]{:S(2)}) collective-permute-start(bf16[64,40,128]{2,1,0:T(8,128)(2,1)S(1)} %all_to_all.15), channel_id=1, source_target_pairs={{0,8},{8,0},{1,9},{9,1},{2,10},{10,2},{3,11},{11,3},{4,12},{12,4},... | collective-permute-start | bytes 1966088 | tf_op jit(solution)/shard_map/ppermute | solution.py:349
  31.7 0.0 copy-done.2
  31.7 0.1 copy.13
  31.8 0.0 copy-start.7
  31.9 0.7 copy-done.7
  32.5 0.9 %collective-permute-done = bf16[64,40,128]{2,1,0:T(8,128)(2,1)S(1)} collective-permute-done((bf16[64,40,128]{2,1,0:T(8,128)(2,1)S(1)}, bf16[64,40,128]{2,1,0:T(8,128)(2,1)S(1)}, u32[]{:S(2)}, u32[]{:S(2)}) %collective-permute-start) | collective-permute-done | bytes 655392 | tf_op jit(solution)/shard_map/ppermute | solution.py:349
  33.4 0.1 broadcast_in_dim.2.mask_ref
  33.5 3.0 %shard_map.111 = bf16[16,8,24,128]{3,2,1,0:T(8,128)(2,1)S(1)} custom-call(bf16[8,8,40,128]{3,2,1,0:T(8,128)(2,1)S(1)} %bitcast.17, bf16[8,8,40,128]{3,2,1,0:T(8,128)(2,1)S(1)} %bitcast.21, bf16[4,128,128]{2,1,0:T(8,128)(2,1)S(1)} %bitcast.19, bf16[128,128]{1,0:T(8,128)(2,1)S(1)} %copy-done.4, f32[256,128]{1,0:T(8,128)S(1)} %broadcast_in_dim.2.mask_ref), custom_call_target="tpu_custom_call" | custom-call | tf_op jit(solution)/shard_map/pallas_call | solution.py:310
  36.6 20.6 %all_to_all.16 = bf16[128,24,128]{2,1,0:T(8,128)(2,1)S(1)} all-to-all(bf16[128,24,128]{2,1,0:T(8,128)(2,1)S(1)} %bitcast.16), channel_id=1, replica_groups=mesh['chip'=8,'core'=2,'narrow'=8] {'chip','core','narrow'}, dimensions={0} | all-to-all | bytes 1572864 | tf_op jit(solution)/shard_map/all_to_all | solution.py:367
  57.2 0.9 %shard_map.112 = (bf16[1280,128]{1,0:T(8,128)(2,1)}, bf16[8,512]{1,0:T(8,128)(2,1)S(1)}) custom-call(bf16[2,4,2,8,24,128]{5,4,3,2,1,0:T(8,128)(2,1)S(1)} %bitcast.14, bf16[512,128]{1,0:T(8,128)(2,1)S(1)} %get-tuple-element.14.normed_ref), custom_call_target="tpu_custom_call" | custom-call | tf_op jit(solution)/shard_map/pallas_call | solution.py:310
  58.1 3.8 %all-to-all-start.2 = ((bf16[128,5,2,128]{3,2,1,0:T(2,128)(2,1)}), bf16[128,5,2,128]{3,2,1,0:T(2,128)(2,1)S(1)}, u32[]{:S(2)}, u32[]{:S(2)}) async-start(bf16[128,5,2,128]{3,2,1,0:T(2,128)(2,1)} %bitcast.9), calls=%async_computation.2 | async-start | bytes 655360 | tf_op jit(solution)/shard_map/all_to_all | solution.py:370
  61.9 0.0 copy-done.1
  61.9 1.2 %shard_map.113 = bf16[16,32,128]{2,1,0:T(8,128)(2,1)} custom-call(bf16[2,4,2,8,24,128]{5,4,3,2,1,0:T(8,128)(2,1)S(1)} %bitcast.15, bf16[8,512]{1,0:T(8,128)(2,1)S(1)} %get-tuple-element.15.bias_ref, bf16[16,32,128]{2,1,0:T(8,128)(2,1)S(1)} %copy-done.1, f32[1,128]{1,0:T(1,128)S(1)} %bitcast.26, bf16[4,128,128]{2,1,0:T(8,128)(2,1)S(1)} %bitcast.20, ...), custom_call_target="tpu_custom_call" | custom-call | flops 100000000 | bytes 4000000 | tf_op jit(solution)/shard_map/pallas_call | solution.py:310
  63.1 10.9 %all-to-all-done.2 = bf16[128,5,2,128]{3,2,1,0:T(2,128)(2,1)S(1)} async-done(((bf16[128,5,2,128]{3,2,1,0:T(2,128)(2,1)}), bf16[128,5,2,128]{3,2,1,0:T(2,128)(2,1)S(1)}, u32[]{:S(2)}, u32[]{:S(2)}) %all-to-all-start.2) | async-done | bytes 327712 | tf_op jit(solution)/shard_map/all_to_all | solution.py:370
  74.0 0.8 %shard_map.114 = (f32[128,512]{1,0:T(8,128)}, f32[4,128]{1,0:T(4,128)}, f32[128,128]{1,0:T(8,128)}, f32[1,128]{1,0:T(1,128)}) custom-call(bf16[1280,128]{1,0:T(8,128)(2,1)S(1)} %bitcast.18, bf16[128,512]{1,0:T(8,128)(2,1)S(1)} %copy-done.2, bf16[4,128]{1,0:T(4,128)(2,1)S(1)} %bitcast.24, f32[1,128]{1,0:T(1,128)S(1)} %bitcast.27), custom_call_target="tpu_custom_call" | custom-call | tf_op jit(solution)/shard_map/pallas_call | solution.py:310
  (7 shorter events, 0.0 us)
Async XLA Ops:
  0.6 0.7 copy-start.5
  0.6 0.7 copy-start.6
  1.3 0.9 %copy-start = (bf16[16,32,128]{2,1,0:T(8,128)(2,1)S(1)}, bf16[16,32,128]{2,1,0:T(8,128)(2,1)}, u32[]{:S(2)}) copy-start(bf16[16,32,128]{2,1,0:T(8,128)(2,1)} %pair_ref.1) | copy-start | bytes 393220
  2.2 0.9 %copy-start.3 = (bf16[16,32,128]{2,1,0:T(8,128)(2,1)S(1)}, bf16[16,32,128]{2,1,0:T(8,128)(2,1)}, u32[]{:S(2)}) copy-start(bf16[16,32,128]{2,1,0:T(8,128)(2,1)} %cot_hbm.1) | copy-start | bytes 393220
  4.2 27.5 %copy-start.2 = (bf16[128,512]{1,0:T(8,128)(2,1)S(1)}, bf16[128,512]{1,0:T(8,128)(2,1)}, u32[]{:S(2)}) copy-start(bf16[128,512]{1,0:T(8,128)(2,1)} %pw_ref.1) | copy-start | bytes 393220
  29.5 3.9 %collective-permute-start = (bf16[64,40,128]{2,1,0:T(8,128)(2,1)S(1)}, bf16[64,40,128]{2,1,0:T(8,128)(2,1)S(1)}, u32[]{:S(2)}, u32[]{:S(2)}) collective-permute-start(bf16[64,40,128]{2,1,0:T(8,128)(2,1)S(1)} %all_to_all.15), channel_id=1, source_target_pairs={{0,8},{8,0},{1,9},{9,1},{2,10},{10,2},{3,11},{11,3},{4,12},{12,4},... | collective-permute-start | bytes 1966088 | tf_op jit(solution)/shard_map/ppermute | solution.py:349
  31.8 0.7 copy-start.7
  32.5 1.0 %copy-start.4 = (bf16[128,128]{1,0:T(8,128)(2,1)S(1)}, bf16[128,128]{1,0:T(8,128)(2,1)}, u32[]{:S(2)}) copy-start(bf16[128,128]{1,0:T(8,128)(2,1)} %ow_ref.1) | copy-start | bytes 98308
  58.1 3.8 %copy-start.1 = (bf16[16,32,128]{2,1,0:T(8,128)(2,1)S(1)}, bf16[16,32,128]{2,1,0:T(8,128)(2,1)}, u32[]{:S(2)}) copy-start(bf16[16,32,128]{2,1,0:T(8,128)(2,1)} %pair_ref.1) | copy-start | bytes 393220
  58.1 16.0 %all-to-all-start.2 = ((bf16[128,5,2,128]{3,2,1,0:T(2,128)(2,1)}), bf16[128,5,2,128]{3,2,1,0:T(2,128)(2,1)S(1)}, u32[]{:S(2)}, u32[]{:S(2)}) async-start(bf16[128,5,2,128]{3,2,1,0:T(2,128)(2,1)} %bitcast.9), calls=%async_computation.2 | async-start | bytes 655360 | tf_op jit(solution)/shard_map/all_to_all | solution.py:370

commit v3 on v2

--- a/solution.py
+++ b/solution.py
@@ -299,7 +299,7 @@
     gg_ref[...] = (dots_row + bias_row) / gain_ref[...]
 
 
-def call(kernel, out_shape, scratch=(), cost=None, outside=0):
+def call(kernel, out_shape, scratch=(), cost=None, outside=0, vmem=32):
     many = isinstance(out_shape, (list, tuple))
     spec = pl.BlockSpec(memory_space=pltpu.VMEM)
 
@@ -313,7 +313,7 @@
             in_specs=specs,
             out_specs=[spec] * len(out_shape) if many else spec,
             scratch_shapes=list(scratch),
-            compiler_params=pltpu.CompilerParams(vmem_limit_bytes=32 * 1024 * 1024),
+            compiler_params=pltpu.CompilerParams(vmem_limit_bytes=vmem * 1024 * 1024),
             cost_estimate=cost,
         )(*args)
 
@@ -344,6 +344,7 @@
             pltpu.SemaphoreType.DMA((3,)),
         ],
         outside=3,
+        vmem=63,
     )(pair_rep, cotangent, gain, wbt)
     own = lax.all_to_all(send, CHIPS, 0, 0, tiled=True)
     other = lax.ppermute(own, "core", [(0, 1), (1, 0)])

time: 75.1 us -> 75.1 us (level)
  Pallas kernels: 7 us -> 9.14 us
  local copies, waits for them, and re-layouts: 3.36 us -> 1.55 us
    pallas_call x5, Pallas kernels: 7 us -> 9.14 us  [run(): pl.pallas_call(kernel, out_shape=out_shape, in_specs=specs, out_specs=[sp...]
    unnamed x17 -> x15, local copies, waits for them, and re-layouts: 3.26 us -> 1.45 us
where the time goes in v3:
time: 75.1 us; the launch traced here: 74.7 us
  blocking collectives  46.1 us (61%)
  waiting for transfers between devices  11.1 us (15%)
  Pallas kernels  9.14 us (12%)
  starting transfers between devices  6 us (8%)
  local copies, waits for them, and re-layouts  1.55 us (2%)
    all_to_all x1, blocking collectives, local(): own = lax.all_to_all(send, CHIPS, 0, 0, tiled=True)  25.6 us
    all_to_all x1, blocking collectives, local(): lax.all_to_all(mid.reshape(DEVICES, MID_ROWS, CH), BOTH, 0, 0, tiled=True)  20.6 us
    all_to_all x1, waiting for transfers between devices, local(): lax.all_to_all(send.reshape(DEVICES, OUT_ROWS // 2, 2, CH), BOTH, 0, 0, t...  10.2 us
    pallas_call x5, Pallas kernels, run(): pl.pallas_call(kernel, out_shape=out_shape, in_specs=specs, out_specs=[sp...  9.14 us
    all_to_all x1, starting transfers between devices, local(): lax.all_to_all(send.reshape(DEVICES, OUT_ROWS // 2, 2, CH), BOTH, 0, 0, t...  3.84 us
    ppermute x1, starting transfers between devices, local(): other = lax.ppermute(own, 'core', [(0, 1), (1, 0)])  2.16 us
  transfers between devices with their start and end apart: 2, of which 2 were waited for; matrix products, arithmetic and copies ran while one was open for 0% of the time, Pallas kernels for 2%

profile of v3, /device:TPU:1, one launch (start us, length us, event | category | flops | bytes accessed | tf_op | source)
XLA Modules:
  0.0 74.7 jit_solution(2374580083984433176)
XLA Ops:
  0.6 3.2 %shard_map.110 = (bf16[64,40,128]{2,1,0:T(8,128)(2,1)}, bf16[512,128]{1,0:T(8,128)(2,1)}) custom-call(bf16[16,32,128]{2,1,0:T(8,128)(2,1)} %pair_ref.1, bf16[16,32,128]{2,1,0:T(8,128)(2,1)} %cot_hbm.1, f32[1,128]{1,0:T(1,128)} %bitcast.25, bf16[4,128]{1,0:T(4,128)(2,1)} %bitcast.22), custom_call_target="tpu_custom_call" | custom-call | tf_op jit(solution)/shard_map/pallas_call | solution.py:310
  3.8 0.0 copy-start.1
  3.8 25.6 %all_to_all.15 = bf16[64,40,128]{2,1,0:T(8,128)(2,1)S(1)} all-to-all(bf16[64,40,128]{2,1,0:T(8,128)(2,1)} %get-tuple-element.13), channel_id=1, replica_groups=mesh['chip'=8,'core'=2,'narrow'=8] {'chip','narrow'}, dimensions={0} | all-to-all | bytes 1310720 | tf_op jit(solution)/shard_map/all_to_all | solution.py:349
  29.4 2.2 %collective-permute-start = (bf16[64,40,128]{2,1,0:T(8,128)(2,1)S(1)}, bf16[64,40,128]{2,1,0:T(8,128)(2,1)S(1)}, u32[]{:S(2)}, u32[]{:S(2)}) collective-permute-start(bf16[64,40,128]{2,1,0:T(8,128)(2,1)S(1)} %all_to_all.15), channel_id=1, source_target_pairs={{0,8},{8,0},{1,9},{9,1},{2,10},{10,2},{3,11},{11,3},{4,12},{12,4},... | collective-permute-start | bytes 1966088 | tf_op jit(solution)/shard_map/ppermute | solution.py:350
  31.5 0.0 copy-done.1
  31.5 0.1 copy.13
  31.7 0.0 copy-start.6
  31.7 0.7 copy-done.6
  32.4 0.9 %collective-permute-done = bf16[64,40,128]{2,1,0:T(8,128)(2,1)S(1)} collective-permute-done((bf16[64,40,128]{2,1,0:T(8,128)(2,1)S(1)}, bf16[64,40,128]{2,1,0:T(8,128)(2,1)S(1)}, u32[]{:S(2)}, u32[]{:S(2)}) %collective-permute-start) | collective-permute-done | bytes 655392 | tf_op jit(solution)/shard_map/ppermute | solution.py:350
  33.3 0.1 broadcast_in_dim.2.mask_ref
  33.4 0.0 copy-done.3
  33.4 3.0 %shard_map.111 = bf16[16,8,24,128]{3,2,1,0:T(8,128)(2,1)S(1)} custom-call(bf16[8,8,40,128]{3,2,1,0:T(8,128)(2,1)S(1)} %bitcast.17, bf16[8,8,40,128]{3,2,1,0:T(8,128)(2,1)S(1)} %bitcast.21, bf16[4,128,128]{2,1,0:T(8,128)(2,1)S(1)} %bitcast.19, bf16[128,128]{1,0:T(8,128)(2,1)S(1)} %copy-done.3, f32[256,128]{1,0:T(8,128)S(1)} %broadcast_in_dim.2.mask_ref), custom_call_target="tpu_custom_call" | custom-call | tf_op jit(solution)/shard_map/pallas_call | solution.py:310
  36.4 0.0 copy-start.2
  36.4 20.6 %all_to_all.16 = bf16[128,24,128]{2,1,0:T(8,128)(2,1)S(1)} all-to-all(bf16[128,24,128]{2,1,0:T(8,128)(2,1)S(1)} %bitcast.16), channel_id=1, replica_groups=mesh['chip'=8,'core'=2,'narrow'=8] {'chip','core','narrow'}, dimensions={0} | all-to-all | bytes 1572864 | tf_op jit(solution)/shard_map/all_to_all | solution.py:368
  57.0 0.0 copy-done.2
  57.0 0.9 %shard_map.112 = (bf16[1280,128]{1,0:T(8,128)(2,1)}, bf16[8,512]{1,0:T(8,128)(2,1)S(1)}) custom-call(bf16[2,4,2,8,24,128]{5,4,3,2,1,0:T(8,128)(2,1)S(1)} %bitcast.14, bf16[512,128]{1,0:T(8,128)(2,1)S(1)} %copy-done.2), custom_call_target="tpu_custom_call" | custom-call | tf_op jit(solution)/shard_map/pallas_call | solution.py:310
  57.9 3.8 %all-to-all-start.2 = ((bf16[128,5,2,128]{3,2,1,0:T(2,128)(2,1)}), bf16[128,5,2,128]{3,2,1,0:T(2,128)(2,1)S(1)}, u32[]{:S(2)}, u32[]{:S(2)}) async-start(bf16[128,5,2,128]{3,2,1,0:T(2,128)(2,1)} %bitcast.9), calls=%async_computation.2 | async-start | bytes 655360 | tf_op jit(solution)/shard_map/all_to_all | solution.py:371
  61.8 0.0 copy-start.4
  61.8 0.0 copy-start.5
  61.8 0.0 copy-done
  61.8 0.6 copy-done.4
  62.5 1.2 %shard_map.113 = bf16[16,32,128]{2,1,0:T(8,128)(2,1)} custom-call(bf16[2,4,2,8,24,128]{5,4,3,2,1,0:T(8,128)(2,1)S(1)} %bitcast.15, bf16[8,512]{1,0:T(8,128)(2,1)S(1)} %get-tuple-element.15.bias_ref, bf16[16,32,128]{2,1,0:T(8,128)(2,1)S(1)} %copy-done, f32[1,128]{1,0:T(1,128)S(1)} %bitcast.26, bf16[4,128,128]{2,1,0:T(8,128)(2,1)S(1)} %bitcast.20, ...), custom_call_target="tpu_custom_call" | custom-call | flops 100000000 | bytes 4000000 | tf_op jit(solution)/shard_map/pallas_call | solution.py:310
  63.7 10.2 %all-to-all-done.2 = bf16[128,5,2,128]{3,2,1,0:T(2,128)(2,1)S(1)} async-done(((bf16[128,5,2,128]{3,2,1,0:T(2,128)(2,1)}), bf16[128,5,2,128]{3,2,1,0:T(2,128)(2,1)S(1)}, u32[]{:S(2)}, u32[]{:S(2)}) %all-to-all-start.2) | async-done | bytes 327712 | tf_op jit(solution)/shard_map/all_to_all | solution.py:371
  73.9 0.8 %shard_map.114 = (f32[128,512]{1,0:T(8,128)}, f32[4,128]{1,0:T(4,128)}, f32[128,128]{1,0:T(8,128)}, f32[1,128]{1,0:T(1,128)}) custom-call(bf16[1280,128]{1,0:T(8,128)(2,1)S(1)} %bitcast.18, bf16[128,512]{1,0:T(8,128)(2,1)S(1)} %copy-done.1, bf16[4,128]{1,0:T(4,128)(2,1)S(1)} %bitcast.24, f32[1,128]{1,0:T(1,128)S(1)} %bitcast.27), custom_call_target="tpu_custom_call" | custom-call | tf_op jit(solution)/shard_map/pallas_call | solution.py:310
  (5 shorter events, 0.0 us)
Async XLA Ops:
  3.8 27.7 %copy-start.1 = (bf16[128,512]{1,0:T(8,128)(2,1)S(1)}, bf16[128,512]{1,0:T(8,128)(2,1)}, u32[]{:S(2)}) copy-start(bf16[128,512]{1,0:T(8,128)(2,1)} %pw_ref.1) | copy-start | bytes 393220
  29.4 3.9 %collective-permute-start = (bf16[64,40,128]{2,1,0:T(8,128)(2,1)S(1)}, bf16[64,40,128]{2,1,0:T(8,128)(2,1)S(1)}, u32[]{:S(2)}, u32[]{:S(2)}) collective-permute-start(bf16[64,40,128]{2,1,0:T(8,128)(2,1)S(1)} %all_to_all.15), channel_id=1, source_target_pairs={{0,8},{8,0},{1,9},{9,1},{2,10},{10,2},{3,11},{11,3},{4,12},{12,4},... | collective-permute-start | bytes 1966088 | tf_op jit(solution)/shard_map/ppermute | solution.py:350
  31.7 0.7 copy-start.6
  32.4 1.0 %copy-start.3 = (bf16[128,128]{1,0:T(8,128)(2,1)S(1)}, bf16[128,128]{1,0:T(8,128)(2,1)}, u32[]{:S(2)}) copy-start(bf16[128,128]{1,0:T(8,128)(2,1)} %ow_ref.1) | copy-start | bytes 98308
  36.4 20.6 %copy-start.2 = (bf16[512,128]{1,0:T(8,128)(2,1)S(1)}, bf16[512,128]{1,0:T(8,128)(2,1)}, u32[]{:S(2)}) copy-start(bf16[512,128]{1,0:T(8,128)(2,1)} %get-tuple-element.14.normed_ref) | copy-start | bytes 393220
  57.9 3.9 %copy-start = (bf16[16,32,128]{2,1,0:T(8,128)(2,1)S(1)}, bf16[16,32,128]{2,1,0:T(8,128)(2,1)}, u32[]{:S(2)}) copy-start(bf16[16,32,128]{2,1,0:T(8,128)(2,1)} %pair_ref.1) | copy-start | bytes 393220
  57.9 16.0 %all-to-all-start.2 = ((bf16[128,5,2,128]{3,2,1,0:T(2,128)(2,1)}), bf16[128,5,2,128]{3,2,1,0:T(2,128)(2,1)S(1)}, u32[]{:S(2)}, u32[]{:S(2)}) async-start(bf16[128,5,2,128]{3,2,1,0:T(2,128)(2,1)} %bitcast.9), calls=%async_computation.2 | async-start | bytes 655360 | tf_op jit(solution)/shard_map/all_to_all | solution.py:371
  61.8 0.7 copy-start.4
  61.8 0.7 copy-start.5

commit v4 on v3

--- a/solution.py
+++ b/solution.py
@@ -24,8 +24,10 @@
 HEADS = 4
 DIM = 32
 IN_ROWS = 40
+PARTS = 4
 TOGETHER = 4
 MID_ROWS = 24
+SUM_ROWS = 32
 OUT_ROWS = 10
 
 NT = (((1,), (1,)), ((), ()))
@@ -48,12 +50,13 @@
 
 
 def pre_kernel(
-    pair_hbm, cot_hbm, gain_hbm, wbt_ref, send_ref, normed_ref, pair_v, cot_v, gain_v, xs, cs, sems
+    pair_hbm, cot_hbm, gain_hbm, wbt_hbm, send_hbm, normed_hbm,
+    pair_v, cot_v, gain_v, wbt_v, send_v, normed_v, xs, cs, sems, out_sems,
 ):
     copies = [
         pltpu.make_async_copy(src, dst, sems.at[i])
         for i, (src, dst) in enumerate(
-            ((pair_hbm, pair_v), (gain_hbm, gain_v), (cot_hbm, cot_v))
+            ((pair_hbm, pair_v), (gain_hbm, gain_v), (wbt_hbm, wbt_v), (cot_hbm, cot_v))
         )
     ]
     for copy in copies:
@@ -62,30 +65,44 @@
     hat, _ = normal(pair_v[...].astype(F32).reshape(TILE, CH))
     copies[1].wait()
     normed = (hat * gain_v[...]).astype(BF)
-    normed_ref[...] = normed
+    normed_v[...] = normed
+    outs = [pltpu.make_async_copy(normed_v, normed_hbm, out_sems.at[PARTS])]
+    outs[0].start()
     xs[...] = normed.astype(F32)
-    bias = mm(wbt_ref[...], normed, NT)
+    copies[2].wait()
+    bias = mm(wbt_v[...], normed, NT)
+    chunks = []
     for pair in range(2):
         rows = [
             bias[h : h + 1, b * CH : (b + 1) * CH]
             for h in (2 * pair, 2 * pair + 1)
             for b in range(4)
         ]
-        chunk = jnp.concatenate(rows, axis=0).astype(BF)
-        for col in range(COLS):
-            send_ref[pair * COLS + col, 32:40, :] = chunk
-    copies[2].wait()
+        chunks.append(jnp.concatenate(rows, axis=0).astype(BF))
+    copies[3].wait()
     cs[...] = cot_v[...].astype(F32).reshape(TILE, CH)
-    for col in range(COLS):
-        x = xs[pl.ds(col, ROWS, stride=COLS), :].astype(BF)
-        c = cs[pl.ds(col, ROWS, stride=COLS), :].astype(BF)
-        for pair in range(2):
-            send_ref[pair * COLS + col, 0:16, :] = x
-            send_ref[pair * COLS + col, 16:32, :] = c
+    for part in range(PARTS):
+        size = COLS // PARTS
+        for col in range(part * size, (part + 1) * size):
+            x = xs[pl.ds(col, ROWS, stride=COLS), :].astype(BF)
+            c = cs[pl.ds(col, ROWS, stride=COLS), :].astype(BF)
+            for pair in range(2):
+                send_v[pair, col, 0:16, :] = x
+                send_v[pair, col, 16:32, :] = c
+                send_v[pair, col, 32:40, :] = chunks[pair]
+        place = pl.ds(part * size, size)
+        copy = pltpu.make_async_copy(
+            send_v.at[:, place], send_hbm.at[:, place], out_sems.at[part]
+        )
+        copy.start()
+        outs.append(copy)
+    for copy in outs:
+        copy.wait()
 
 
 def attention_kernel(
-    own_ref, other_ref, wall_ref, ow_ref, mask_ref, send_ref, bias_s, sum_s, tail_s, grad_s, gout_s
+    own_ref, other_ref, wall_ref, ow_ref, mask_ref, keep_ref, give_ref,
+    bias_s, sum_s, tail_s, grad_s, gout_s,
 ):
     core = lax.axis_index("core")
     head = 2 * (lax.axis_index("chip") // 4) + core
@@ -98,6 +115,11 @@
         own, other = own_ref[:, n, start:stop, :], other_ref[:, n, start:stop, :]
         low, high = jnp.where(core == 0, own, other), jnp.where(core == 0, other, own)
         return jnp.stack([low, high], axis=1)
+
+    def put(value, n, start, stop):
+        even, odd = value[:, 0], value[:, 1]
+        keep_ref[:, n, start:stop, :] = jnp.where(core == 0, even, odd)
+        give_ref[:, n, start:stop, :] = jnp.where(core == 0, odd, even)
 
     group = lane_group((64, CH))
     for half in range(2):
@@ -181,8 +203,8 @@
         else:
             grad_s[...] += part
             gout_s[...] += out_part
-        turned = jnp.transpose(u.grads.astype(F32)).astype(BF)
-        send_ref[:, u.n, 0:16, :] = turned.reshape(N_WIDE, ROWS, CH)
+        d_normed = mm(u.grads, weight, TN).astype(BF)
+        put(d_normed.reshape(N_CHIP, 2, ROWS, CH), u.n, 0, 16)
 
     for first in range(0, N_NARROW, TOGETHER):
         units = [project(n) for n in range(first, first + TOGETHER)]
@@ -211,17 +233,26 @@
     out_part = gout_s[...]
     for r in range(4):
         tail_s[pl.ds(5 + 8 * r, DIM, stride=32), :] = out_part
-    tail = tail_s[...].astype(BF).reshape(N_WIDE, N_NARROW, 8, CH)
-    send_ref[:, :, 16:24, :] = tail
-
-
-def of_head(recv_ref, h, start, stop):
-    got = recv_ref[h // 2, :, h % 2, :, start:stop, :]
-    return got.reshape(COLS, stop - start, CH)
+    tail = tail_s[...].astype(BF).reshape(N_CHIP, 2, N_NARROW, 8, CH)
+    put(tail, slice(None), 16, 24)
+
+
+def join_kernel(keep_ref, got_ref, send_ref):
+    core = lax.axis_index("core")
+    total = keep_ref[:, 0:16, :].astype(F32) + got_ref[:, 0:16, :].astype(F32)
+    send_ref[:, 0:16, :] = total.astype(BF)
+    keep, got = keep_ref[:, 16:24, :], got_ref[:, 16:24, :]
+    send_ref[:, 16:24, :] = jnp.where(core == 0, keep, got)
+    send_ref[:, 24:32, :] = jnp.where(core == 0, got, keep)
 
 
 def reduce_kernel(recv_ref, normed_ref, send_ref, bias_ref):
-    sums = [jnp.sum(of_head(recv_ref, h, 16, 24).astype(F32), axis=0) for h in range(HEADS)]
+    sums = [
+        jnp.sum(
+            recv_ref[h // 2, :, 16 + 8 * (h % 2) : 24 + 8 * (h % 2), :].astype(F32), axis=0
+        )
+        for h in range(HEADS)
+    ]
     blocks = [
         jnp.concatenate([sums[h][b : b + 1] for h in range(HEADS)], axis=0) for b in range(4)
     ]
@@ -250,12 +281,9 @@
         send_ref[i * 80 : (i + 1) * 80, :] = block
 
 
-def pair_kernel(recv_ref, bias_ref, pair_ref, gain_ref, wall_ref, wbt_ref, out_ref, ds):
-    total = jnp.zeros((TILE, CH), F32)
-    for h in range(HEADS):
-        g = of_head(recv_ref, h, 0, 16).reshape(TILE, CH)
-        total = total + mm(g, wall_ref[h])
-    ds[...] = total
+def pair_kernel(recv_ref, bias_ref, pair_ref, gain_ref, wbt_ref, out_ref, ds):
+    total = recv_ref[0, :, 0:16, :].astype(F32) + recv_ref[1, :, 0:16, :].astype(F32)
+    ds[...] = total.reshape(TILE, CH)
     d_normed = jnp.concatenate([ds[pl.ds(r, COLS, stride=ROWS), :] for r in range(ROWS)], axis=0)
     wbt = wbt_ref[...].astype(F32)
     wbt = jnp.concatenate([wbt, jnp.zeros_like(wbt)], axis=0).astype(BF)
@@ -299,18 +327,15 @@
     gg_ref[...] = (dots_row + bias_row) / gain_ref[...]
 
 
-def call(kernel, out_shape, scratch=(), cost=None, outside=0, vmem=32):
+def call(kernel, out_shape, scratch=(), cost=None, hbm=False, vmem=32):
     many = isinstance(out_shape, (list, tuple))
-    spec = pl.BlockSpec(memory_space=pltpu.VMEM)
+    spec = pl.BlockSpec(memory_space=pltpu.HBM if hbm else pltpu.VMEM)
 
     def run(*args):
-        specs = [
-            pl.BlockSpec(memory_space=pltpu.HBM) if i < outside else spec for i in range(len(args))
-        ]
         return pl.pallas_call(
             kernel,
             out_shape=out_shape,
-            in_specs=specs,
+            in_specs=[spec] * len(args),
             out_specs=[spec] * len(out_shape) if many else spec,
             scratch_shapes=list(scratch),
             compiler_params=pltpu.CompilerParams(vmem_limit_bytes=vmem * 1024 * 1024),
@@ -322,6 +347,16 @@
 
 def shape(*dims, dtype=BF):
     return jax.ShapeDtypeStruct(dims, dtype)
+
+
+def exchange(x, axes, tile):
+    count, rows, lanes = x.shape
+    x = x.reshape(count, rows // tile, tile, lanes)
+    return lax.all_to_all(x, axes, 0, 0, tiled=True).reshape(count, rows, lanes)
+
+
+def swap(x):
+    return lax.ppermute(x, "core", [(0, 1), (1, 0)])
 
 
 def local(pair_rep, cotangent, norm_gain, proj_weight, bias_weight, out_weight, residue_mask):
@@ -331,26 +366,31 @@
     masking = (residue_mask.astype(F32) - 1.0) * MASK_FILL
     masking = jnp.broadcast_to(masking[:, None], (LENGTH, CH))
     tile_f32 = pltpu.VMEM((TILE, CH), F32)
+    half = DEVICES // 2
 
     send, normed = call(
         pre_kernel,
-        [shape(DEVICES // 2, IN_ROWS, CH), shape(TILE, CH)],
+        [shape(2, COLS, IN_ROWS, CH), shape(TILE, CH)],
         [
             pltpu.VMEM((ROWS, COLS, CH), BF),
             pltpu.VMEM((ROWS, COLS, CH), BF),
             pltpu.VMEM((1, CH), F32),
+            pltpu.VMEM((HEADS, CH), BF),
+            pltpu.VMEM((2, COLS, IN_ROWS, CH), BF),
+            pltpu.VMEM((TILE, CH), BF),
             tile_f32,
             tile_f32,
-            pltpu.SemaphoreType.DMA((3,)),
+            pltpu.SemaphoreType.DMA((4,)),
+            pltpu.SemaphoreType.DMA((PARTS + 1,)),
         ],
-        outside=3,
+        hbm=True,
         vmem=63,
     )(pair_rep, cotangent, gain, wbt)
-    own = lax.all_to_all(send, CHIPS, 0, 0, tiled=True)
-    other = lax.ppermute(own, "core", [(0, 1), (1, 0)])
-    mid = call(
+    own = exchange(send.reshape(half, IN_ROWS, CH), CHIPS, 4)
+    other = swap(own)
+    keep, give = call(
         attention_kernel,
-        shape(N_WIDE, N_NARROW, MID_ROWS, CH),
+        [shape(N_CHIP, N_NARROW, MID_ROWS, CH)] * 2,
         [
             pltpu.VMEM((2, LENGTH, CH), F32),
             pltpu.VMEM((2, LENGTH, CH), F32),
@@ -365,16 +405,19 @@
         out_weight,
         masking,
     )
-    mid = lax.all_to_all(mid.reshape(DEVICES, MID_ROWS, CH), BOTH, 0, 0, tiled=True)
-    mid = mid.reshape(2, N_CHIP // 2, 2, N_NARROW, MID_ROWS, CH)
+    got = swap(give)
+    mid = call(join_kernel, shape(half, SUM_ROWS, CH))(
+        keep.reshape(half, MID_ROWS, CH), got.reshape(half, MID_ROWS, CH)
+    )
+    mid = exchange(mid, CHIPS, 8).reshape(2, COLS, SUM_ROWS, CH)
     send, bias = call(reduce_kernel, [shape(DEVICES * OUT_ROWS, CH), shape(8, TILE)])(mid, normed)
-    last = lax.all_to_all(send.reshape(DEVICES, OUT_ROWS // 2, 2, CH), BOTH, 0, 0, tiled=True)
+    last = exchange(send.reshape(DEVICES, OUT_ROWS, CH), BOTH, 2)
     d_pair = call(
         pair_kernel,
         shape(ROWS, COLS, CH),
         [tile_f32],
         pl.CostEstimate(flops=100_000_000, bytes_accessed=4_000_000, transcendentals=512),
-    )(mid, bias, pair_rep, gain, wall, wbt)
+    )(mid, bias, pair_rep, gain, wbt)
     grad_proj, grad_bias, grad_out, grad_gain = call(
         final_kernel,
         [

time: 75.1 us -> 74.3 us (0.989)
  blocking collectives: 46.1 us -> 42.9 us
  starting transfers between devices: 6 us -> 7.87 us
  waiting for transfers between devices: 11.1 us -> 12.5 us
    all_to_all x2, blocking collectives: 46.1 us -> 42.9 us  [exchange(): return lax.all_to_all(x, axes, 0, 0, tiled=True).reshape(count, rows, lanes)]
    all_to_all x1, starting transfers between devices: 3.84 us -> 5.25 us  [exchange(): return lax.all_to_all(x, axes, 0, 0, tiled=True).reshape(count, rows, lanes)]
    ppermute x1 -> x2, waiting for transfers between devices: 0.91 us -> 2.26 us  [swap(): return lax.ppermute(x, 'core', [(0, 1), (1, 0)])]
    pallas_call x5 -> x6, Pallas kernels: 9.14 us -> 8.47 us  [run(): pl.pallas_call(kernel, out_shape=out_shape, in_specs=[spec] * len(args),...]
    ppermute x1 -> x2, starting transfers between devices: 2.16 us -> 2.63 us  [swap(): return lax.ppermute(x, 'core', [(0, 1), (1, 0)])]
  transfers between devices with their start and end apart: 2 -> 3, of which waited for: 2 -> 3; matrix products, arithmetic and copies ran while one was open for 0% -> 0% of each run, Pallas kernels for 2% -> 1%
where the time goes in v4:
time: 74.3 us; the launch traced here: 74 us
  blocking collectives  42.9 us (58%)
  waiting for transfers between devices  12.5 us (17%)
  Pallas kernels  8.47 us (11%)
  starting transfers between devices  7.87 us (11%)
  local copies, waits for them, and re-layouts  1.55 us (2%)
    all_to_all x2, blocking collectives, exchange(): return lax.all_to_all(x, axes, 0, 0, tiled=True).reshape(count, rows, lanes)  42.9 us
    all_to_all x1, waiting for transfers between devices, exchange(): return lax.all_to_all(x, axes, 0, 0, tiled=True).reshape(count, rows, lanes)  10.2 us
    pallas_call x6, Pallas kernels, run(): pl.pallas_call(kernel, out_shape=out_shape, in_specs=[spec] * len(args),...  8.47 us
    all_to_all x1, starting transfers between devices, exchange(): return lax.all_to_all(x, axes, 0, 0, tiled=True).reshape(count, rows, lanes)  5.25 us
    ppermute x2, starting transfers between devices, swap(): return lax.ppermute(x, 'core', [(0, 1), (1, 0)])  2.63 us
    ppermute x2, waiting for transfers between devices, swap(): return lax.ppermute(x, 'core', [(0, 1), (1, 0)])  2.26 us
  transfers between devices with their start and end apart: 3, of which 3 were waited for; matrix products, arithmetic and copies ran while one was open for 0% of the time, Pallas kernels for 1%

profile of v4, /device:TPU:1, one launch (start us, length us, event | category | flops | bytes accessed | tf_op | source)
XLA Modules:
  0.0 74.0 jit_solution(13550211790132674307)
XLA Ops:
  0.6 2.4 %shard_map.110 = (bf16[2,32,40,128]{3,2,1,0:T(8,128)(2,1)}, bf16[512,128]{1,0:T(8,128)(2,1)}) custom-call(bf16[16,32,128]{2,1,0:T(8,128)(2,1)} %pair_ref.1, bf16[16,32,128]{2,1,0:T(8,128)(2,1)} %cot_hbm.1, f32[1,128]{1,0:T(1,128)} %bitcast.31, bf16[4,128]{1,0:T(4,128)(2,1)} %bitcast.28), custom_call_target="tpu_custom_call" | custom-call | tf_op jit(solution)/shard_map/pallas_call | solution.py:335
  3.0 0.0 copy-start.1
  3.1 25.6 %all_to_all.15 = bf16[64,10,4,128]{3,2,1,0:T(4,128)(2,1)S(1)} all-to-all(bf16[64,10,4,128]{3,2,1,0:T(4,128)(2,1)} %bitcast.34), channel_id=1, replica_groups=mesh['chip'=8,'core'=2,'narrow'=8] {'chip','narrow'}, dimensions={0} | all-to-all | bytes 1310720 | tf_op jit(solution)/shard_map/all_to_all | solution.py:355
  28.6 2.2 %collective-permute-start = (bf16[64,40,128]{2,1,0:T(8,128)(2,1)S(1)}, bf16[64,40,128]{2,1,0:T(8,128)(2,1)S(1)}, u32[]{:S(2)}, u32[]{:S(2)}) collective-permute-start(bf16[64,40,128]{2,1,0:T(8,128)(2,1)S(1)} %bitcast.20), channel_id=1, source_target_pairs={{0,8},{8,0},{1,9},{9,1},{2,10},{10,2},{3,11},{11,3},{4,12},{12,4},... | collective-permute-start | bytes 1966088 | tf_op jit(solution)/shard_map/ppermute | solution.py:359
  30.8 0.1 copy.13
  30.9 0.0 copy-start.6
  30.9 0.7 copy-done.6
  31.6 0.9 %collective-permute-done = bf16[64,40,128]{2,1,0:T(8,128)(2,1)S(1)} collective-permute-done((bf16[64,40,128]{2,1,0:T(8,128)(2,1)S(1)}, bf16[64,40,128]{2,1,0:T(8,128)(2,1)S(1)}, u32[]{:S(2)}, u32[]{:S(2)}) %collective-permute-start) | collective-permute-done | bytes 655392 | tf_op jit(solution)/shard_map/ppermute | solution.py:359
  32.5 0.1 broadcast_in_dim.2.mask_ref
  32.6 3.1 %shard_map.111 = (bf16[8,8,24,128]{3,2,1,0:T(8,128)(2,1)S(1)}, bf16[8,8,24,128]{3,2,1,0:T(8,128)(2,1)S(1)}) custom-call(bf16[8,8,40,128]{3,2,1,0:T(8,128)(2,1)S(1)} %bitcast.21, bf16[8,8,40,128]{3,2,1,0:T(8,128)(2,1)S(1)} %bitcast.24, bf16[4,128,128]{2,1,0:T(8,128)(2,1)S(1)} %bitcast.25, bf16[128,128]{1,0:T(8,128)(2,1)S(1)} %copy-done.3, ...), custom_call_target="tpu_custom_call" | custom-call | tf_op jit(solution)/shard_map/pallas_call | solution.py:335
  35.7 0.5 collective-permute-start.1
  36.2 1.3 %collective-permute-done.1 = bf16[8,8,24,128]{3,2,1,0:T(8,128)(2,1)S(1)} collective-permute-done((bf16[8,8,24,128]{3,2,1,0:T(8,128)(2,1)S(1)}, bf16[8,8,24,128]{3,2,1,0:T(8,128)(2,1)S(1)}, u32[]{:S(2)}, u32[]{:S(2)}) %collective-permute-start.1) | collective-permute-done | bytes 393248 | tf_op jit(solution)/shard_map/ppermute | solution.py:359
  37.5 0.1 shard_map.112
  37.7 0.0 copy-start.2
  37.7 17.3 %all_to_all.16 = bf16[64,4,8,128]{3,2,1,0:T(8,128)(2,1)S(1)} all-to-all(bf16[64,4,8,128]{3,2,1,0:T(8,128)(2,1)S(1)} %bitcast.22), channel_id=1, replica_groups=mesh['chip'=8,'core'=2,'narrow'=8] {'chip','narrow'}, dimensions={0} | all-to-all | bytes 1048576 | tf_op jit(solution)/shard_map/all_to_all | solution.py:355
  55.0 0.0 copy-done.2
  55.0 0.9 %shard_map.113 = (bf16[1280,128]{1,0:T(8,128)(2,1)}, bf16[8,512]{1,0:T(8,128)(2,1)S(1)}) custom-call(bf16[2,32,32,128]{3,2,1,0:T(8,128)(2,1)S(1)} %bitcast.18, bf16[512,128]{1,0:T(8,128)(2,1)S(1)} %copy-done.2), custom_call_target="tpu_custom_call" | custom-call | tf_op jit(solution)/shard_map/pallas_call | solution.py:335
  55.9 5.2 %all-to-all-start.2 = ((bf16[128,5,2,128]{3,2,1,0:T(2,128)(2,1)}), bf16[128,5,2,128]{3,2,1,0:T(2,128)(2,1)S(1)}, u32[]{:S(2)}, u32[]{:S(2)}) async-start(bf16[128,5,2,128]{3,2,1,0:T(2,128)(2,1)} %bitcast.13), calls=%async_computation.2 | async-start | bytes 655360 | tf_op jit(solution)/shard_map/all_to_all | solution.py:355
  61.2 0.0 copy-start.4
  61.2 0.0 copy-start.5
  61.2 0.6 copy-done.4
  61.9 1.1 %shard_map.114 = bf16[16,32,128]{2,1,0:T(8,128)(2,1)} custom-call(bf16[2,32,32,128]{3,2,1,0:T(8,128)(2,1)S(1)} %bitcast.19, bf16[8,512]{1,0:T(8,128)(2,1)S(1)} %get-tuple-element.19.bias_ref, bf16[16,32,128]{2,1,0:T(8,128)(2,1)S(1)} %copy-done, f32[1,128]{1,0:T(1,128)S(1)} %bitcast.32, bf16[4,128]{1,0:T(4,128)(2,1)S(1)} %bitcast.29), custom_call_target="tpu_custom_call" | custom-call | flops 100000000 | bytes 4000000 | tf_op jit(solution)/shard_map/pallas_call | solution.py:335
  62.9 10.2 %all-to-all-done.2 = bf16[128,5,2,128]{3,2,1,0:T(2,128)(2,1)S(1)} async-done(((bf16[128,5,2,128]{3,2,1,0:T(2,128)(2,1)}), bf16[128,5,2,128]{3,2,1,0:T(2,128)(2,1)S(1)}, u32[]{:S(2)}, u32[]{:S(2)}) %all-to-all-start.2) | async-done | bytes 327712 | tf_op jit(solution)/shard_map/all_to_all | solution.py:355
  73.2 0.8 %shard_map.115 = (f32[128,512]{1,0:T(8,128)}, f32[4,128]{1,0:T(4,128)}, f32[128,128]{1,0:T(8,128)}, f32[1,128]{1,0:T(1,128)}) custom-call(bf16[1280,128]{1,0:T(8,128)(2,1)S(1)} %bitcast.23, bf16[128,512]{1,0:T(8,128)(2,1)S(1)} %copy-done.1, bf16[4,128]{1,0:T(4,128)(2,1)S(1)} %bitcast.30, f32[1,128]{1,0:T(1,128)S(1)} %bitcast.33), custom_call_target="tpu_custom_call" | custom-call | tf_op jit(solution)/shard_map/pallas_call | solution.py:335
  (8 shorter events, 0.0 us)
Async XLA Ops:
  3.0 27.7 %copy-start.1 = (bf16[128,512]{1,0:T(8,128)(2,1)S(1)}, bf16[128,512]{1,0:T(8,128)(2,1)}, u32[]{:S(2)}) copy-start(bf16[128,512]{1,0:T(8,128)(2,1)} %pw_ref.1) | copy-start | bytes 393220
  28.6 3.9 %collective-permute-start = (bf16[64,40,128]{2,1,0:T(8,128)(2,1)S(1)}, bf16[64,40,128]{2,1,0:T(8,128)(2,1)S(1)}, u32[]{:S(2)}, u32[]{:S(2)}) collective-permute-start(bf16[64,40,128]{2,1,0:T(8,128)(2,1)S(1)} %bitcast.20), channel_id=1, source_target_pairs={{0,8},{8,0},{1,9},{9,1},{2,10},{10,2},{3,11},{11,3},{4,12},{12,4},... | collective-permute-start | bytes 1966088 | tf_op jit(solution)/shard_map/ppermute | solution.py:359
  30.9 0.7 copy-start.6
  31.6 1.0 %copy-start.3 = (bf16[128,128]{1,0:T(8,128)(2,1)S(1)}, bf16[128,128]{1,0:T(8,128)(2,1)}, u32[]{:S(2)}) copy-start(bf16[128,128]{1,0:T(8,128)(2,1)} %ow_ref.1) | copy-start | bytes 98308
  35.7 1.8 %collective-permute-start.1 = (bf16[8,8,24,128]{3,2,1,0:T(8,128)(2,1)S(1)}, bf16[8,8,24,128]{3,2,1,0:T(8,128)(2,1)S(1)}, u32[]{:S(2)}, u32[]{:S(2)}) collective-permute-start(bf16[8,8,24,128]{3,2,1,0:T(8,128)(2,1)S(1)} %get-tuple-element.17), channel_id=1, source_target_pairs={{0,8},{8,0},{1,9},{9,1},{2,10},{10,2},{3,11},{11,3},{4,12},{12,4},... | collective-permute-start | bytes 1179656 | tf_op jit(solution)/shard_map/ppermute | solution.py:359
  37.7 17.3 %copy-start.2 = (bf16[512,128]{1,0:T(8,128)(2,1)S(1)}, bf16[512,128]{1,0:T(8,128)(2,1)}, u32[]{:S(2)}) copy-start(bf16[512,128]{1,0:T(8,128)(2,1)} %get-tuple-element.18.normed_ref) | copy-start | bytes 393220
  55.9 5.3 %copy-start = (bf16[16,32,128]{2,1,0:T(8,128)(2,1)S(1)}, bf16[16,32,128]{2,1,0:T(8,128)(2,1)}, u32[]{:S(2)}) copy-start(bf16[16,32,128]{2,1,0:T(8,128)(2,1)} %pair_ref.1) | copy-start | bytes 393220
  55.9 17.3 %all-to-all-start.2 = ((bf16[128,5,2,128]{3,2,1,0:T(2,128)(2,1)}), bf16[128,5,2,128]{3,2,1,0:T(2,128)(2,1)S(1)}, u32[]{:S(2)}, u32[]{:S(2)}) async-start(bf16[128,5,2,128]{3,2,1,0:T(2,128)(2,1)} %bitcast.13), calls=%async_computation.2 | async-start | bytes 655360 | tf_op jit(solution)/shard_map/all_to_all | solution.py:355
  61.2 0.7 copy-start.4
  61.2 0.7 copy-start.5

commit v5 on v4

--- a/solution.py
+++ b/solution.py
@@ -23,9 +23,10 @@
 CH = 128
 HEADS = 4
 DIM = 32
-IN_ROWS = 40
+HALF = 8
+IN_ROWS = 32
 PARTS = 4
-TOGETHER = 4
+TOGETHER = 8
 MID_ROWS = 24
 SUM_ROWS = 32
 OUT_ROWS = 10
@@ -45,8 +46,13 @@
     return centered * inverse, inverse
 
 
-def lane_group(shape):
-    return lax.broadcasted_iota(jnp.int32, shape, 1) // COLS
+def lane_group(shape, size=DIM):
+    return lax.broadcasted_iota(jnp.int32, shape, 1) // size
+
+
+def turn(x, lanes):
+    lanes %= CH
+    return pltpu.roll(x, lanes, 1) if lanes else x
 
 
 def pre_kernel(
@@ -64,32 +70,38 @@
     copies[0].wait()
     hat, _ = normal(pair_v[...].astype(F32).reshape(TILE, CH))
     copies[1].wait()
-    normed = (hat * gain_v[...]).astype(BF)
-    normed_v[...] = normed
+    normed = (hat * gain_v[...]).astype(BF).astype(F32)
+    xs[...] = normed
+    groups = normed.reshape(TILE // (2 * HALF), 2, HALF, CH)
+    halves = [groups[:, s].reshape(TILE // 2, CH) for s in range(2)]
+    split = jnp.concatenate(halves, axis=0).astype(BF)
+    normed_v[...] = split
     outs = [pltpu.make_async_copy(normed_v, normed_hbm, out_sems.at[PARTS])]
     outs[0].start()
-    xs[...] = normed.astype(F32)
     copies[2].wait()
-    bias = mm(wbt_v[...], normed, NT)
-    chunks = []
-    for pair in range(2):
-        rows = [
-            bias[h : h + 1, b * CH : (b + 1) * CH]
-            for h in (2 * pair, 2 * pair + 1)
-            for b in range(4)
-        ]
-        chunks.append(jnp.concatenate(rows, axis=0).astype(BF))
+    bias = mm(wbt_v[...], split, NT)
+    chunks = [
+        jnp.concatenate(
+            [
+                bias[h : h + 1, (2 * s + kb) * CH : (2 * s + kb + 1) * CH]
+                for h in range(HEADS)
+                for kb in range(2)
+            ],
+            axis=0,
+        )
+        for s in range(2)
+    ]
     copies[3].wait()
     cs[...] = cot_v[...].astype(F32).reshape(TILE, CH)
     for part in range(PARTS):
         size = COLS // PARTS
         for col in range(part * size, (part + 1) * size):
             x = xs[pl.ds(col, ROWS, stride=COLS), :].astype(BF)
-            c = cs[pl.ds(col, ROWS, stride=COLS), :].astype(BF)
-            for pair in range(2):
-                send_v[pair, col, 0:16, :] = x
-                send_v[pair, col, 16:32, :] = c
-                send_v[pair, col, 32:40, :] = chunks[pair]
+            c = cs[pl.ds(col, ROWS, stride=COLS), :]
+            for s in range(2):
+                send_v[s, col, 0:16, :] = x
+                rest = jnp.concatenate([c[s * HALF : (s + 1) * HALF], chunks[s]], axis=0)
+                send_v[s, col, 16:32, :] = rest.astype(BF)
         place = pl.ds(part * size, size)
         copy = pltpu.make_async_copy(
             send_v.at[:, place], send_hbm.at[:, place], out_sems.at[part]
@@ -102,137 +114,149 @@
 
 def attention_kernel(
     own_ref, other_ref, wall_ref, ow_ref, mask_ref, keep_ref, give_ref,
-    bias_s, sum_s, tail_s, grad_s, gout_s,
+    bias_s, sum_s, tail_s, kv_s, qg_s, gout_s,
 ):
     core = lax.axis_index("core")
-    head = 2 * (lax.axis_index("chip") // 4) + core
+    side = lax.axis_index("chip") // 4
     scale = DIM**-0.5
-    weight = wall_ref[head]
-    out_w = ow_ref[pl.ds(pl.multiple_of(head * DIM, DIM), DIM), :]
+    two = [wall_ref[2 * core + hh] for hh in range(2)]
+    w_kv = jnp.concatenate([w[DIM : 3 * DIM] for w in two], axis=0)
+    w_qg = jnp.concatenate([w[:DIM] for w in two] + [w[3 * DIM :] for w in two], axis=0)
+    out_w = ow_ref[pl.ds(pl.multiple_of(core * 2 * DIM, 2 * DIM), 2 * DIM), :]
     zero = jnp.zeros((DIM, CH), BF)
 
-    def rows(n, start, stop):
-        own, other = own_ref[:, n, start:stop, :], other_ref[:, n, start:stop, :]
+    def rows(n, start):
+        own, other = [ref[:, n, start : start + HALF, :] for ref in (own_ref, other_ref)]
         low, high = jnp.where(core == 0, own, other), jnp.where(core == 0, other, own)
-        return jnp.stack([low, high], axis=1)
+        return jnp.stack([low, high], axis=1).astype(F32).reshape(N_WIDE * HALF, CH)
+
+    group = lane_group((N_WIDE, CH), 16)
+    for n in range(N_NARROW):
+        tail_s[n * CH : (n + 1) * CH, :] = rows(n, 24)
+    for hh in range(2):
+        for kb in range(2):
+            got = []
+            for n in range(N_NARROW):
+                at = n * CH + 2 * hh + kb
+                first = tail_s[pl.ds(at, N_WIDE, stride=8), :]
+                second = tail_s[pl.ds(at + 4, N_WIDE, stride=8), :]
+                got.append(jnp.where(core == 0, first, second))
+            for kq in range(HALF):
+                acc = got[0]
+                acc = turn(acc, -kq * 16)
+                for n in range(1, N_NARROW):
+                    acc = jnp.where(group == n, turn(got[n], (n - kq) * 16), acc)
+                bias_s.at[hh][pl.ds(kb * CH + kq, N_WIDE, stride=HALF), :] = acc
+
+    class Unit:
+        pass
+
+    def project(n):
+        u = Unit()
+        u.n = n
+        parts = [rows(n, 0).astype(BF), rows(n, HALF).astype(BF)]
+        u.x = jnp.concatenate(parts, axis=0)
+        u.x_own = jnp.where(side == 0, parts[0], parts[1])
+        u.cot = rows(n, 16).astype(BF)
+        u.kv = mm(u.x, w_kv, NT).astype(BF)
+        kv_t = mm(w_kv, u.x, NT).astype(BF)
+        qg = mm(w_qg, u.x_own, NT)
+        og = mm(out_w, u.cot, NT)
+        u.pieces = []
+        for hh in range(2):
+            h = Unit()
+            h.n, h.hh, h.kv = n, hh, u.kv
+            h.q = qg[hh * DIM : (hh + 1) * DIM].astype(BF)
+            h.gate = jax.nn.sigmoid(qg[(2 + hh) * DIM : (3 + hh) * DIM])
+            h.og = og[hh * DIM : (hh + 1) * DIM]
+            h.da = (h.og * h.gate).astype(BF)
+            h.k, h.v = [kv_t[(2 * hh + t) * DIM : (2 * hh + t + 1) * DIM] for t in range(2)]
+            u.pieces.append(h)
+        return u
+
+    def score(h):
+        top = [jnp.concatenate(pair, axis=1) for pair in ((h.q, zero), (zero, h.da))]
+        rest = [jnp.concatenate([zero, zero], axis=1)] * 2
+        right = jnp.concatenate(top + rest if h.hh == 0 else rest + top, axis=0)
+        both = mm(h.kv, right)
+        h.logits, h.d_soft = both[:, :CH], both[:, CH:]
+
+    def softmax(h):
+        logits = h.logits * scale + bias_s[h.hh] + mask_ref[...]
+        top = jnp.max(logits, axis=0, keepdims=True)
+        e = jnp.exp(logits - top)
+        h.soft = e * (1.0 / jnp.sum(e, axis=0, keepdims=True))
+        h.soft_bf = h.soft.astype(BF)
+
+    def attend(h):
+        h.att = mm(h.v, h.soft_bf)
+        h.delta = jnp.sum(h.da.astype(F32) * h.att, axis=0, keepdims=True)
+
+    def logit_grads(h):
+        h.d_log = (h.soft * (h.d_soft - h.delta)).astype(BF)
+        if h.n == 0:
+            sum_s[h.hh] = h.d_log.astype(F32)
+        else:
+            sum_s[h.hh] += h.d_log.astype(F32)
+
+    def gradients(h):
+        h.dq = mm(h.k, h.d_log) * scale
+        h.dk = mm(h.q, h.d_log, NT) * scale
+        h.dv = mm(h.da, h.soft_bf, NT)
+        h.dg = h.og * h.att * h.gate * (1.0 - h.gate)
+        h.gated = (h.gate * h.att).astype(BF)
+
+    def emit(u):
+        one, other = u.pieces
+        kv_grads = jnp.concatenate([one.dk, one.dv, other.dk, other.dv], axis=0).astype(BF)
+        qg_grads = jnp.concatenate([one.dq, other.dq, one.dg, other.dg], axis=0).astype(BF)
+        gated = jnp.concatenate([one.gated, other.gated], axis=0)
+        sums = (mm(kv_grads, u.x), mm(qg_grads, u.x_own), mm(gated, u.cot))
+        for ref, part in zip((kv_s, qg_s, gout_s), sums):
+            if u.n == 0:
+                ref[...] = part
+            else:
+                ref[...] += part
+        d_normed = mm(kv_grads, w_kv, TN)
+        d_own = mm(qg_grads, w_qg, TN)
+        both = [
+            (d_normed[i * CH : (i + 1) * CH] + jnp.where(side == i, d_own, 0.0)).reshape(
+                N_CHIP, 2, HALF, CH
+            )
+            for i in range(2)
+        ]
+        put(jnp.concatenate(both, axis=2).astype(BF), u.n, 0, 16)
 
     def put(value, n, start, stop):
         even, odd = value[:, 0], value[:, 1]
         keep_ref[:, n, start:stop, :] = jnp.where(core == 0, even, odd)
         give_ref[:, n, start:stop, :] = jnp.where(core == 0, odd, even)
 
-    group = lane_group((64, CH))
-    for half in range(2):
-        got = []
-        for q in range(4):
-            both = rows(half * 4 + q, 32, 40).astype(F32).reshape(N_WIDE, 8, CH)
-            got.append(jnp.where(core == 0, both[:, 0:4], both[:, 4:8]).reshape(64, CH))
-        for kq in range(4):
-            acc = jnp.zeros((64, CH), F32)
-            for q in range(4):
-                shift = (q - kq) * COLS % CH
-                acc = jnp.where(group == q, pltpu.roll(got[q], shift, 1) if shift else got[q], acc)
-            bias_s.at[half][pl.ds(kq, 64, stride=4), :] = acc
-
-    class Unit:
-        pass
-
-    def project(n):
-        u = Unit()
-        u.n = n
-        u.x = rows(n, 0, 16).reshape(LENGTH, CH)
-        u.cot = rows(n, 16, 32).reshape(LENGTH, CH)
-        projected = mm(weight, u.x, NT)
-        u.kv = mm(u.x, weight[DIM : 3 * DIM], NT).astype(BF)
-        u.q, u.k, u.v = [projected[DIM * t : DIM * (t + 1)].astype(BF) for t in range(3)]
-        u.gate = jax.nn.sigmoid(projected[3 * DIM :])
-        u.og = mm(out_w, u.cot, NT)
-        u.da = (u.og * u.gate).astype(BF)
-        return u
-
-    def score(u, half):
-        part = slice(half * CH, (half + 1) * CH)
-        h = Unit()
-        h.half, h.q, h.da, h.v, h.n = half, u.q[:, part], u.da[:, part], u.v, u.n
-        right = jnp.concatenate(
-            [
-                jnp.concatenate([h.q, zero], axis=1),
-                jnp.concatenate([zero, h.da], axis=1),
-            ],
-            axis=0,
-        )
-        both = mm(u.kv, right)
-        h.logits, h.d_soft = both[:, :CH], both[:, CH:]
-        return h
-
-    def softmax(h):
-        logits = h.logits * scale + bias_s[h.half] + mask_ref[...]
-        top = jnp.max(logits, axis=0, keepdims=True)
-        e = jnp.exp(logits - top)
-        h.soft = e * (1.0 / jnp.sum(e, axis=0, keepdims=True))
-        h.soft_bf = h.soft.astype(BF)
-
-    def attend(h):
-        h.att = mm(h.v, h.soft_bf)
-        h.delta = jnp.sum(h.da.astype(F32) * h.att, axis=0, keepdims=True)
-
-    def logit_grads(h):
-        h.d_log = (h.soft * (h.d_soft - h.delta)).astype(BF)
-        if h.n == 0:
-            sum_s[h.half] = h.d_log.astype(F32)
-        else:
-            sum_s[h.half] += h.d_log.astype(F32)
-
-    def gradients(u, halves):
-        d_log = jnp.concatenate([h.d_log for h in halves], axis=1)
-        soft_bf = jnp.concatenate([h.soft_bf for h in halves], axis=1)
-        att = jnp.concatenate([h.att for h in halves], axis=1)
-        dq = mm(u.k, d_log) * scale
-        dk = mm(u.q, d_log, NT) * scale
-        dv = mm(u.da, soft_bf, NT)
-        dg = u.og * att * u.gate * (1.0 - u.gate)
-        u.grads = jnp.concatenate([dq, dk, dv, dg], axis=0).astype(BF)
-        u.gated = (u.gate * att).astype(BF)
-
-    def emit(u):
-        part = mm(u.grads, u.x)
-        out_part = mm(u.gated, u.cot)
-        if u.n == 0:
-            grad_s[...] = part
-            gout_s[...] = out_part
-        else:
-            grad_s[...] += part
-            gout_s[...] += out_part
-        d_normed = mm(u.grads, weight, TN).astype(BF)
-        put(d_normed.reshape(N_CHIP, 2, ROWS, CH), u.n, 0, 16)
-
     for first in range(0, N_NARROW, TOGETHER):
         units = [project(n) for n in range(first, first + TOGETHER)]
-        pieces = [[score(u, half) for half in range(2)] for u in units]
-        flat = [h for halves in pieces for h in halves]
-        for step in (softmax, attend, logit_grads):
+        flat = [h for u in units for h in u.pieces]
+        for step in (score, softmax, attend, logit_grads, gradients):
             for h in flat:
                 step(h)
-        for u, halves in zip(units, pieces):
-            gradients(u, halves)
         for u in units:
             emit(u)
 
-    tail_s[...] = jnp.zeros_like(tail_s)
-    for n in range(N_NARROW):
-        half, q = n // 4, n % 4
-        acc = jnp.zeros((64, CH), F32)
-        for kq in range(4):
-            got = sum_s.at[half][pl.ds(kq, 64, stride=4), :]
-            shift = (kq - q) * COLS % CH
-            acc = jnp.where(group == kq, pltpu.roll(got, shift, 1) if shift else got, acc)
-        for w in range(N_WIDE):
-            at = (w * N_NARROW + n) * 8
-            tail_s[at : at + 4, :] = acc[w * 4 : (w + 1) * 4, :]
-    tail_s[pl.ds(4, DEVICES, stride=8), :] = jnp.transpose(grad_s[...])
-    out_part = gout_s[...]
-    for r in range(4):
-        tail_s[pl.ds(5 + 8 * r, DIM, stride=32), :] = out_part
+    for hh in range(2):
+        for kb in range(2):
+            got = [
+                sum_s.at[hh][pl.ds(kb * CH + kq, N_WIDE, stride=HALF), :] for kq in range(HALF)
+            ]
+            for n in range(N_NARROW):
+                acc = turn(got[0], -n * 16)
+                for kq in range(1, HALF):
+                    acc = jnp.where(group == kq, turn(got[kq], (kq - n) * 16), acc)
+                tail_s[pl.ds(n * 8 + 2 * hh + kb, N_WIDE, stride=64), :] = acc
+    tail_s[pl.ds(4, DEVICES, stride=8), :] = jnp.transpose(kv_s[...])
+    tail_s[pl.ds(5, DEVICES, stride=8), :] = jnp.transpose(qg_s[...])
+    for hh in range(2):
+        out_part = gout_s[hh * DIM : (hh + 1) * DIM, :]
+        for r in range(4):
+            tail_s[pl.ds(6 + hh + 8 * r, DIM, stride=32), :] = out_part
     tail = tail_s[...].astype(BF).reshape(N_CHIP, 2, N_NARROW, 8, CH)
     put(tail, slice(None), 16, 24)
 
@@ -248,32 +272,42 @@
 
 def reduce_kernel(recv_ref, normed_ref, send_ref, bias_ref):
     sums = [
-        jnp.sum(
-            recv_ref[h // 2, :, 16 + 8 * (h % 2) : 24 + 8 * (h % 2), :].astype(F32), axis=0
-        )
-        for h in range(HEADS)
+        [
+            jnp.sum(recv_ref[s, :, 16 + 8 * c : 24 + 8 * c, :].astype(F32), axis=0)
+            for c in range(2)
+        ]
+        for s in range(2)
     ]
-    blocks = [
-        jnp.concatenate([sums[h][b : b + 1] for h in range(HEADS)], axis=0) for b in range(4)
-    ]
+    blocks = []
+    for s in range(2):
+        for kb in range(2):
+            parts = [sums[s][h // 2][h % 2 * 2 + kb :][:1] for h in range(HEADS)]
+            blocks.append(jnp.concatenate(parts, axis=0))
     bias = jnp.concatenate(blocks, axis=1)
     bias = jnp.concatenate([bias, jnp.zeros_like(bias)], axis=0).astype(BF)
     bias_ref[...] = bias
     grad_bias = mm(bias, normed_ref[...])[:HEADS]
+    total = [sums[0][c] + sums[1][c] for c in range(2)]
     group = lane_group((1, CH))
     rows = []
     for t in range(4):
         row = jnp.zeros((1, CH), F32)
         for h in range(HEADS):
-            shift = (h - t) * COLS % CH
-            got = sums[h][4:5]
-            row = jnp.where(group == h, pltpu.roll(got, shift, 1) if shift else got, row)
+            own = total[h // 2]
+            got, place = {
+                0: (own[5:6], h % 2),
+                1: (own[4:5], h % 2 * 2),
+                2: (own[4:5], h % 2 * 2 + 1),
+                3: (own[5:6], 2 + h % 2),
+            }[t]
+            row = jnp.where(group == h, turn(got, (h - place) * DIM), row)
         rows.append(row)
     place = lax.rem(lax.axis_index("narrow"), 4)
     row = jnp.zeros((1, CH), F32)
     for h in range(HEADS):
-        shift = lax.rem(h * COLS + CH - place * COLS, CH)
-        row = jnp.where(group == h, pltpu.roll(sums[h][5:6], shift, 1), row)
+        shift = lax.rem(h * DIM + CH - place * DIM, CH)
+        got = total[h // 2][6 + h % 2 :][:1]
+        row = jnp.where(group == h, pltpu.roll(got, shift, 1), row)
     rows += [row, jnp.zeros((1, CH), F32), grad_bias]
     chunk = jnp.concatenate(rows, axis=0)
     block = jnp.concatenate([chunk] * 8, axis=0).astype(BF)
@@ -287,7 +321,8 @@
     d_normed = jnp.concatenate([ds[pl.ds(r, COLS, stride=ROWS), :] for r in range(ROWS)], axis=0)
     wbt = wbt_ref[...].astype(F32)
     wbt = jnp.concatenate([wbt, jnp.zeros_like(wbt)], axis=0).astype(BF)
-    d_normed = d_normed + mm(bias_ref[...], wbt, TN)
+    split = mm(bias_ref[...], wbt, TN).reshape(2, TILE // (2 * HALF), HALF, CH)
+    d_normed = d_normed + jnp.stack([split[0], split[1]], axis=1).reshape(TILE, CH)
     hat, inverse = normal(pair_ref[...].astype(F32).reshape(TILE, CH))
     d_hat = d_normed * gain_ref[...]
     d_pair = inverse * (
@@ -364,6 +399,7 @@
     wbt = bias_weight.T
     wall = proj_weight.reshape(CH, 4, HEADS, DIM).transpose(2, 1, 3, 0).reshape(HEADS, CH, CH)
     masking = (residue_mask.astype(F32) - 1.0) * MASK_FILL
+    masking = masking.reshape(N_WIDE, 2, HALF).transpose(1, 0, 2).reshape(LENGTH)
     masking = jnp.broadcast_to(masking[:, None], (LENGTH, CH))
     tile_f32 = pltpu.VMEM((TILE, CH), F32)
     half = DEVICES // 2
@@ -396,7 +432,8 @@
             pltpu.VMEM((2, LENGTH, CH), F32),
             pltpu.VMEM((DEVICES * 8, CH), F32),
             pltpu.VMEM((CH, CH), F32),
-            pltpu.VMEM((DIM, CH), F32),
+            pltpu.VMEM((CH, CH), F32),
+            pltpu.VMEM((2 * DIM, CH), F32),
         ],
     )(
         own.reshape(N_CHIP, N_NARROW, IN_ROWS, CH),

time: 74.3 us -> 73.2 us (0.985)
  blocking collectives: 42.9 us -> 41.7 us
    all_to_all x2, blocking collectives: 42.9 us -> 41.7 us  [exchange(): return lax.all_to_all(x, axes, 0, 0, tiled=True).reshape(count, rows, lanes)]
where the time goes in v5:
time: 73.2 us; the launch traced here: 72.8 us
  blocking collectives  41.7 us (57%)
  waiting for transfers between devices  12.7 us (17%)
  Pallas kernels  8.89 us (12%)
  starting transfers between devices  7.64 us (10%)
  local copies, waits for them, and re-layouts  1.09 us (1%)
  between operations  0.77 us (1%)
    all_to_all x2, blocking collectives, exchange(): return lax.all_to_all(x, axes, 0, 0, tiled=True).reshape(count, rows, lanes)  41.7 us
    all_to_all x1, waiting for transfers between devices, exchange(): return lax.all_to_all(x, axes, 0, 0, tiled=True).reshape(count, rows, lanes)  10.2 us
    pallas_call x6, Pallas kernels, run(): pl.pallas_call(kernel, out_shape=out_shape, in_specs=[spec] * len(args),...  8.89 us
    all_to_all x1, starting transfers between devices, exchange(): return lax.all_to_all(x, axes, 0, 0, tiled=True).reshape(count, rows, lanes)  5.24 us
    ppermute x2, waiting for transfers between devices, swap(): return lax.ppermute(x, 'core', [(0, 1), (1, 0)])  2.51 us
    ppermute x2, starting transfers between devices, swap(): return lax.ppermute(x, 'core', [(0, 1), (1, 0)])  2.4 us
  transfers between devices with their start and end apart: 3, of which 3 were waited for; matrix products, arithmetic and copies ran while one was open for 0% of the time, Pallas kernels for 1%

profile of v5, /device:TPU:1, one launch (start us, length us, event | category | flops | bytes accessed | tf_op | source)
XLA Modules:
  0.0 72.8 jit_solution(6285445040219979891)
XLA Ops:
  0.6 2.4 %shard_map.110 = (bf16[2,32,32,128]{3,2,1,0:T(8,128)(2,1)}, bf16[512,128]{1,0:T(8,128)(2,1)}) custom-call(bf16[16,32,128]{2,1,0:T(8,128)(2,1)} %pair_ref.1, bf16[16,32,128]{2,1,0:T(8,128)(2,1)} %cot_hbm.1, f32[1,128]{1,0:T(1,128)} %bitcast.32, bf16[4,128]{1,0:T(4,128)(2,1)} %bitcast.29), custom_call_target="tpu_custom_call" | custom-call | tf_op jit(solution)/shard_map/pallas_call | solution.py:370
  3.0 0.0 copy-start.1
  3.0 24.4 %all_to_all.15 = bf16[64,8,4,128]{3,2,1,0:T(4,128)(2,1)S(1)} all-to-all(bf16[64,8,4,128]{3,2,1,0:T(4,128)(2,1)} %bitcast.35), channel_id=1, replica_groups=mesh['chip'=8,'core'=2,'narrow'=8] {'chip','narrow'}, dimensions={0} | all-to-all | bytes 1048576 | tf_op jit(solution)/shard_map/all_to_all | solution.py:390
  27.4 2.0 %collective-permute-start = (bf16[64,32,128]{2,1,0:T(8,128)(2,1)S(1)}, bf16[64,32,128]{2,1,0:T(8,128)(2,1)S(1)}, u32[]{:S(2)}, u32[]{:S(2)}) collective-permute-start(bf16[64,32,128]{2,1,0:T(8,128)(2,1)S(1)} %bitcast.22), channel_id=1, source_target_pairs={{0,8},{8,0},{1,9},{9,1},{2,10},{10,2},{3,11},{11,3},{4,12},{12,4},... | collective-permute-start | bytes 1572872 | tf_op jit(solution)/shard_map/ppermute | solution.py:394
  29.4 0.1 reshape.46
  29.5 0.1 broadcast_in_dim.7
  29.6 0.1 copy.13
  29.7 0.0 copy-start.3
  29.7 1.2 %collective-permute-done = bf16[64,32,128]{2,1,0:T(8,128)(2,1)S(1)} collective-permute-done((bf16[64,32,128]{2,1,0:T(8,128)(2,1)S(1)}, bf16[64,32,128]{2,1,0:T(8,128)(2,1)S(1)}, u32[]{:S(2)}, u32[]{:S(2)}) %collective-permute-start) | collective-permute-done | bytes 524320 | tf_op jit(solution)/shard_map/ppermute | solution.py:394
  30.9 0.1 broadcast_in_dim.8.mask_ref
  31.0 3.6 %shard_map.111 = (bf16[8,8,24,128]{3,2,1,0:T(8,128)(2,1)S(1)}, bf16[8,8,24,128]{3,2,1,0:T(8,128)(2,1)S(1)}) custom-call(bf16[8,8,32,128]{3,2,1,0:T(8,128)(2,1)S(1)} %bitcast.23, bf16[8,8,32,128]{3,2,1,0:T(8,128)(2,1)S(1)} %bitcast.25, bf16[4,128,128]{2,1,0:T(8,128)(2,1)S(1)} %bitcast.26, bf16[128,128]{1,0:T(8,128)(2,1)S(1)} %copy-done.3, ...), custom_call_target="tpu_custom_call" | custom-call | tf_op jit(solution)/shard_map/pallas_call | solution.py:370
  34.6 0.5 collective-permute-start.1
  35.0 1.4 %collective-permute-done.1 = bf16[8,8,24,128]{3,2,1,0:T(8,128)(2,1)S(1)} collective-permute-done((bf16[8,8,24,128]{3,2,1,0:T(8,128)(2,1)S(1)}, bf16[8,8,24,128]{3,2,1,0:T(8,128)(2,1)S(1)}, u32[]{:S(2)}, u32[]{:S(2)}) %collective-permute-start.1) | collective-permute-done | bytes 393248 | tf_op jit(solution)/shard_map/ppermute | solution.py:394
  36.4 0.1 shard_map.112
  36.5 0.0 copy-start.2
  36.5 17.3 %all_to_all.16 = bf16[64,4,8,128]{3,2,1,0:T(8,128)(2,1)S(1)} all-to-all(bf16[64,4,8,128]{3,2,1,0:T(8,128)(2,1)S(1)} %bitcast.21), channel_id=1, replica_groups=mesh['chip'=8,'core'=2,'narrow'=8] {'chip','narrow'}, dimensions={0} | all-to-all | bytes 1048576 | tf_op jit(solution)/shard_map/all_to_all | solution.py:390
  53.8 0.9 %shard_map.113 = (bf16[1280,128]{1,0:T(8,128)(2,1)}, bf16[8,512]{1,0:T(8,128)(2,1)S(1)}) custom-call(bf16[2,32,32,128]{3,2,1,0:T(8,128)(2,1)S(1)} %bitcast.19, bf16[512,128]{1,0:T(8,128)(2,1)S(1)} %copy-done.2), custom_call_target="tpu_custom_call" | custom-call | tf_op jit(solution)/shard_map/pallas_call | solution.py:370
  54.8 5.2 %all-to-all-start.2 = ((bf16[128,5,2,128]{3,2,1,0:T(2,128)(2,1)}), bf16[128,5,2,128]{3,2,1,0:T(2,128)(2,1)S(1)}, u32[]{:S(2)}, u32[]{:S(2)}) async-start(bf16[128,5,2,128]{3,2,1,0:T(2,128)(2,1)} %bitcast.14), calls=%async_computation.2 | async-start | bytes 655360 | tf_op jit(solution)/shard_map/all_to_all | solution.py:390
  60.0 0.0 copy-start.4
  60.0 0.0 copy-start.5
  60.1 0.6 copy-done.4
  60.7 1.1 %shard_map.114 = bf16[16,32,128]{2,1,0:T(8,128)(2,1)} custom-call(bf16[2,32,32,128]{3,2,1,0:T(8,128)(2,1)S(1)} %bitcast.20, bf16[8,512]{1,0:T(8,128)(2,1)S(1)} %get-tuple-element.19.bias_ref, bf16[16,32,128]{2,1,0:T(8,128)(2,1)S(1)} %copy-done, f32[1,128]{1,0:T(1,128)S(1)} %bitcast.33, bf16[4,128]{1,0:T(4,128)(2,1)S(1)} %bitcast.30), custom_call_target="tpu_custom_call" | custom-call | flops 100000000 | bytes 4000000 | tf_op jit(solution)/shard_map/pallas_call | solution.py:370
  61.8 10.2 %all-to-all-done.2 = bf16[128,5,2,128]{3,2,1,0:T(2,128)(2,1)S(1)} async-done(((bf16[128,5,2,128]{3,2,1,0:T(2,128)(2,1)}), bf16[128,5,2,128]{3,2,1,0:T(2,128)(2,1)S(1)}, u32[]{:S(2)}, u32[]{:S(2)}) %all-to-all-start.2) | async-done | bytes 327712 | tf_op jit(solution)/shard_map/all_to_all | solution.py:390
  72.0 0.8 %shard_map.115 = (f32[128,512]{1,0:T(8,128)}, f32[4,128]{1,0:T(4,128)}, f32[128,128]{1,0:T(8,128)}, f32[1,128]{1,0:T(1,128)}) custom-call(bf16[1280,128]{1,0:T(8,128)(2,1)S(1)} %bitcast.24, bf16[128,512]{1,0:T(8,128)(2,1)S(1)} %copy-done.1, bf16[4,128]{1,0:T(4,128)(2,1)S(1)} %bitcast.31, f32[1,128]{1,0:T(1,128)S(1)} %bitcast.34), custom_call_target="tpu_custom_call" | custom-call | tf_op jit(solution)/shard_map/pallas_call | solution.py:370
  (11 shorter events, 0.0 us)
Async XLA Ops:
  3.0 26.6 %copy-start.1 = (bf16[128,512]{1,0:T(8,128)(2,1)S(1)}, bf16[128,512]{1,0:T(8,128)(2,1)}, u32[]{:S(2)}) copy-start(bf16[128,512]{1,0:T(8,128)(2,1)} %pw_ref.1) | copy-start | bytes 393220
  27.4 2.0 %copy-start.6 = (s32[256]{0:T(256)S(1)}, s32[256]{0:T(256)}, u32[]{:S(2)}) copy-start(s32[256]{0:T(256)} %param.13) | copy-start | bytes 3076
  27.4 3.5 %collective-permute-start = (bf16[64,32,128]{2,1,0:T(8,128)(2,1)S(1)}, bf16[64,32,128]{2,1,0:T(8,128)(2,1)S(1)}, u32[]{:S(2)}, u32[]{:S(2)}) collective-permute-start(bf16[64,32,128]{2,1,0:T(8,128)(2,1)S(1)} %bitcast.22), channel_id=1, source_target_pairs={{0,8},{8,0},{1,9},{9,1},{2,10},{10,2},{3,11},{11,3},{4,12},{12,4},... | collective-permute-start | bytes 1572872 | tf_op jit(solution)/shard_map/ppermute | solution.py:394
  29.7 1.3 %copy-start.3 = (bf16[128,128]{1,0:T(8,128)(2,1)S(1)}, bf16[128,128]{1,0:T(8,128)(2,1)}, u32[]{:S(2)}) copy-start(bf16[128,128]{1,0:T(8,128)(2,1)} %ow_ref.1) | copy-start | bytes 98308
  34.6 1.8 %collective-permute-start.1 = (bf16[8,8,24,128]{3,2,1,0:T(8,128)(2,1)S(1)}, bf16[8,8,24,128]{3,2,1,0:T(8,128)(2,1)S(1)}, u32[]{:S(2)}, u32[]{:S(2)}) collective-permute-start(bf16[8,8,24,128]{3,2,1,0:T(8,128)(2,1)S(1)} %get-tuple-element.17), channel_id=1, source_target_pairs={{0,8},{8,0},{1,9},{9,1},{2,10},{10,2},{3,11},{11,3},{4,12},{12,4},... | collective-permute-start | bytes 1179656 | tf_op jit(solution)/shard_map/ppermute | solution.py:394
  36.5 17.3 %copy-start.2 = (bf16[512,128]{1,0:T(8,128)(2,1)S(1)}, bf16[512,128]{1,0:T(8,128)(2,1)}, u32[]{:S(2)}) copy-start(bf16[512,128]{1,0:T(8,128)(2,1)} %get-tuple-element.18.normed_ref) | copy-start | bytes 393220
  54.8 5.3 %copy-start = (bf16[16,32,128]{2,1,0:T(8,128)(2,1)S(1)}, bf16[16,32,128]{2,1,0:T(8,128)(2,1)}, u32[]{:S(2)}) copy-start(bf16[16,32,128]{2,1,0:T(8,128)(2,1)} %pair_ref.1) | copy-start | bytes 393220
  54.8 17.2 %all-to-all-start.2 = ((bf16[128,5,2,128]{3,2,1,0:T(2,128)(2,1)}), bf16[128,5,2,128]{3,2,1,0:T(2,128)(2,1)S(1)}, u32[]{:S(2)}, u32[]{:S(2)}) async-start(bf16[128,5,2,128]{3,2,1,0:T(2,128)(2,1)} %bitcast.14), calls=%async_computation.2 | async-start | bytes 655360 | tf_op jit(solution)/shard_map/all_to_all | solution.py:390
  60.0 0.7 copy-start.4
  60.0 0.7 copy-start.5

commit v6 on v5

--- a/solution.py
+++ b/solution.py
@@ -25,7 +25,6 @@
 DIM = 32
 HALF = 8
 IN_ROWS = 32
-PARTS = 4
 TOGETHER = 8
 MID_ROWS = 24
 SUM_ROWS = 32
@@ -56,8 +55,8 @@
 
 
 def pre_kernel(
-    pair_hbm, cot_hbm, gain_hbm, wbt_hbm, send_hbm, normed_hbm,
-    pair_v, cot_v, gain_v, wbt_v, send_v, normed_v, xs, cs, sems, out_sems,
+    pair_hbm, cot_hbm, gain_hbm, wbt_hbm, send_ref, normed_ref,
+    pair_v, cot_v, gain_v, wbt_v, xs, cs, sems,
 ):
     copies = [
         pltpu.make_async_copy(src, dst, sems.at[i])
@@ -75,9 +74,7 @@
     groups = normed.reshape(TILE // (2 * HALF), 2, HALF, CH)
     halves = [groups[:, s].reshape(TILE // 2, CH) for s in range(2)]
     split = jnp.concatenate(halves, axis=0).astype(BF)
-    normed_v[...] = split
-    outs = [pltpu.make_async_copy(normed_v, normed_hbm, out_sems.at[PARTS])]
-    outs[0].start()
+    normed_ref[...] = split
     copies[2].wait()
     bias = mm(wbt_v[...], split, NT)
     chunks = [
@@ -93,23 +90,13 @@
     ]
     copies[3].wait()
     cs[...] = cot_v[...].astype(F32).reshape(TILE, CH)
-    for part in range(PARTS):
-        size = COLS // PARTS
-        for col in range(part * size, (part + 1) * size):
-            x = xs[pl.ds(col, ROWS, stride=COLS), :].astype(BF)
-            c = cs[pl.ds(col, ROWS, stride=COLS), :]
-            for s in range(2):
-                send_v[s, col, 0:16, :] = x
-                rest = jnp.concatenate([c[s * HALF : (s + 1) * HALF], chunks[s]], axis=0)
-                send_v[s, col, 16:32, :] = rest.astype(BF)
-        place = pl.ds(part * size, size)
-        copy = pltpu.make_async_copy(
-            send_v.at[:, place], send_hbm.at[:, place], out_sems.at[part]
-        )
-        copy.start()
-        outs.append(copy)
-    for copy in outs:
-        copy.wait()
+    for col in range(COLS):
+        x = xs[pl.ds(col, ROWS, stride=COLS), :].astype(BF)
+        c = cs[pl.ds(col, ROWS, stride=COLS), :]
+        for s in range(2):
+            send_ref[s, col, 0:16, :] = x
+            rest = jnp.concatenate([c[s * HALF : (s + 1) * HALF], chunks[s]], axis=0)
+            send_ref[s, col, 16:32, :] = rest.astype(BF)
 
 
 def attention_kernel(
@@ -126,13 +113,14 @@
     zero = jnp.zeros((DIM, CH), BF)
 
     def rows(n, start):
-        own, other = [ref[:, n, start : start + HALF, :] for ref in (own_ref, other_ref)]
+        own, other = [ref[:, n, start : start + ROWS, :] for ref in (own_ref, other_ref)]
         low, high = jnp.where(core == 0, own, other), jnp.where(core == 0, other, own)
-        return jnp.stack([low, high], axis=1).astype(F32).reshape(N_WIDE * HALF, CH)
+        both = jnp.stack([low, high], axis=1).astype(F32).reshape(N_WIDE, 2, HALF, CH)
+        return [both[:, i].reshape(N_WIDE * HALF, CH) for i in range(2)]
 
     group = lane_group((N_WIDE, CH), 16)
     for n in range(N_NARROW):
-        tail_s[n * CH : (n + 1) * CH, :] = rows(n, 24)
+        tail_s[n * CH : (n + 1) * CH, :] = rows(n, 16)[1]
     for hh in range(2):
         for kb in range(2):
             got = []
@@ -154,18 +142,18 @@
     def project(n):
         u = Unit()
         u.n = n
-        parts = [rows(n, 0).astype(BF), rows(n, HALF).astype(BF)]
+        parts = [part.astype(BF) for part in rows(n, 0)]
         u.x = jnp.concatenate(parts, axis=0)
         u.x_own = jnp.where(side == 0, parts[0], parts[1])
-        u.cot = rows(n, 16).astype(BF)
-        u.kv = mm(u.x, w_kv, NT).astype(BF)
+        u.cot = rows(n, 16)[0].astype(BF)
         kv_t = mm(w_kv, u.x, NT).astype(BF)
         qg = mm(w_qg, u.x_own, NT)
         og = mm(out_w, u.cot, NT)
         u.pieces = []
         for hh in range(2):
             h = Unit()
-            h.n, h.hh, h.kv = n, hh, u.kv
+            h.n, h.hh = n, hh
+            h.kv = mm(u.x, w_kv[2 * hh * DIM : (2 * hh + 2) * DIM], NT).astype(BF)
             h.q = qg[hh * DIM : (hh + 1) * DIM].astype(BF)
             h.gate = jax.nn.sigmoid(qg[(2 + hh) * DIM : (3 + hh) * DIM])
             h.og = og[hh * DIM : (hh + 1) * DIM]
@@ -175,9 +163,9 @@
         return u
 
     def score(h):
-        top = [jnp.concatenate(pair, axis=1) for pair in ((h.q, zero), (zero, h.da))]
-        rest = [jnp.concatenate([zero, zero], axis=1)] * 2
-        right = jnp.concatenate(top + rest if h.hh == 0 else rest + top, axis=0)
+        right = jnp.concatenate(
+            [jnp.concatenate(pair, axis=1) for pair in ((h.q, zero), (zero, h.da))], axis=0
+        )
         both = mm(h.kv, right)
         h.logits, h.d_soft = both[:, :CH], both[:, CH:]
 
@@ -362,18 +350,19 @@
     gg_ref[...] = (dots_row + bias_row) / gain_ref[...]
 
 
-def call(kernel, out_shape, scratch=(), cost=None, hbm=False, vmem=32):
+def call(kernel, out_shape, scratch=(), cost=None, hbm=False):
     many = isinstance(out_shape, (list, tuple))
-    spec = pl.BlockSpec(memory_space=pltpu.HBM if hbm else pltpu.VMEM)
+    spec = pl.BlockSpec(memory_space=pltpu.VMEM)
+    in_spec = pl.BlockSpec(memory_space=pltpu.HBM) if hbm else spec
 
     def run(*args):
         return pl.pallas_call(
             kernel,
             out_shape=out_shape,
-            in_specs=[spec] * len(args),
+            in_specs=[in_spec] * len(args),
             out_specs=[spec] * len(out_shape) if many else spec,
             scratch_shapes=list(scratch),
-            compiler_params=pltpu.CompilerParams(vmem_limit_bytes=vmem * 1024 * 1024),
+            compiler_params=pltpu.CompilerParams(vmem_limit_bytes=32 * 1024 * 1024),
             cost_estimate=cost,
         )(*args)
 
@@ -406,27 +395,23 @@
 
     send, normed = call(
         pre_kernel,
-        [shape(2, COLS, IN_ROWS, CH), shape(TILE, CH)],
+        [pltpu.VMEM((2, COLS, IN_ROWS, CH), BF), pltpu.VMEM((TILE, CH), BF)],
         [
             pltpu.VMEM((ROWS, COLS, CH), BF),
             pltpu.VMEM((ROWS, COLS, CH), BF),
             pltpu.VMEM((1, CH), F32),
             pltpu.VMEM((HEADS, CH), BF),
-            pltpu.VMEM((2, COLS, IN_ROWS, CH), BF),
-            pltpu.VMEM((TILE, CH), BF),
             tile_f32,
             tile_f32,
             pltpu.SemaphoreType.DMA((4,)),
-            pltpu.SemaphoreType.DMA((PARTS + 1,)),
         ],
         hbm=True,
-        vmem=63,
-    )(pair_rep, cotangent, gain, wbt)
+    )(*[pltpu.with_memory_space_constraint(a, pltpu.HBM) for a in (pair_rep, cotangent, gain, wbt)])
     own = exchange(send.reshape(half, IN_ROWS, CH), CHIPS, 4)
     other = swap(own)
     keep, give = call(
         attention_kernel,
-        [shape(N_CHIP, N_NARROW, MID_ROWS, CH)] * 2,
+        [pltpu.VMEM((N_CHIP, N_NARROW, MID_ROWS, CH), BF)] * 2,
         [
             pltpu.VMEM((2, LENGTH, CH), F32),
             pltpu.VMEM((2, LENGTH, CH), F32),
@@ -443,11 +428,11 @@
         masking,
     )
     got = swap(give)
-    mid = call(join_kernel, shape(half, SUM_ROWS, CH))(
+    mid = call(join_kernel, pltpu.VMEM((half, SUM_ROWS, CH), BF))(
         keep.reshape(half, MID_ROWS, CH), got.reshape(half, MID_ROWS, CH)
     )
     mid = exchange(mid, CHIPS, 8).reshape(2, COLS, SUM_ROWS, CH)
-    send, bias = call(reduce_kernel, [shape(DEVICES * OUT_ROWS, CH), shape(8, TILE)])(mid, normed)
+    send, bias = call(reduce_kernel, [pltpu.VMEM((DEVICES * OUT_ROWS, CH), BF), pltpu.VMEM((8, TILE), BF)])(mid, normed)
     last = exchange(send.reshape(DEVICES, OUT_ROWS, CH), BOTH, 2)
     d_pair = call(
         pair_kernel,

time: 73.2 us -> 72 us (0.984)
  Pallas kernels: 8.89 us -> 8.1 us
    pallas_call x6, Pallas kernels: 8.89 us -> 8.1 us  [run(): pl.pallas_call(kernel, out_shape=out_shape, in_specs=[in_spec] * len(args...]
  transfers between devices with their start and end apart: 3 -> 3, of which waited for: 3 -> 3; matrix products, arithmetic and copies ran while one was open for 0% -> 0% of each run, Pallas kernels for 1% -> 2%
where the time goes in v6:
time: 72 us; the launch traced here: 71.7 us
  blocking collectives  41.4 us (58%)
  waiting for transfers between devices  12.7 us (18%)
  Pallas kernels  8.1 us (11%)
  starting transfers between devices  7.65 us (11%)
  local copies, waits for them, and re-layouts  1.08 us (2%)
  between operations  0.76 us (1%)
    all_to_all x2, blocking collectives, exchange(): return lax.all_to_all(x, axes, 0, 0, tiled=True).reshape(count, rows, lanes)  41.4 us
    all_to_all x1, waiting for transfers between devices, exchange(): return lax.all_to_all(x, axes, 0, 0, tiled=True).reshape(count, rows, lanes)  10.2 us
    pallas_call x6, Pallas kernels, run(): pl.pallas_call(kernel, out_shape=out_shape, in_specs=[in_spec] * len(args...  8.1 us
    all_to_all x1, starting transfers between devices, exchange(): return lax.all_to_all(x, axes, 0, 0, tiled=True).reshape(count, rows, lanes)  5.25 us
    ppermute x2, waiting for transfers between devices, swap(): return lax.ppermute(x, 'core', [(0, 1), (1, 0)])  2.51 us
    ppermute x2, starting transfers between devices, swap(): return lax.ppermute(x, 'core', [(0, 1), (1, 0)])  2.41 us
  transfers between devices with their start and end apart: 3, of which 3 were waited for; matrix products, arithmetic and copies ran while one was open for 0% of the time, Pallas kernels for 2%

profile of v6, /device:TPU:1, one launch (start us, length us, event | category | flops | bytes accessed | tf_op | source)
XLA Modules:
  0.0 71.7 jit_solution(14270073825250725145)
XLA Ops:
  0.6 1.7 %shard_map.110 = (bf16[2,32,32,128]{3,2,1,0:T(8,128)(2,1)S(1)}, bf16[512,128]{1,0:T(8,128)(2,1)S(1)}) custom-call(bf16[16,32,128]{2,1,0:T(8,128)(2,1)} %pair_ref.1, bf16[16,32,128]{2,1,0:T(8,128)(2,1)} %cot_hbm.1, f32[1,128]{1,0:T(1,128)} %bitcast.33, bf16[4,128]{1,0:T(4,128)(2,1)} %bitcast.30), custom_call_target="tpu_custom_call" | custom-call | tf_op jit(solution)/shard_map/pallas_call | solution.py:359
  2.3 0.0 copy-start.1
  2.3 24.2 %all_to_all.15 = bf16[64,8,4,128]{3,2,1,0:T(4,128)(2,1)S(1)} all-to-all(bf16[64,8,4,128]{3,2,1,0:T(4,128)(2,1)S(1)} %bitcast.25), channel_id=1, replica_groups=mesh['chip'=8,'core'=2,'narrow'=8] {'chip','narrow'}, dimensions={0} | all-to-all | bytes 1048576 | tf_op jit(solution)/shard_map/all_to_all | solution.py:379
  26.5 2.0 %collective-permute-start = (bf16[64,32,128]{2,1,0:T(8,128)(2,1)S(1)}, bf16[64,32,128]{2,1,0:T(8,128)(2,1)S(1)}, u32[]{:S(2)}, u32[]{:S(2)}) collective-permute-start(bf16[64,32,128]{2,1,0:T(8,128)(2,1)S(1)} %bitcast.22), channel_id=1, source_target_pairs={{0,8},{8,0},{1,9},{9,1},{2,10},{10,2},{3,11},{11,3},{4,12},{12,4},... | collective-permute-start | bytes 1572872 | tf_op jit(solution)/shard_map/ppermute | solution.py:383
  28.5 0.0 copy-done.5
  28.5 0.1 reshape.46
  28.6 0.1 broadcast_in_dim.7
  28.7 0.1 copy.13
  28.8 0.0 copy-start.2
  28.8 1.2 %collective-permute-done = bf16[64,32,128]{2,1,0:T(8,128)(2,1)S(1)} collective-permute-done((bf16[64,32,128]{2,1,0:T(8,128)(2,1)S(1)}, bf16[64,32,128]{2,1,0:T(8,128)(2,1)S(1)}, u32[]{:S(2)}, u32[]{:S(2)}) %collective-permute-start) | collective-permute-done | bytes 524320 | tf_op jit(solution)/shard_map/ppermute | solution.py:383
  30.0 0.1 broadcast_in_dim.8.mask_ref
  30.1 3.5 %shard_map.111 = (bf16[8,8,24,128]{3,2,1,0:T(8,128)(2,1)S(1)}, bf16[8,8,24,128]{3,2,1,0:T(8,128)(2,1)S(1)}) custom-call(bf16[8,8,32,128]{3,2,1,0:T(8,128)(2,1)S(1)} %bitcast.23, bf16[8,8,32,128]{3,2,1,0:T(8,128)(2,1)S(1)} %bitcast.26, bf16[4,128,128]{2,1,0:T(8,128)(2,1)S(1)} %bitcast.27, bf16[128,128]{1,0:T(8,128)(2,1)S(1)} %copy-done.2, ...), custom_call_target="tpu_custom_call" | custom-call | tf_op jit(solution)/shard_map/pallas_call | solution.py:359
  33.6 0.5 collective-permute-start.1
  34.0 1.3 %collective-permute-done.1 = bf16[8,8,24,128]{3,2,1,0:T(8,128)(2,1)S(1)} collective-permute-done((bf16[8,8,24,128]{3,2,1,0:T(8,128)(2,1)S(1)}, bf16[8,8,24,128]{3,2,1,0:T(8,128)(2,1)S(1)}, u32[]{:S(2)}, u32[]{:S(2)}) %collective-permute-start.1) | collective-permute-done | bytes 393248 | tf_op jit(solution)/shard_map/ppermute | solution.py:383
  35.4 0.1 shard_map.112
  35.5 17.2 %all_to_all.16 = bf16[64,4,8,128]{3,2,1,0:T(8,128)(2,1)S(1)} all-to-all(bf16[64,4,8,128]{3,2,1,0:T(8,128)(2,1)S(1)} %bitcast.21), channel_id=1, replica_groups=mesh['chip'=8,'core'=2,'narrow'=8] {'chip','narrow'}, dimensions={0} | all-to-all | bytes 1048576 | tf_op jit(solution)/shard_map/all_to_all | solution.py:379
  52.7 0.9 %shard_map.113 = (bf16[1280,128]{1,0:T(8,128)(2,1)}, bf16[8,512]{1,0:T(8,128)(2,1)S(1)}) custom-call(bf16[2,32,32,128]{3,2,1,0:T(8,128)(2,1)S(1)} %bitcast.19, bf16[512,128]{1,0:T(8,128)(2,1)S(1)} %get-tuple-element.18.normed_ref), custom_call_target="tpu_custom_call" | custom-call | tf_op jit(solution)/shard_map/pallas_call | solution.py:359
  53.6 5.2 %all-to-all-start.2 = ((bf16[128,5,2,128]{3,2,1,0:T(2,128)(2,1)}), bf16[128,5,2,128]{3,2,1,0:T(2,128)(2,1)S(1)}, u32[]{:S(2)}, u32[]{:S(2)}) async-start(bf16[128,5,2,128]{3,2,1,0:T(2,128)(2,1)} %bitcast.14), calls=%async_computation.2 | async-start | bytes 655360 | tf_op jit(solution)/shard_map/all_to_all | solution.py:379
  58.9 0.0 copy-start.3
  58.9 0.0 copy-start.4
  58.9 0.6 copy-done.3
  59.6 1.1 %shard_map.114 = bf16[16,32,128]{2,1,0:T(8,128)(2,1)} custom-call(bf16[2,32,32,128]{3,2,1,0:T(8,128)(2,1)S(1)} %bitcast.20, bf16[8,512]{1,0:T(8,128)(2,1)S(1)} %get-tuple-element.19.bias_ref, bf16[16,32,128]{2,1,0:T(8,128)(2,1)S(1)} %copy-done, f32[1,128]{1,0:T(1,128)S(1)} %bitcast.34, bf16[4,128]{1,0:T(4,128)(2,1)S(1)} %bitcast.31), custom_call_target="tpu_custom_call" | custom-call | flops 100000000 | bytes 4000000 | tf_op jit(solution)/shard_map/pallas_call | solution.py:359
  60.6 10.2 %all-to-all-done.2 = bf16[128,5,2,128]{3,2,1,0:T(2,128)(2,1)S(1)} async-done(((bf16[128,5,2,128]{3,2,1,0:T(2,128)(2,1)}), bf16[128,5,2,128]{3,2,1,0:T(2,128)(2,1)S(1)}, u32[]{:S(2)}, u32[]{:S(2)}) %all-to-all-start.2) | async-done | bytes 327712 | tf_op jit(solution)/shard_map/all_to_all | solution.py:379
  70.9 0.8 %shard_map.115 = (f32[128,512]{1,0:T(8,128)}, f32[4,128]{1,0:T(4,128)}, f32[128,128]{1,0:T(8,128)}, f32[1,128]{1,0:T(1,128)}) custom-call(bf16[1280,128]{1,0:T(8,128)(2,1)S(1)} %bitcast.24, bf16[128,512]{1,0:T(8,128)(2,1)S(1)} %copy-done.1, bf16[4,128]{1,0:T(4,128)(2,1)S(1)} %bitcast.32, f32[1,128]{1,0:T(1,128)S(1)} %bitcast.35), custom_call_target="tpu_custom_call" | custom-call | tf_op jit(solution)/shard_map/pallas_call | solution.py:359
  (9 shorter events, 0.0 us)
Async XLA Ops:
  2.3 26.3 %copy-start.1 = (bf16[128,512]{1,0:T(8,128)(2,1)S(1)}, bf16[128,512]{1,0:T(8,128)(2,1)}, u32[]{:S(2)}) copy-start(bf16[128,512]{1,0:T(8,128)(2,1)} %pw_ref.1) | copy-start | bytes 393220
  26.5 2.0 %copy-start.5 = (s32[256]{0:T(256)S(1)}, s32[256]{0:T(256)}, u32[]{:S(2)}) copy-start(s32[256]{0:T(256)} %param.13) | copy-start | bytes 3076
  26.5 3.5 %collective-permute-start = (bf16[64,32,128]{2,1,0:T(8,128)(2,1)S(1)}, bf16[64,32,128]{2,1,0:T(8,128)(2,1)S(1)}, u32[]{:S(2)}, u32[]{:S(2)}) collective-permute-start(bf16[64,32,128]{2,1,0:T(8,128)(2,1)S(1)} %bitcast.22), channel_id=1, source_target_pairs={{0,8},{8,0},{1,9},{9,1},{2,10},{10,2},{3,11},{11,3},{4,12},{12,4},... | collective-permute-start | bytes 1572872 | tf_op jit(solution)/shard_map/ppermute | solution.py:383
  28.8 1.3 %copy-start.2 = (bf16[128,128]{1,0:T(8,128)(2,1)S(1)}, bf16[128,128]{1,0:T(8,128)(2,1)}, u32[]{:S(2)}) copy-start(bf16[128,128]{1,0:T(8,128)(2,1)} %ow_ref.1) | copy-start | bytes 98308
  33.6 1.8 %collective-permute-start.1 = (bf16[8,8,24,128]{3,2,1,0:T(8,128)(2,1)S(1)}, bf16[8,8,24,128]{3,2,1,0:T(8,128)(2,1)S(1)}, u32[]{:S(2)}, u32[]{:S(2)}) collective-permute-start(bf16[8,8,24,128]{3,2,1,0:T(8,128)(2,1)S(1)} %get-tuple-element.17), channel_id=1, source_target_pairs={{0,8},{8,0},{1,9},{9,1},{2,10},{10,2},{3,11},{11,3},{4,12},{12,4},... | collective-permute-start | bytes 1179656 | tf_op jit(solution)/shard_map/ppermute | solution.py:383
  53.6 5.3 %copy-start = (bf16[16,32,128]{2,1,0:T(8,128)(2,1)S(1)}, bf16[16,32,128]{2,1,0:T(8,128)(2,1)}, u32[]{:S(2)}) copy-start(bf16[16,32,128]{2,1,0:T(8,128)(2,1)} %pair_ref.1) | copy-start | bytes 393220
  53.6 17.3 %all-to-all-start.2 = ((bf16[128,5,2,128]{3,2,1,0:T(2,128)(2,1)}), bf16[128,5,2,128]{3,2,1,0:T(2,128)(2,1)S(1)}, u32[]{:S(2)}, u32[]{:S(2)}) async-start(bf16[128,5,2,128]{3,2,1,0:T(2,128)(2,1)} %bitcast.14), calls=%async_computation.2 | async-start | bytes 655360 | tf_op jit(solution)/shard_map/all_to_all | solution.py:379
  58.9 0.7 copy-start.3
  58.9 0.7 copy-start.4

commit v7 on v6

--- a/solution.py
+++ b/solution.py
@@ -55,8 +55,8 @@
 
 
 def pre_kernel(
-    pair_hbm, cot_hbm, gain_hbm, wbt_hbm, send_ref, normed_ref,
-    pair_v, cot_v, gain_v, wbt_v, xs, cs, sems,
+    pair_hbm, cot_hbm, gain_hbm, wbt_hbm, send_ref, normed_ref, pair_v, gain_v, wbt_v,
+    cot_v, xs, cs, sems,
 ):
     copies = [
         pltpu.make_async_copy(src, dst, sems.at[i])
@@ -66,16 +66,16 @@
     ]
     for copy in copies:
         copy.start()
-    copies[0].wait()
+    for copy in copies:
+        copy.wait()
+    cs[...] = cot_v[...].astype(F32).reshape(TILE, CH)
     hat, _ = normal(pair_v[...].astype(F32).reshape(TILE, CH))
-    copies[1].wait()
     normed = (hat * gain_v[...]).astype(BF).astype(F32)
     xs[...] = normed
     groups = normed.reshape(TILE // (2 * HALF), 2, HALF, CH)
     halves = [groups[:, s].reshape(TILE // 2, CH) for s in range(2)]
     split = jnp.concatenate(halves, axis=0).astype(BF)
     normed_ref[...] = split
-    copies[2].wait()
     bias = mm(wbt_v[...], split, NT)
     chunks = [
         jnp.concatenate(
@@ -88,8 +88,6 @@
         )
         for s in range(2)
     ]
-    copies[3].wait()
-    cs[...] = cot_v[...].astype(F32).reshape(TILE, CH)
     for col in range(COLS):
         x = xs[pl.ds(col, ROWS, stride=COLS), :].astype(BF)
         c = cs[pl.ds(col, ROWS, stride=COLS), :]
@@ -303,7 +301,7 @@
         send_ref[i * 80 : (i + 1) * 80, :] = block
 
 
-def pair_kernel(recv_ref, bias_ref, pair_ref, gain_ref, wbt_ref, out_ref, ds):
+def pair_grads(recv_ref, bias_ref, pair_ref, gain_ref, wbt_ref, out_ref, ds):
     total = recv_ref[0, :, 0:16, :].astype(F32) + recv_ref[1, :, 0:16, :].astype(F32)
     ds[...] = total.reshape(TILE, CH)
     d_normed = jnp.concatenate([ds[pl.ds(r, COLS, stride=ROWS), :] for r in range(ROWS)], axis=0)
@@ -321,7 +319,11 @@
     out_ref[...] = d_pair.astype(BF).reshape(ROWS, COLS, CH)
 
 
-def final_kernel(recv_ref, pw_ref, wbt_ref, gain_ref, gp_ref, gb_ref, go_ref, gg_ref, vs):
+def final_kernel(
+    recv_ref, mid_ref, bias_ref, pair_ref, pw_ref, wbt_ref, gain_ref,
+    out_ref, gp_ref, gb_ref, go_ref, gg_ref, vs, ds,
+):
+    pair_grads(mid_ref, bias_ref, pair_ref, gain_ref, wbt_ref, out_ref, ds)
     vs[...] = recv_ref[...].astype(F32)
     dots = jnp.zeros((CH, CH), F32)
     for t in range(4):
@@ -393,14 +395,17 @@
     tile_f32 = pltpu.VMEM((TILE, CH), F32)
     half = DEVICES // 2
 
-    send, normed = call(
+    send, normed, pair_here, gain, wbt = call(
         pre_kernel,
-        [pltpu.VMEM((2, COLS, IN_ROWS, CH), BF), pltpu.VMEM((TILE, CH), BF)],
-        [
-            pltpu.VMEM((ROWS, COLS, CH), BF),
+        [
+            pltpu.VMEM((2, COLS, IN_ROWS, CH), BF),
+            pltpu.VMEM((TILE, CH), BF),
             pltpu.VMEM((ROWS, COLS, CH), BF),
             pltpu.VMEM((1, CH), F32),
             pltpu.VMEM((HEADS, CH), BF),
+        ],
+        [
+            pltpu.VMEM((ROWS, COLS, CH), BF),
             tile_f32,
             tile_f32,
             pltpu.SemaphoreType.DMA((4,)),
@@ -434,22 +439,17 @@
     mid = exchange(mid, CHIPS, 8).reshape(2, COLS, SUM_ROWS, CH)
     send, bias = call(reduce_kernel, [pltpu.VMEM((DEVICES * OUT_ROWS, CH), BF), pltpu.VMEM((8, TILE), BF)])(mid, normed)
     last = exchange(send.reshape(DEVICES, OUT_ROWS, CH), BOTH, 2)
-    d_pair = call(
-        pair_kernel,
-        shape(ROWS, COLS, CH),
-        [tile_f32],
-        pl.CostEstimate(flops=100_000_000, bytes_accessed=4_000_000, transcendentals=512),
-    )(mid, bias, pair_rep, gain, wbt)
-    grad_proj, grad_bias, grad_out, grad_gain = call(
+    d_pair, grad_proj, grad_bias, grad_out, grad_gain = call(
         final_kernel,
         [
+            shape(ROWS, COLS, CH),
             shape(CH, 4 * CH, dtype=F32),
             shape(HEADS, CH, dtype=F32),
             shape(CH, CH, dtype=F32),
             shape(1, CH, dtype=F32),
         ],
-        [pltpu.VMEM((DEVICES * OUT_ROWS, CH), F32)],
-    )(last.reshape(DEVICES * OUT_ROWS, CH), proj_weight, wbt, gain)
+        [pltpu.VMEM((DEVICES * OUT_ROWS, CH), F32), tile_f32],
+    )(last.reshape(DEVICES * OUT_ROWS, CH), mid, bias, pair_here, proj_weight, wbt, gain)
     return (d_pair, grad_proj, grad_bias.T, grad_out, grad_gain.reshape(CH))
 
 

time: 72 us -> 71.4 us (level)
  blocking collectives: 41.4 us -> 58.4 us
  waiting for transfers between devices: 12.7 us -> 2.51 us
  starting transfers between devices: 7.65 us -> 2.41 us
  Pallas kernels: 8.1 us -> 6.66 us
    all_to_all x2 -> x3, blocking collectives: 41.4 us -> 58.4 us  [exchange(): return lax.all_to_all(x, axes, 0, 0, tiled=True).reshape(count, rows, lanes)]
    all_to_all x1 -> x0, waiting for transfers between devices: 10.2 us -> none  [exchange(): return lax.all_to_all(x, axes, 0, 0, tiled=True).reshape(count, rows, lanes)]
    all_to_all x1 -> x0, starting transfers between devices: 5.25 us -> none  [exchange(): return lax.all_to_all(x, axes, 0, 0, tiled=True).reshape(count, rows, lanes)]
    pallas_call x6 -> x5, Pallas kernels: 8.1 us -> 6.66 us  [run(): pl.pallas_call(kernel, out_shape=out_shape, in_specs=[in_spec] * len(args...]
  transfers between devices with their start and end apart: 3 -> 2, of which waited for: 3 -> 2; matrix products, arithmetic and copies ran while one was open for 0% -> 0% of each run, Pallas kernels for 2% -> 0%
where the time goes in v7:
time: 71.4 us; the launch traced here: 71.1 us
  blocking collectives  58.4 us (82%)
  Pallas kernels  6.66 us (9%)
  waiting for transfers between devices  2.51 us (4%)
  starting transfers between devices  2.41 us (3%)
  between operations  0.73 us (1%)
    all_to_all x3, blocking collectives, exchange(): return lax.all_to_all(x, axes, 0, 0, tiled=True).reshape(count, rows, lanes)  58.4 us
    pallas_call x5, Pallas kernels, run(): pl.pallas_call(kernel, out_shape=out_shape, in_specs=[in_spec] * len(args...  6.66 us
    ppermute x2, waiting for transfers between devices, swap(): return lax.ppermute(x, 'core', [(0, 1), (1, 0)])  2.51 us
    ppermute x2, starting transfers between devices, swap(): return lax.ppermute(x, 'core', [(0, 1), (1, 0)])  2.41 us
  transfers between devices with their start and end apart: 2, of which 2 were waited for; matrix products, arithmetic and copies ran while one was open for 0% of the time, Pallas kernels for 0%

profile of v7, /device:TPU:1, one launch (start us, length us, event | category | flops | bytes accessed | tf_op | source)
XLA Modules:
  0.0 71.1 jit_solution(18358848389517859662)
XLA Ops:
  0.6 1.6 %shard_map.110 = (bf16[2,32,32,128]{3,2,1,0:T(8,128)(2,1)S(1)}, bf16[512,128]{1,0:T(8,128)(2,1)S(1)}, bf16[16,32,128]{2,1,0:T(8,128)(2,1)S(1)}, f32[1,128]{1,0:T(1,128)S(1)}, bf16[4,128]{1,0:T(4,128)(2,1)S(1)}) custom-call(bf16[16,32,128]{2,1,0:T(8,128)(2,1)} %pair_hbm.1, bf16[16,32,128]{2,1,0:T(8,128)(2,1)} %cot_hbm.1, f32[1,128]{1,0:T(1,128)} %bitcast.34, ...), custom_call_target="tpu_custom_call" | custom-call | tf_op jit(solution)/shard_map/pallas_call | solution.py:361
  2.3 0.0 copy-start
  2.3 24.2 %all_to_all.15 = bf16[64,8,4,128]{3,2,1,0:T(4,128)(2,1)S(1)} all-to-all(bf16[64,8,4,128]{3,2,1,0:T(4,128)(2,1)S(1)} %bitcast.25), channel_id=1, replica_groups=mesh['chip'=8,'core'=2,'narrow'=8] {'chip','narrow'}, dimensions={0} | all-to-all | bytes 1048576 | tf_op jit(solution)/shard_map/all_to_all | solution.py:381
  26.5 0.0 copy-start.2
  26.5 2.0 %collective-permute-start = (bf16[64,32,128]{2,1,0:T(8,128)(2,1)S(1)}, bf16[64,32,128]{2,1,0:T(8,128)(2,1)S(1)}, u32[]{:S(2)}, u32[]{:S(2)}) collective-permute-start(bf16[64,32,128]{2,1,0:T(8,128)(2,1)S(1)} %bitcast.22), channel_id=1, source_target_pairs={{0,8},{8,0},{1,9},{9,1},{2,10},{10,2},{3,11},{11,3},{4,12},{12,4},... | collective-permute-start | bytes 1572872 | tf_op jit(solution)/shard_map/ppermute | solution.py:385
  28.4 0.0 copy-done.2
  28.4 0.1 reshape.46
  28.5 0.1 broadcast_in_dim.7
  28.6 0.0 copy-done
  28.6 0.1 copy.13
  28.8 0.0 copy-start.1
  28.8 1.2 %collective-permute-done = bf16[64,32,128]{2,1,0:T(8,128)(2,1)S(1)} collective-permute-done((bf16[64,32,128]{2,1,0:T(8,128)(2,1)S(1)}, bf16[64,32,128]{2,1,0:T(8,128)(2,1)S(1)}, u32[]{:S(2)}, u32[]{:S(2)}) %collective-permute-start) | collective-permute-done | bytes 524320 | tf_op jit(solution)/shard_map/ppermute | solution.py:385
  29.9 0.1 broadcast_in_dim.8.mask_ref
  30.0 0.0 copy-done.1
  30.1 3.5 %shard_map.111 = (bf16[8,8,24,128]{3,2,1,0:T(8,128)(2,1)S(1)}, bf16[8,8,24,128]{3,2,1,0:T(8,128)(2,1)S(1)}) custom-call(bf16[8,8,32,128]{3,2,1,0:T(8,128)(2,1)S(1)} %bitcast.23, bf16[8,8,32,128]{3,2,1,0:T(8,128)(2,1)S(1)} %bitcast.26, bf16[4,128,128]{2,1,0:T(8,128)(2,1)S(1)} %bitcast.27, bf16[128,128]{1,0:T(8,128)(2,1)S(1)} %copy-done.1, ...), custom_call_target="tpu_custom_call" | custom-call | tf_op jit(solution)/shard_map/pallas_call | solution.py:361
  33.5 0.5 collective-permute-start.1
  34.0 1.3 %collective-permute-done.1 = bf16[8,8,24,128]{3,2,1,0:T(8,128)(2,1)S(1)} collective-permute-done((bf16[8,8,24,128]{3,2,1,0:T(8,128)(2,1)S(1)}, bf16[8,8,24,128]{3,2,1,0:T(8,128)(2,1)S(1)}, u32[]{:S(2)}, u32[]{:S(2)}) %collective-permute-start.1) | collective-permute-done | bytes 393248 | tf_op jit(solution)/shard_map/ppermute | solution.py:385
  35.3 0.1 shard_map.112
  35.5 17.2 %all_to_all.16 = bf16[64,4,8,128]{3,2,1,0:T(8,128)(2,1)S(1)} all-to-all(bf16[64,4,8,128]{3,2,1,0:T(8,128)(2,1)S(1)} %bitcast.21), channel_id=1, replica_groups=mesh['chip'=8,'core'=2,'narrow'=8] {'chip','narrow'}, dimensions={0} | all-to-all | bytes 1048576 | tf_op jit(solution)/shard_map/all_to_all | solution.py:381
  52.7 0.2 shard_map.113
  52.9 17.0 %all_to_all.17 = bf16[128,5,2,128]{3,2,1,0:T(2,128)(2,1)S(1)} all-to-all(bf16[128,5,2,128]{3,2,1,0:T(2,128)(2,1)S(1)} %bitcast.30), channel_id=1, replica_groups=mesh['chip'=8,'core'=2,'narrow'=8] {'chip','core','narrow'}, dimensions={0} | all-to-all | bytes 655360 | tf_op jit(solution)/shard_map/all_to_all | solution.py:381
  69.9 1.2 %shard_map.114 = (bf16[16,32,128]{2,1,0:T(8,128)(2,1)}, f32[128,512]{1,0:T(8,128)}, f32[4,128]{1,0:T(4,128)}, f32[128,128]{1,0:T(8,128)}, f32[1,128]{1,0:T(1,128)}) custom-call(bf16[1280,128]{1,0:T(8,128)(2,1)S(1)} %bitcast.24, bf16[2,32,32,128]{3,2,1,0:T(8,128)(2,1)S(1)} %bitcast.20, bf16[8,512]{1,0:T(8,128)(2,1)S(1)} %get-tuple-element.24.bias_ref, ...), custom_call_target="tpu_custom_call" | custom-call | tf_op jit(solution)/shard_map/pallas_call | solution.py:361
  (3 shorter events, 0.0 us)
Async XLA Ops:
  2.3 26.3 %copy-start = (bf16[128,512]{1,0:T(8,128)(2,1)S(1)}, bf16[128,512]{1,0:T(8,128)(2,1)}, u32[]{:S(2)}) copy-start(bf16[128,512]{1,0:T(8,128)(2,1)} %pw_ref.1) | copy-start | bytes 393220
  26.5 2.0 %copy-start.2 = (s32[256]{0:T(256)S(1)}, s32[256]{0:T(256)}, u32[]{:S(2)}) copy-start(s32[256]{0:T(256)} %param.13) | copy-start | bytes 3076
  26.5 3.5 %collective-permute-start = (bf16[64,32,128]{2,1,0:T(8,128)(2,1)S(1)}, bf16[64,32,128]{2,1,0:T(8,128)(2,1)S(1)}, u32[]{:S(2)}, u32[]{:S(2)}) collective-permute-start(bf16[64,32,128]{2,1,0:T(8,128)(2,1)S(1)} %bitcast.22), channel_id=1, source_target_pairs={{0,8},{8,0},{1,9},{9,1},{2,10},{10,2},{3,11},{11,3},{4,12},{12,4},... | collective-permute-start | bytes 1572872 | tf_op jit(solution)/shard_map/ppermute | solution.py:385
  28.8 1.3 %copy-start.1 = (bf16[128,128]{1,0:T(8,128)(2,1)S(1)}, bf16[128,128]{1,0:T(8,128)(2,1)}, u32[]{:S(2)}) copy-start(bf16[128,128]{1,0:T(8,128)(2,1)} %ow_ref.1) | copy-start | bytes 98308
  33.5 1.8 %collective-permute-start.1 = (bf16[8,8,24,128]{3,2,1,0:T(8,128)(2,1)S(1)}, bf16[8,8,24,128]{3,2,1,0:T(8,128)(2,1)S(1)}, u32[]{:S(2)}, u32[]{:S(2)}) collective-permute-start(bf16[8,8,24,128]{3,2,1,0:T(8,128)(2,1)S(1)} %get-tuple-element.21), channel_id=1, source_target_pairs={{0,8},{8,0},{1,9},{9,1},{2,10},{10,2},{3,11},{11,3},{4,12},{12,4},... | collective-permute-start | bytes 1179656 | tf_op jit(solution)/shard_map/ppermute | solution.py:385

commit v8 on v7

--- a/solution.py
+++ b/solution.py
@@ -55,28 +55,30 @@
 
 
 def pre_kernel(
-    pair_hbm, cot_hbm, gain_hbm, wbt_hbm, send_ref, normed_ref, pair_v, gain_v, wbt_v,
+    pair_hbm, cot_hbm, gain_ref, wbt_ref, send_ref, normed_ref, pair_v, gain_v, wbt_v,
     cot_v, xs, cs, sems,
 ):
     copies = [
         pltpu.make_async_copy(src, dst, sems.at[i])
         for i, (src, dst) in enumerate(
-            ((pair_hbm, pair_v), (gain_hbm, gain_v), (wbt_hbm, wbt_v), (cot_hbm, cot_v))
+            ((pair_hbm, pair_v), (cot_hbm, cot_v))
         )
     ]
     for copy in copies:
         copy.start()
+    gain_v[...] = gain_ref[...]
+    wbt_v[...] = wbt_ref[...]
     for copy in copies:
         copy.wait()
     cs[...] = cot_v[...].astype(F32).reshape(TILE, CH)
     hat, _ = normal(pair_v[...].astype(F32).reshape(TILE, CH))
-    normed = (hat * gain_v[...]).astype(BF).astype(F32)
+    normed = (hat * gain_ref[...]).astype(BF).astype(F32)
     xs[...] = normed
     groups = normed.reshape(TILE // (2 * HALF), 2, HALF, CH)
     halves = [groups[:, s].reshape(TILE // 2, CH) for s in range(2)]
     split = jnp.concatenate(halves, axis=0).astype(BF)
     normed_ref[...] = split
-    bias = mm(wbt_v[...], split, NT)
+    bias = mm(wbt_ref[...], split, NT)
     chunks = [
         jnp.concatenate(
             [
@@ -352,16 +354,16 @@
     gg_ref[...] = (dots_row + bias_row) / gain_ref[...]
 
 
-def call(kernel, out_shape, scratch=(), cost=None, hbm=False):
+def call(kernel, out_shape, scratch=(), cost=None, hbm=0):
     many = isinstance(out_shape, (list, tuple))
     spec = pl.BlockSpec(memory_space=pltpu.VMEM)
-    in_spec = pl.BlockSpec(memory_space=pltpu.HBM) if hbm else spec
+    outside = pl.BlockSpec(memory_space=pltpu.HBM)
 
     def run(*args):
         return pl.pallas_call(
             kernel,
             out_shape=out_shape,
-            in_specs=[in_spec] * len(args),
+            in_specs=[outside] * hbm + [spec] * (len(args) - hbm),
             out_specs=[spec] * len(out_shape) if many else spec,
             scratch_shapes=list(scratch),
             compiler_params=pltpu.CompilerParams(vmem_limit_bytes=32 * 1024 * 1024),
@@ -408,10 +410,10 @@
             pltpu.VMEM((ROWS, COLS, CH), BF),
             tile_f32,
             tile_f32,
-            pltpu.SemaphoreType.DMA((4,)),
+            pltpu.SemaphoreType.DMA((2,)),
         ],
-        hbm=True,
-    )(*[pltpu.with_memory_space_constraint(a, pltpu.HBM) for a in (pair_rep, cotangent, gain, wbt)])
+        hbm=2,
+    )(*[pltpu.with_memory_space_constraint(a, pltpu.HBM) for a in (pair_rep, cotangent)], gain, wbt)
     own = exchange(send.reshape(half, IN_ROWS, CH), CHIPS, 4)
     other = swap(own)
     keep, give = call(

time: 71.4 us -> 72 us (level)
  no operation moved by 1% of the time
where the time goes in v8:
time: 72 us; the launch traced here: 71.8 us
  blocking collectives  58.4 us (81%)
  Pallas kernels  6.61 us (9%)
  waiting for transfers between devices  2.51 us (3%)
  starting transfers between devices  2.41 us (3%)
  local copies, waits for them, and re-layouts  1.08 us (2%)
  between operations  0.75 us (1%)
    all_to_all x3, blocking collectives, exchange(): return lax.all_to_all(x, axes, 0, 0, tiled=True).reshape(count, rows, lanes)  58.4 us
    pallas_call x5, Pallas kernels, run(): pl.pallas_call(kernel, out_shape=out_shape, in_specs=[outside] * hbm + [s...  6.61 us
    ppermute x2, waiting for transfers between devices, swap(): return lax.ppermute(x, 'core', [(0, 1), (1, 0)])  2.51 us
    ppermute x2, starting transfers between devices, swap(): return lax.ppermute(x, 'core', [(0, 1), (1, 0)])  2.41 us
  transfers between devices with their start and end apart: 2, of which 2 were waited for; matrix products, arithmetic and copies ran while one was open for 0% of the time, Pallas kernels for 0%

profile of v8, /device:TPU:1, one launch (start us, length us, event | category | flops | bytes accessed | tf_op | source)
XLA Modules:
  0.0 71.8 jit_solution(9659091694093703188)
XLA Ops:
  0.6 0.0 copy-start.2
  0.6 0.0 copy-start.3
  0.7 0.7 copy-done.2
  1.3 1.6 %shard_map.110 = (bf16[2,32,32,128]{3,2,1,0:T(8,128)(2,1)S(1)}, bf16[512,128]{1,0:T(8,128)(2,1)S(1)}, bf16[16,32,128]{2,1,0:T(8,128)(2,1)S(1)}, f32[1,128]{1,0:T(1,128)S(1)}, bf16[4,128]{1,0:T(4,128)(2,1)S(1)}) custom-call(bf16[16,32,128]{2,1,0:T(8,128)(2,1)} %pair_hbm.1, bf16[16,32,128]{2,1,0:T(8,128)(2,1)} %cot_hbm.1, f32[1,128]{1,0:T(1,128)S(1)} %bitcast.32, ...), custom_call_target="tpu_custom_call" | custom-call | tf_op jit(solution)/shard_map/pallas_call | solution.py:363
  2.9 0.0 copy-start
  2.9 24.2 %all_to_all.15 = bf16[64,8,4,128]{3,2,1,0:T(4,128)(2,1)S(1)} all-to-all(bf16[64,8,4,128]{3,2,1,0:T(4,128)(2,1)S(1)} %bitcast.25), channel_id=1, replica_groups=mesh['chip'=8,'core'=2,'narrow'=8] {'chip','narrow'}, dimensions={0} | all-to-all | bytes 1048576 | tf_op jit(solution)/shard_map/all_to_all | solution.py:383
  27.1 2.0 %collective-permute-start = (bf16[64,32,128]{2,1,0:T(8,128)(2,1)S(1)}, bf16[64,32,128]{2,1,0:T(8,128)(2,1)S(1)}, u32[]{:S(2)}, u32[]{:S(2)}) collective-permute-start(bf16[64,32,128]{2,1,0:T(8,128)(2,1)S(1)} %bitcast.22), channel_id=1, source_target_pairs={{0,8},{8,0},{1,9},{9,1},{2,10},{10,2},{3,11},{11,3},{4,12},{12,4},... | collective-permute-start | bytes 1572872 | tf_op jit(solution)/shard_map/ppermute | solution.py:387
  29.0 0.0 copy-done.4
  29.0 0.1 reshape.46
  29.2 0.1 broadcast_in_dim.7
  29.3 0.0 copy-done
  29.3 0.1 copy.13
  29.4 0.0 copy-start.1
  29.4 1.2 %collective-permute-done = bf16[64,32,128]{2,1,0:T(8,128)(2,1)S(1)} collective-permute-done((bf16[64,32,128]{2,1,0:T(8,128)(2,1)S(1)}, bf16[64,32,128]{2,1,0:T(8,128)(2,1)S(1)}, u32[]{:S(2)}, u32[]{:S(2)}) %collective-permute-start) | collective-permute-done | bytes 524320 | tf_op jit(solution)/shard_map/ppermute | solution.py:387
  30.6 0.1 broadcast_in_dim.8.mask_ref
  30.7 0.0 copy-done.1
  30.7 3.5 %shard_map.111 = (bf16[8,8,24,128]{3,2,1,0:T(8,128)(2,1)S(1)}, bf16[8,8,24,128]{3,2,1,0:T(8,128)(2,1)S(1)}) custom-call(bf16[8,8,32,128]{3,2,1,0:T(8,128)(2,1)S(1)} %bitcast.23, bf16[8,8,32,128]{3,2,1,0:T(8,128)(2,1)S(1)} %bitcast.26, bf16[4,128,128]{2,1,0:T(8,128)(2,1)S(1)} %bitcast.27, bf16[128,128]{1,0:T(8,128)(2,1)S(1)} %copy-done.1, ...), custom_call_target="tpu_custom_call" | custom-call | tf_op jit(solution)/shard_map/pallas_call | solution.py:363
  34.2 0.5 collective-permute-start.1
  34.6 1.3 %collective-permute-done.1 = bf16[8,8,24,128]{3,2,1,0:T(8,128)(2,1)S(1)} collective-permute-done((bf16[8,8,24,128]{3,2,1,0:T(8,128)(2,1)S(1)}, bf16[8,8,24,128]{3,2,1,0:T(8,128)(2,1)S(1)}, u32[]{:S(2)}, u32[]{:S(2)}) %collective-permute-start.1) | collective-permute-done | bytes 393248 | tf_op jit(solution)/shard_map/ppermute | solution.py:387
  36.0 0.1 shard_map.112
  36.1 17.2 %all_to_all.16 = bf16[64,4,8,128]{3,2,1,0:T(8,128)(2,1)S(1)} all-to-all(bf16[64,4,8,128]{3,2,1,0:T(8,128)(2,1)S(1)} %bitcast.21), channel_id=1, replica_groups=mesh['chip'=8,'core'=2,'narrow'=8] {'chip','narrow'}, dimensions={0} | all-to-all | bytes 1048576 | tf_op jit(solution)/shard_map/all_to_all | solution.py:383
  53.3 0.2 shard_map.113
  53.5 17.0 %all_to_all.17 = bf16[128,5,2,128]{3,2,1,0:T(2,128)(2,1)S(1)} all-to-all(bf16[128,5,2,128]{3,2,1,0:T(2,128)(2,1)S(1)} %bitcast.30), channel_id=1, replica_groups=mesh['chip'=8,'core'=2,'narrow'=8] {'chip','core','narrow'}, dimensions={0} | all-to-all | bytes 655360 | tf_op jit(solution)/shard_map/all_to_all | solution.py:383
  70.5 1.2 %shard_map.114 = (bf16[16,32,128]{2,1,0:T(8,128)(2,1)}, f32[128,512]{1,0:T(8,128)}, f32[4,128]{1,0:T(4,128)}, f32[128,128]{1,0:T(8,128)}, f32[1,128]{1,0:T(1,128)}) custom-call(bf16[1280,128]{1,0:T(8,128)(2,1)S(1)} %bitcast.24, bf16[2,32,32,128]{3,2,1,0:T(8,128)(2,1)S(1)} %bitcast.20, bf16[8,512]{1,0:T(8,128)(2,1)S(1)} %get-tuple-element.24.bias_ref, ...), custom_call_target="tpu_custom_call" | custom-call | tf_op jit(solution)/shard_map/pallas_call | solution.py:363
  (5 shorter events, 0.0 us)
Async XLA Ops:
  0.6 0.7 copy-start.2
  0.6 0.7 copy-start.3
  2.9 26.4 %copy-start = (bf16[128,512]{1,0:T(8,128)(2,1)S(1)}, bf16[128,512]{1,0:T(8,128)(2,1)}, u32[]{:S(2)}) copy-start(bf16[128,512]{1,0:T(8,128)(2,1)} %pw_ref.1) | copy-start | bytes 393220
  27.1 2.0 %copy-start.4 = (s32[256]{0:T(256)S(1)}, s32[256]{0:T(256)}, u32[]{:S(2)}) copy-start(s32[256]{0:T(256)} %param.13) | copy-start | bytes 3076
  27.1 3.5 %collective-permute-start = (bf16[64,32,128]{2,1,0:T(8,128)(2,1)S(1)}, bf16[64,32,128]{2,1,0:T(8,128)(2,1)S(1)}, u32[]{:S(2)}, u32[]{:S(2)}) collective-permute-start(bf16[64,32,128]{2,1,0:T(8,128)(2,1)S(1)} %bitcast.22), channel_id=1, source_target_pairs={{0,8},{8,0},{1,9},{9,1},{2,10},{10,2},{3,11},{11,3},{4,12},{12,4},... | collective-permute-start | bytes 1572872 | tf_op jit(solution)/shard_map/ppermute | solution.py:387
  29.4 1.3 %copy-start.1 = (bf16[128,128]{1,0:T(8,128)(2,1)S(1)}, bf16[128,128]{1,0:T(8,128)(2,1)}, u32[]{:S(2)}) copy-start(bf16[128,128]{1,0:T(8,128)(2,1)} %ow_ref.1) | copy-start | bytes 98308
  34.2 1.8 %collective-permute-start.1 = (bf16[8,8,24,128]{3,2,1,0:T(8,128)(2,1)S(1)}, bf16[8,8,24,128]{3,2,1,0:T(8,128)(2,1)S(1)}, u32[]{:S(2)}, u32[]{:S(2)}) collective-permute-start(bf16[8,8,24,128]{3,2,1,0:T(8,128)(2,1)S(1)} %get-tuple-element.21), channel_id=1, source_target_pairs={{0,8},{8,0},{1,9},{9,1},{2,10},{10,2},{3,11},{11,3},{4,12},{12,4},... | collective-permute-start | bytes 1179656 | tf_op jit(solution)/shard_map/ppermute | solution.py:387

commit v9 on v7

--- a/solution.py
+++ b/solution.py
@@ -92,9 +92,9 @@
         x = xs[pl.ds(col, ROWS, stride=COLS), :].astype(BF)
         c = cs[pl.ds(col, ROWS, stride=COLS), :]
         for s in range(2):
-            send_ref[s, col, 0:16, :] = x
+            send_ref[1 - s, COLS - 1 - col, 0:16, :] = x
             rest = jnp.concatenate([c[s * HALF : (s + 1) * HALF], chunks[s]], axis=0)
-            send_ref[s, col, 16:32, :] = rest.astype(BF)
+            send_ref[1 - s, COLS - 1 - col, 16:32, :] = rest.astype(BF)
 
 
 def attention_kernel(
@@ -111,7 +111,11 @@
     zero = jnp.zeros((DIM, CH), BF)
 
     def rows(n, start):
-        own, other = [ref[:, n, start : start + ROWS, :] for ref in (own_ref, other_ref)]
+        place = N_NARROW - 1 - n
+        own, other = [
+            jnp.stack([ref[m, place, start : start + ROWS, :] for m in reversed(range(N_CHIP))])
+            for ref in (own_ref, other_ref)
+        ]
         low, high = jnp.where(core == 0, own, other), jnp.where(core == 0, other, own)
         both = jnp.stack([low, high], axis=1).astype(F32).reshape(N_WIDE, 2, HALF, CH)
         return [both[:, i].reshape(N_WIDE * HALF, CH) for i in range(2)]
@@ -412,7 +416,21 @@
         ],
         hbm=True,
     )(*[pltpu.with_memory_space_constraint(a, pltpu.HBM) for a in (pair_rep, cotangent, gain, wbt)])
-    own = exchange(send.reshape(half, IN_ROWS, CH), CHIPS, 4)
+    own = lax.all_to_all(
+        send.reshape(half, IN_ROWS // 4, 4, CH),
+        BOTH,
+        0,
+        0,
+        tiled=True,
+        axis_index_groups=[
+            [
+                m * 2 * N_NARROW + core * N_NARROW + n
+                for m in reversed(range(N_CHIP))
+                for n in reversed(range(N_NARROW))
+            ]
+            for core in range(2)
+        ],
+    ).reshape(half, IN_ROWS, CH)
     other = swap(own)
     keep, give = call(
         attention_kernel,

time: 71.4 us -> 70.3 us (0.985)
  blocking collectives: 58.4 us -> 57.3 us
    all_to_all x3 -> x2, blocking collectives: 58.4 us -> 37.2 us  [exchange(): return lax.all_to_all(x, axes, 0, 0, tiled=True).reshape(count, rows, lanes)]
    all_to_all x0 -> x1, blocking collectives: none -> 20.1 us  [local(): lax.all_to_all(send.reshape(half, IN_ROWS // 4, 4, CH), BOTH, 0, 0, tiled...]
where the time goes in v9:
time: 70.3 us; the launch traced here: 70.1 us
  blocking collectives  57.3 us (82%)
  Pallas kernels  6.66 us (9%)
  waiting for transfers between devices  2.51 us (4%)
  starting transfers between devices  2.49 us (4%)
  between operations  0.73 us (1%)
    all_to_all x2, blocking collectives, exchange(): return lax.all_to_all(x, axes, 0, 0, tiled=True).reshape(count, rows, lanes)  37.2 us
    all_to_all x1, blocking collectives, local(): lax.all_to_all(send.reshape(half, IN_ROWS // 4, 4, CH), BOTH, 0, 0, tiled...  20.1 us
    pallas_call x5, Pallas kernels, run(): pl.pallas_call(kernel, out_shape=out_shape, in_specs=[in_spec] * len(args...  6.66 us
    ppermute x2, waiting for transfers between devices, swap(): return lax.ppermute(x, 'core', [(0, 1), (1, 0)])  2.51 us
    ppermute x2, starting transfers between devices, swap(): return lax.ppermute(x, 'core', [(0, 1), (1, 0)])  2.49 us
  transfers between devices with their start and end apart: 2, of which 2 were waited for; matrix products, arithmetic and copies ran while one was open for 0% of the time, Pallas kernels for 0%

profile of v9, /device:TPU:1, one launch (start us, length us, event | category | flops | bytes accessed | tf_op | source)
XLA Modules:
  0.0 70.1 jit_solution(4271581907522018979)
XLA Ops:
  0.6 1.6 %shard_map.110 = (bf16[2,32,32,128]{3,2,1,0:T(8,128)(2,1)S(1)}, bf16[512,128]{1,0:T(8,128)(2,1)S(1)}, bf16[16,32,128]{2,1,0:T(8,128)(2,1)S(1)}, f32[1,128]{1,0:T(1,128)S(1)}, bf16[4,128]{1,0:T(4,128)(2,1)S(1)}) custom-call(bf16[16,32,128]{2,1,0:T(8,128)(2,1)} %pair_hbm.1, bf16[16,32,128]{2,1,0:T(8,128)(2,1)} %cot_hbm.1, f32[1,128]{1,0:T(1,128)} %bitcast.34, ...), custom_call_target="tpu_custom_call" | custom-call | tf_op jit(solution)/shard_map/pallas_call | solution.py:365
  2.3 0.0 copy-start
  2.3 20.1 %all_to_all.15 = bf16[64,8,4,128]{3,2,1,0:T(4,128)(2,1)S(1)} all-to-all(bf16[64,8,4,128]{3,2,1,0:T(4,128)(2,1)S(1)} %bitcast.25), channel_id=1, replica_groups={{119,118,117,116,115,114,113,112,103,102,101,100,99,98,97,96,87,86,85,8..., dimensions={0} | all-to-all | bytes 1048576 | tf_op jit(solution)/shard_map/all_to_all | solution.py:419
  22.3 0.0 copy-start.2
  22.3 2.0 %collective-permute-start = (bf16[64,32,128]{2,1,0:T(8,128)(2,1)S(1)}, bf16[64,32,128]{2,1,0:T(8,128)(2,1)S(1)}, u32[]{:S(2)}, u32[]{:S(2)}) collective-permute-start(bf16[64,32,128]{2,1,0:T(8,128)(2,1)S(1)} %bitcast.22), channel_id=1, source_target_pairs={{0,8},{8,0},{1,9},{9,1},{2,10},{10,2},{3,11},{11,3},{4,12},{12,4},... | collective-permute-start | bytes 1572872 | tf_op jit(solution)/shard_map/ppermute | solution.py:389
  24.4 0.0 copy-done.2
  24.4 0.1 reshape.50
  24.5 0.1 broadcast_in_dim.7
  24.6 0.0 copy-done
  24.6 0.1 copy.13
  24.8 0.0 copy-start.1
  24.8 1.2 %collective-permute-done = bf16[64,32,128]{2,1,0:T(8,128)(2,1)S(1)} collective-permute-done((bf16[64,32,128]{2,1,0:T(8,128)(2,1)S(1)}, bf16[64,32,128]{2,1,0:T(8,128)(2,1)S(1)}, u32[]{:S(2)}, u32[]{:S(2)}) %collective-permute-start) | collective-permute-done | bytes 524320 | tf_op jit(solution)/shard_map/ppermute | solution.py:389
  25.9 0.1 broadcast_in_dim.8.mask_ref
  26.0 0.0 copy-done.1
  26.0 3.5 %shard_map.111 = (bf16[8,8,24,128]{3,2,1,0:T(8,128)(2,1)S(1)}, bf16[8,8,24,128]{3,2,1,0:T(8,128)(2,1)S(1)}) custom-call(bf16[8,8,32,128]{3,2,1,0:T(8,128)(2,1)S(1)} %bitcast.23, bf16[8,8,32,128]{3,2,1,0:T(8,128)(2,1)S(1)} %bitcast.26, bf16[4,128,128]{2,1,0:T(8,128)(2,1)S(1)} %bitcast.27, bf16[128,128]{1,0:T(8,128)(2,1)S(1)} %copy-done.1, ...), custom_call_target="tpu_custom_call" | custom-call | tf_op jit(solution)/shard_map/pallas_call | solution.py:365
  29.5 0.5 collective-permute-start.1
  30.0 1.4 %collective-permute-done.1 = bf16[8,8,24,128]{3,2,1,0:T(8,128)(2,1)S(1)} collective-permute-done((bf16[8,8,24,128]{3,2,1,0:T(8,128)(2,1)S(1)}, bf16[8,8,24,128]{3,2,1,0:T(8,128)(2,1)S(1)}, u32[]{:S(2)}, u32[]{:S(2)}) %collective-permute-start.1) | collective-permute-done | bytes 393248 | tf_op jit(solution)/shard_map/ppermute | solution.py:389
  31.3 0.1 shard_map.112
  31.4 20.2 %all_to_all.16 = bf16[64,4,8,128]{3,2,1,0:T(8,128)(2,1)S(1)} all-to-all(bf16[64,4,8,128]{3,2,1,0:T(8,128)(2,1)S(1)} %bitcast.21), channel_id=1, replica_groups=mesh['chip'=8,'core'=2,'narrow'=8] {'chip','narrow'}, dimensions={0} | all-to-all | bytes 1048576 | tf_op jit(solution)/shard_map/all_to_all | solution.py:385
  51.6 0.2 shard_map.113
  51.8 17.0 %all_to_all.17 = bf16[128,5,2,128]{3,2,1,0:T(2,128)(2,1)S(1)} all-to-all(bf16[128,5,2,128]{3,2,1,0:T(2,128)(2,1)S(1)} %bitcast.30), channel_id=1, replica_groups=mesh['chip'=8,'core'=2,'narrow'=8] {'chip','core','narrow'}, dimensions={0} | all-to-all | bytes 655360 | tf_op jit(solution)/shard_map/all_to_all | solution.py:385
  68.9 1.2 %shard_map.114 = (bf16[16,32,128]{2,1,0:T(8,128)(2,1)}, f32[128,512]{1,0:T(8,128)}, f32[4,128]{1,0:T(4,128)}, f32[128,128]{1,0:T(8,128)}, f32[1,128]{1,0:T(1,128)}) custom-call(bf16[1280,128]{1,0:T(8,128)(2,1)S(1)} %bitcast.24, bf16[2,32,32,128]{3,2,1,0:T(8,128)(2,1)S(1)} %bitcast.20, bf16[8,512]{1,0:T(8,128)(2,1)S(1)} %get-tuple-element.24.bias_ref, ...), custom_call_target="tpu_custom_call" | custom-call | tf_op jit(solution)/shard_map/pallas_call | solution.py:365
  (3 shorter events, 0.0 us)
Async XLA Ops:
  2.3 22.3 %copy-start = (bf16[128,512]{1,0:T(8,128)(2,1)S(1)}, bf16[128,512]{1,0:T(8,128)(2,1)}, u32[]{:S(2)}) copy-start(bf16[128,512]{1,0:T(8,128)(2,1)} %pw_ref.1) | copy-start | bytes 393220
  22.3 2.0 %copy-start.2 = (s32[256]{0:T(256)S(1)}, s32[256]{0:T(256)}, u32[]{:S(2)}) copy-start(s32[256]{0:T(256)} %param.13) | copy-start | bytes 3076
  22.3 3.6 %collective-permute-start = (bf16[64,32,128]{2,1,0:T(8,128)(2,1)S(1)}, bf16[64,32,128]{2,1,0:T(8,128)(2,1)S(1)}, u32[]{:S(2)}, u32[]{:S(2)}) collective-permute-start(bf16[64,32,128]{2,1,0:T(8,128)(2,1)S(1)} %bitcast.22), channel_id=1, source_target_pairs={{0,8},{8,0},{1,9},{9,1},{2,10},{10,2},{3,11},{11,3},{4,12},{12,4},... | collective-permute-start | bytes 1572872 | tf_op jit(solution)/shard_map/ppermute | solution.py:389
  24.8 1.3 %copy-start.1 = (bf16[128,128]{1,0:T(8,128)(2,1)S(1)}, bf16[128,128]{1,0:T(8,128)(2,1)}, u32[]{:S(2)}) copy-start(bf16[128,128]{1,0:T(8,128)(2,1)} %ow_ref.1) | copy-start | bytes 98308
  29.5 1.8 %collective-permute-start.1 = (bf16[8,8,24,128]{3,2,1,0:T(8,128)(2,1)S(1)}, bf16[8,8,24,128]{3,2,1,0:T(8,128)(2,1)S(1)}, u32[]{:S(2)}, u32[]{:S(2)}) collective-permute-start(bf16[8,8,24,128]{3,2,1,0:T(8,128)(2,1)S(1)} %get-tuple-element.21), channel_id=1, source_target_pairs={{0,8},{8,0},{1,9},{9,1},{2,10},{10,2},{3,11},{11,3},{4,12},{12,4},... | collective-permute-start | bytes 1179656 | tf_op jit(solution)/shard_map/ppermute | solution.py:389

commit v10 on v7

--- a/solution.py
+++ b/solution.py
@@ -9,7 +9,6 @@
 MASK_FILL = 1000000000.0
 BF = jnp.bfloat16
 F32 = jnp.float32
-CHIPS = ("chip", "narrow")
 BOTH = ("chip", "core", "narrow")
 
 ROWS = 16
@@ -92,9 +91,9 @@
         x = xs[pl.ds(col, ROWS, stride=COLS), :].astype(BF)
         c = cs[pl.ds(col, ROWS, stride=COLS), :]
         for s in range(2):
-            send_ref[s, col, 0:16, :] = x
+            send_ref[1 - s, COLS - 1 - col, 0:16, :] = x
             rest = jnp.concatenate([c[s * HALF : (s + 1) * HALF], chunks[s]], axis=0)
-            send_ref[s, col, 16:32, :] = rest.astype(BF)
+            send_ref[1 - s, COLS - 1 - col, 16:32, :] = rest.astype(BF)
 
 
 def attention_kernel(
@@ -111,7 +110,11 @@
     zero = jnp.zeros((DIM, CH), BF)
 
     def rows(n, start):
-        own, other = [ref[:, n, start : start + ROWS, :] for ref in (own_ref, other_ref)]
+        place = N_NARROW - 1 - n
+        own, other = [
+            jnp.stack([ref[m, place, start : start + ROWS, :] for m in reversed(range(N_CHIP))])
+            for ref in (own_ref, other_ref)
+        ]
         low, high = jnp.where(core == 0, own, other), jnp.where(core == 0, other, own)
         both = jnp.stack([low, high], axis=1).astype(F32).reshape(N_WIDE, 2, HALF, CH)
         return [both[:, i].reshape(N_WIDE * HALF, CH) for i in range(2)]
@@ -247,11 +250,17 @@
     put(tail, slice(None), 16, 24)
 
 
+def reverse(x):
+    return jnp.stack([x[i] for i in reversed(range(x.shape[0]))])
+
+
 def join_kernel(keep_ref, got_ref, send_ref):
     core = lax.axis_index("core")
     total = keep_ref[:, 0:16, :].astype(F32) + got_ref[:, 0:16, :].astype(F32)
-    send_ref[:, 0:16, :] = total.astype(BF)
-    keep, got = keep_ref[:, 16:24, :], got_ref[:, 16:24, :]
+    send_ref[:, 0:16, :] = reverse(total.astype(BF))
+    tails = [ref[:, 16:24, :].astype(F32) for ref in (keep_ref, got_ref)]
+    first = lax.broadcasted_iota(jnp.int32, tails[0].shape, 1) < 4
+    keep, got = [jnp.where(first, reverse(t), t).astype(BF) for t in tails]
     send_ref[:, 16:24, :] = jnp.where(core == 0, keep, got)
     send_ref[:, 24:32, :] = jnp.where(core == 0, got, keep)
 
@@ -259,7 +268,7 @@
 def reduce_kernel(recv_ref, normed_ref, send_ref, bias_ref):
     sums = [
         [
-            jnp.sum(recv_ref[s, :, 16 + 8 * c : 24 + 8 * c, :].astype(F32), axis=0)
+            jnp.sum(recv_ref[1 - s, :, 16 + 8 * c : 24 + 8 * c, :].astype(F32), axis=0)
             for c in range(2)
         ]
         for s in range(2)
@@ -288,7 +297,7 @@
             }[t]
             row = jnp.where(group == h, turn(got, (h - place) * DIM), row)
         rows.append(row)
-    place = lax.rem(lax.axis_index("narrow"), 4)
+    place = lax.rem(N_NARROW - 1 - lax.axis_index("narrow"), 4)
     row = jnp.zeros((1, CH), F32)
     for h in range(HEADS):
         shift = lax.rem(h * DIM + CH - place * DIM, CH)
@@ -303,7 +312,7 @@
 
 def pair_grads(recv_ref, bias_ref, pair_ref, gain_ref, wbt_ref, out_ref, ds):
     total = recv_ref[0, :, 0:16, :].astype(F32) + recv_ref[1, :, 0:16, :].astype(F32)
-    ds[...] = total.reshape(TILE, CH)
+    ds[...] = reverse(total).reshape(TILE, CH)
     d_normed = jnp.concatenate([ds[pl.ds(r, COLS, stride=ROWS), :] for r in range(ROWS)], axis=0)
     wbt = wbt_ref[...].astype(F32)
     wbt = jnp.concatenate([wbt, jnp.zeros_like(wbt)], axis=0).astype(BF)
@@ -375,10 +384,20 @@
     return jax.ShapeDtypeStruct(dims, dtype)
 
 
-def exchange(x, axes, tile):
+def backward(x, tile, cores=((0,), (1,))):
     count, rows, lanes = x.shape
+    groups = [
+        [
+            (m * 2 + core) * N_NARROW + n
+            for m in reversed(range(N_CHIP))
+            for core in group
+            for n in reversed(range(N_NARROW))
+        ]
+        for group in cores
+    ]
     x = x.reshape(count, rows // tile, tile, lanes)
-    return lax.all_to_all(x, axes, 0, 0, tiled=True).reshape(count, rows, lanes)
+    x = lax.all_to_all(x, BOTH, 0, 0, tiled=True, axis_index_groups=groups)
+    return x.reshape(count, rows, lanes)
 
 
 def swap(x):
@@ -412,7 +431,7 @@
         ],
         hbm=True,
     )(*[pltpu.with_memory_space_constraint(a, pltpu.HBM) for a in (pair_rep, cotangent, gain, wbt)])
-    own = exchange(send.reshape(half, IN_ROWS, CH), CHIPS, 4)
+    own = backward(send.reshape(half, IN_ROWS, CH), 4)
     other = swap(own)
     keep, give = call(
         attention_kernel,
@@ -436,9 +455,9 @@
     mid = call(join_kernel, pltpu.VMEM((half, SUM_ROWS, CH), BF))(
         keep.reshape(half, MID_ROWS, CH), got.reshape(half, MID_ROWS, CH)
     )
-    mid = exchange(mid, CHIPS, 8).reshape(2, COLS, SUM_ROWS, CH)
+    mid = backward(mid, 8).reshape(2, COLS, SUM_ROWS, CH)
     send, bias = call(reduce_kernel, [pltpu.VMEM((DEVICES * OUT_ROWS, CH), BF), pltpu.VMEM((8, TILE), BF)])(mid, normed)
-    last = exchange(send.reshape(DEVICES, OUT_ROWS, CH), BOTH, 2)
+    last = backward(send.reshape(DEVICES, OUT_ROWS, CH), 2, [(0, 1)])
     d_pair, grad_proj, grad_bias, grad_out, grad_gain = call(
         final_kernel,
         [

time: 71.4 us -> 70.1 us (0.982)
  blocking collectives: 58.4 us -> 57 us
    all_to_all x3, blocking collectives: 58.4 us -> 57 us  [backward(): x = lax.all_to_all(x, BOTH, 0, 0, tiled=True, axis_index_groups=groups)]
where the time goes in v10:
time: 70.1 us; the launch traced here: 69.9 us
  blocking collectives  57 us (81%)
  Pallas kernels  6.72 us (10%)
  waiting for transfers between devices  2.51 us (4%)
  starting transfers between devices  2.49 us (4%)
  between operations  0.73 us (1%)
    all_to_all x3, blocking collectives, backward(): x = lax.all_to_all(x, BOTH, 0, 0, tiled=True, axis_index_groups=groups)  57 us
    pallas_call x5, Pallas kernels, run(): pl.pallas_call(kernel, out_shape=out_shape, in_specs=[in_spec] * len(args...  6.72 us
    ppermute x2, waiting for transfers between devices, swap(): return lax.ppermute(x, 'core', [(0, 1), (1, 0)])  2.51 us
    ppermute x2, starting transfers between devices, swap(): return lax.ppermute(x, 'core', [(0, 1), (1, 0)])  2.49 us
  transfers between devices with their start and end apart: 2, of which 2 were waited for; matrix products, arithmetic and copies ran while one was open for 0% of the time, Pallas kernels for 0%

profile of v10, /device:TPU:1, one launch (start us, length us, event | category | flops | bytes accessed | tf_op | source)
XLA Modules:
  0.0 69.9 jit_solution(6248536709009047698)
XLA Ops:
  0.6 1.6 %shard_map.110 = (bf16[2,32,32,128]{3,2,1,0:T(8,128)(2,1)S(1)}, bf16[512,128]{1,0:T(8,128)(2,1)S(1)}, bf16[16,32,128]{2,1,0:T(8,128)(2,1)S(1)}, f32[1,128]{1,0:T(1,128)S(1)}, bf16[4,128]{1,0:T(4,128)(2,1)S(1)}) custom-call(bf16[16,32,128]{2,1,0:T(8,128)(2,1)} %pair_hbm.1, bf16[16,32,128]{2,1,0:T(8,128)(2,1)} %cot_hbm.1, f32[1,128]{1,0:T(1,128)} %bitcast.34, ...), custom_call_target="tpu_custom_call" | custom-call | tf_op jit(solution)/shard_map/pallas_call | solution.py:370
  2.3 0.0 copy-start
  2.3 20.1 %all_to_all.15 = bf16[64,8,4,128]{3,2,1,0:T(4,128)(2,1)S(1)} all-to-all(bf16[64,8,4,128]{3,2,1,0:T(4,128)(2,1)S(1)} %bitcast.25), channel_id=1, replica_groups={{119,118,117,116,115,114,113,112,103,102,101,100,99,98,97,96,87,86,85,8..., dimensions={0} | all-to-all | bytes 1048576 | tf_op jit(solution)/shard_map/all_to_all | solution.py:399
  22.3 0.0 copy-start.2
  22.3 2.0 %collective-permute-start = (bf16[64,32,128]{2,1,0:T(8,128)(2,1)S(1)}, bf16[64,32,128]{2,1,0:T(8,128)(2,1)S(1)}, u32[]{:S(2)}, u32[]{:S(2)}) collective-permute-start(bf16[64,32,128]{2,1,0:T(8,128)(2,1)S(1)} %bitcast.22), channel_id=1, source_target_pairs={{0,8},{8,0},{1,9},{9,1},{2,10},{10,2},{3,11},{11,3},{4,12},{12,4},... | collective-permute-start | bytes 1572872 | tf_op jit(solution)/shard_map/ppermute | solution.py:404
  24.4 0.0 copy-done.2
  24.4 0.1 reshape.46
  24.5 0.1 broadcast_in_dim.7
  24.6 0.0 copy-done
  24.6 0.1 copy.13
  24.8 0.0 copy-start.1
  24.8 1.2 %collective-permute-done = bf16[64,32,128]{2,1,0:T(8,128)(2,1)S(1)} collective-permute-done((bf16[64,32,128]{2,1,0:T(8,128)(2,1)S(1)}, bf16[64,32,128]{2,1,0:T(8,128)(2,1)S(1)}, u32[]{:S(2)}, u32[]{:S(2)}) %collective-permute-start) | collective-permute-done | bytes 524320 | tf_op jit(solution)/shard_map/ppermute | solution.py:404
  25.9 0.1 broadcast_in_dim.8.mask_ref
  26.0 0.0 copy-done.1
  26.0 3.5 %shard_map.111 = (bf16[8,8,24,128]{3,2,1,0:T(8,128)(2,1)S(1)}, bf16[8,8,24,128]{3,2,1,0:T(8,128)(2,1)S(1)}) custom-call(bf16[8,8,32,128]{3,2,1,0:T(8,128)(2,1)S(1)} %bitcast.23, bf16[8,8,32,128]{3,2,1,0:T(8,128)(2,1)S(1)} %bitcast.26, bf16[4,128,128]{2,1,0:T(8,128)(2,1)S(1)} %bitcast.27, bf16[128,128]{1,0:T(8,128)(2,1)S(1)} %copy-done.1, ...), custom_call_target="tpu_custom_call" | custom-call | tf_op jit(solution)/shard_map/pallas_call | solution.py:370
  29.5 0.5 collective-permute-start.1
  30.0 1.4 %collective-permute-done.1 = bf16[8,8,24,128]{3,2,1,0:T(8,128)(2,1)S(1)} collective-permute-done((bf16[8,8,24,128]{3,2,1,0:T(8,128)(2,1)S(1)}, bf16[8,8,24,128]{3,2,1,0:T(8,128)(2,1)S(1)}, u32[]{:S(2)}, u32[]{:S(2)}) %collective-permute-start.1) | collective-permute-done | bytes 393248 | tf_op jit(solution)/shard_map/ppermute | solution.py:404
  31.3 0.2 shard_map.112
  31.5 17.0 %all_to_all.16 = bf16[64,4,8,128]{3,2,1,0:T(8,128)(2,1)S(1)} all-to-all(bf16[64,4,8,128]{3,2,1,0:T(8,128)(2,1)S(1)} %bitcast.21), channel_id=1, replica_groups={{119,118,117,116,115,114,113,112,103,102,101,100,99,98,97,96,87,86,85,8..., dimensions={0} | all-to-all | bytes 1048576 | tf_op jit(solution)/shard_map/all_to_all | solution.py:399
  48.5 0.2 shard_map.113
  48.7 19.9 %all_to_all.17 = bf16[128,5,2,128]{3,2,1,0:T(2,128)(2,1)S(1)} all-to-all(bf16[128,5,2,128]{3,2,1,0:T(2,128)(2,1)S(1)} %bitcast.30), channel_id=1, replica_groups={{119,118,117,116,115,114,113,112,127,126,125,124,123,122,121,120,103,10..., dimensions={0} | all-to-all | bytes 655360 | tf_op jit(solution)/shard_map/all_to_all | solution.py:399
  68.6 1.2 %shard_map.114 = (bf16[16,32,128]{2,1,0:T(8,128)(2,1)}, f32[128,512]{1,0:T(8,128)}, f32[4,128]{1,0:T(4,128)}, f32[128,128]{1,0:T(8,128)}, f32[1,128]{1,0:T(1,128)}) custom-call(bf16[1280,128]{1,0:T(8,128)(2,1)S(1)} %bitcast.24, bf16[2,32,32,128]{3,2,1,0:T(8,128)(2,1)S(1)} %bitcast.20, bf16[8,512]{1,0:T(8,128)(2,1)S(1)} %get-tuple-element.24.bias_ref, ...), custom_call_target="tpu_custom_call" | custom-call | tf_op jit(solution)/shard_map/pallas_call | solution.py:370
  (3 shorter events, 0.0 us)
Async XLA Ops:
  2.3 22.3 %copy-start = (bf16[128,512]{1,0:T(8,128)(2,1)S(1)}, bf16[128,512]{1,0:T(8,128)(2,1)}, u32[]{:S(2)}) copy-start(bf16[128,512]{1,0:T(8,128)(2,1)} %pw_ref.1) | copy-start | bytes 393220
  22.3 2.0 %copy-start.2 = (s32[256]{0:T(256)S(1)}, s32[256]{0:T(256)}, u32[]{:S(2)}) copy-start(s32[256]{0:T(256)} %param.13) | copy-start | bytes 3076
  22.3 3.6 %collective-permute-start = (bf16[64,32,128]{2,1,0:T(8,128)(2,1)S(1)}, bf16[64,32,128]{2,1,0:T(8,128)(2,1)S(1)}, u32[]{:S(2)}, u32[]{:S(2)}) collective-permute-start(bf16[64,32,128]{2,1,0:T(8,128)(2,1)S(1)} %bitcast.22), channel_id=1, source_target_pairs={{0,8},{8,0},{1,9},{9,1},{2,10},{10,2},{3,11},{11,3},{4,12},{12,4},... | collective-permute-start | bytes 1572872 | tf_op jit(solution)/shard_map/ppermute | solution.py:404
  24.8 1.3 %copy-start.1 = (bf16[128,128]{1,0:T(8,128)(2,1)S(1)}, bf16[128,128]{1,0:T(8,128)(2,1)}, u32[]{:S(2)}) copy-start(bf16[128,128]{1,0:T(8,128)(2,1)} %ow_ref.1) | copy-start | bytes 98308
  29.5 1.8 %collective-permute-start.1 = (bf16[8,8,24,128]{3,2,1,0:T(8,128)(2,1)S(1)}, bf16[8,8,24,128]{3,2,1,0:T(8,128)(2,1)S(1)}, u32[]{:S(2)}, u32[]{:S(2)}) collective-permute-start(bf16[8,8,24,128]{3,2,1,0:T(8,128)(2,1)S(1)} %get-tuple-element.21), channel_id=1, source_target_pairs={{0,8},{8,0},{1,9},{9,1},{2,10},{10,2},{3,11},{11,3},{4,12},{12,4},... | collective-permute-start | bytes 1179656 | tf_op jit(solution)/shard_map/ppermute | solution.py:404
